TPU v7x, 512 devices: a whole 4x4x16 slice. The times are simulated.
512 devices in a mesh: slab: 4 (over x_lo, core), mapx: 16 (over z), mapy: 8 (over y, x_hi).
Axes of the slice: x: 4 (x_hi: 2, x_lo: 2; x = x_hi * 2 + x_lo), y: 4, z: 16, core: 2. Of those that a mesh axis runs over, the one named last changes fastest.
Arguments:
- pressure: float32 [32, 1536, 2048], P('slab', 'mapx', 'mapy'), may hold values from -2 to 2
- porosity: float32 [32, 1536, 2048], P('slab', 'mapx', 'mapy'), may hold values from 0.1 to 0.5
- lithology: int32 [32, 1536, 2048], P('slab', 'mapx', 'mapy'), may hold values from 0 to 3
- layer_solid: float32 [32], P('slab'), may hold values from 0.05 to 0.15
Outputs:
- pressure_new: float32 [32, 1536, 2048], P('slab', 'mapx', 'mapy')
- porosity_new: float32 [32, 1536, 2048], P('slab', 'mapx', 'mapy')
- thickness_new: float32 [32, 1536, 2048], P('slab', 'mapx', 'mapy')
All inputs are finite; a program needn't handle non-finite values.
Results may differ from a plain program's by a relative error of at most 0.00015.
Values sent between devices are 32-bit elements; how exact they have to be, the bound alone decides.
No kernel may reach another device: no remote copies, remote signals or barrier semaphores. Data moves between devices by JAX's collectives and lax.ppermute only.
A program may use at most 64 MiB of HBM per device.

v0:
```python
import jax
import jax.numpy as jnp
from jax import lax
from jax.sharding import PartitionSpec as P

PHI_SURFACE = (0.45, 0.55, 0.65, 0.4)
ATHY_RATE = (0.25, 0.45, 0.8, 0.35)
MOB_BASE = (1.0, 0.0, -1.5, -0.5)
MOB_SLOPE = (6.0, 5.0, 8.0, 4.0)
GRAIN_DENSITY = (2.65, 2.68, 2.72, 2.71)
WATER_DENSITY = 1.03
SPECTRUM_MID = 1.0
SPECTRUM_HALF = 0.95
SIGMA_RATIO = SPECTRUM_MID / SPECTRUM_HALF
RHO_FIRST = 1.0 / SIGMA_RATIO
RHO_SECOND = 1.0 / (2.0 * SIGMA_RATIO - RHO_FIRST)


def padded_2(array, sides, width):
    for axis, dim in sides:
        size, length = (lax.axis_size(axis), array.shape[dim])
        up = [(i, (i + 1) % size) for i in range(size - 1)]
        down = [(j, i) for i, j in up]
        last = lax.slice_in_dim(array, length - width, length, axis=dim)
        leading = lax.slice_in_dim(array, 0, width, axis=dim)
        before = lax.ppermute(last, axis, up)
        after = lax.ppermute(leading, axis, down)
        array = jnp.concatenate([before, array, after], axis=dim)
    return array


def carried_in(value, axis, join, neutral):
    count, mine = (lax.axis_size(axis), lax.axis_index(axis))
    pieces = lax.all_gather(value, axis)
    total = jnp.full_like(value, 0) + jnp.asarray(neutral, value.dtype)

    def hop(position, total):
        longer = join(total, pieces[position])
        return jnp.where(position < mine, longer, total)

    return lax.fori_loop(0, count - 1, hop, total)


def lookup(lithology, table):
    result = jnp.zeros(lithology.shape, jnp.float32)
    for index, entry in enumerate(table):
        result = result + jnp.where(lithology == index, jnp.float32(entry), jnp.float32(0.0))
    return result


def neighbours(padded):
    return [
        padded[2:, 1:-1, 1:-1],
        padded[:-2, 1:-1, 1:-1],
        padded[1:-1, 2:, 1:-1],
        padded[1:-1, :-2, 1:-1],
        padded[1:-1, 1:-1, 2:],
        padded[1:-1, 1:-1, :-2],
    ]


def harmonic(centre, padded):
    result = []
    for other in neighbours(padded):
        total = centre + other
        safe_total = jnp.where(total > 0.0, total, 1.0)
        result.append(2.0 * centre * other / safe_total)
    return result


def operate_padded(trans, field, padded):
    result = field
    for weight, beside in zip(trans, neighbours(padded)):
        result = result + weight * (field - beside)
    return result


def add_loads(earlier, later):
    return earlier + later


def body(pressure, porosity, lithology, layer_solid):
    mobility = jnp.exp(
        lookup(lithology, MOB_BASE) + lookup(lithology, MOB_SLOPE) * (porosity - 0.35)
    )
    mob_padded = padded_2(mobility, (("slab", 0), ("mapx", 1), ("mapy", 2)), 1)
    trans = harmonic(mobility, mob_padded)
    diag = 1.0 + trans[0] + trans[1] + trans[2] + trans[3] + trans[4] + trans[5]

    def operate(field):
        padded = padded_2(field, (("slab", 0), ("mapx", 1), ("mapy", 2)), 1)
        return operate_padded(trans, field, padded)

    first_res = pressure - operate(pressure)
    first_step = first_res / (SPECTRUM_MID * diag)
    middle = pressure + first_step
    second_res = pressure - operate(middle)
    second_step = (
        RHO_SECOND * RHO_FIRST * first_step + 2.0 * RHO_SECOND / SPECTRUM_HALF * second_res / diag
    )
    pressure_new = middle + second_step
    solid = layer_solid[:, None, None]
    load = (lookup(lithology, GRAIN_DENSITY) + WATER_DENSITY * porosity / (1.0 - porosity)) * solid
    local_sum = jnp.cumsum(load, axis=0)
    column_total = local_sum[-1]
    above = carried_in(column_total, "slab", add_loads, jnp.zeros_like(column_total))
    overburden = above[None] + local_sum - 0.5 * load
    stress = jnp.maximum(overburden - pressure_new, 0.0)
    porosity_new = lookup(lithology, PHI_SURFACE) * jnp.exp(-lookup(lithology, ATHY_RATE) * stress)
    thickness_new = solid / (1.0 - porosity_new)
    return (pressure_new, porosity_new, thickness_new)


def solution(mesh):
    in_specs = (
        P("slab", "mapx", "mapy"),
        P("slab", "mapx", "mapy"),
        P("slab", "mapx", "mapy"),
        P("slab"),
    )
    out_specs = (P("slab", "mapx", "mapy"), P("slab", "mapx", "mapy"), P("slab", "mapx", "mapy"))
    return jax.shard_map(body, mesh=mesh, in_specs=in_specs, out_specs=out_specs, check_vma=False)
```

profile of v0, /device:TPU:366, one launch (start us, length us, event | category | flops | bytes accessed | tf_op | source)
XLA Modules:
  0.0 114.2 jit_solution(4687029810346926080)
XLA Ops:
  1.6 2.2 %collective-permute-start.1 = (f32[1,96,256]{2,1,0:T(8,128)S(1)}, f32[1,96,256]{2,1,0:T(8,128)S(1)}, u32[]{:S(2)}, u32[]{:S(2)}) collective-permute-start(f32[1,96,256]{2,1,0:T(8,128)S(1)} %get-tuple-element.135), channel_id=1, source_target_pairs={{128,0},{256,128},{384,256},{129,1},{257,129},{385,257},{130,2},{2... | collective-permute-start | bytes 294920 | tf_op jit(solution)/shard_map/ppermute | solution.py:27
  3.8 2.2 %collective-permute-start.3 = (f32[1,96,256]{2,1,0:T(8,128)S(1)}, f32[1,96,256]{2,1,0:T(8,128)S(1)}, u32[]{:S(2)}, u32[]{:S(2)}) collective-permute-start(f32[1,96,256]{2,1,0:T(8,128)S(1)} %get-tuple-element.136), channel_id=1, source_target_pairs={{0,128},{128,256},{256,384},{1,129},{129,257},{257,385},{2,130},{1... | collective-permute-start | bytes 294920 | tf_op jit(solution)/shard_map/ppermute | solution.py:26
  5.9 3.1 %add_exponential_fusion = (f32[8,96,256]{2,1,0:T(8,128)S(1)}, pred[8,96,256]{2,1,0:T(8,128)(4,1)S(1)}, pred[8,96,256]{2,1,0:T(8,128)(4,1)}, pred[8,96,256]{2,1,0:T(8,128)(4,1)}, pred[8,96,256]{2,1,0:T(8,128)(4,1)}) fusion(f32[8,96,256]{2,1,0:T(8,128)} %param.7, s32[8,96,256]{2,1,0:T(8,128)} %param.8), kind=kLoop, calls=%fused_computation.113 | loop fusion | flops 3735552 | bytes 3145728 | tf_op jit(solution)/shard_map/exp | solution.py:83
  9.0 1.9 %collective-permute-start.2 = (f32[1,96,256]{2,1,0:T(8,128)S(1)}, f32[1,96,256]{2,1,0:T(8,128)S(1)}, u32[]{:S(2)}, u32[]{:S(2)}) collective-permute-start(f32[1,96,256]{2,1,0:T(8,128)S(1)} %get-tuple-element.133), channel_id=1, source_target_pairs={{0,128},{128,256},{256,384},{1,129},{129,257},{257,385},{2,130},{1... | collective-permute-start | bytes 294920 | tf_op jit(solution)/shard_map/ppermute | solution.py:26
  10.9 3.6 %collective-permute-start = (f32[1,96,256]{2,1,0:T(8,128)S(1)}, f32[1,96,256]{2,1,0:T(8,128)S(1)}, u32[]{:S(2)}, u32[]{:S(2)}) collective-permute-start(f32[1,96,256]{2,1,0:T(8,128)S(1)} %get-tuple-element.134), channel_id=1, source_target_pairs={{128,0},{256,128},{384,256},{129,1},{257,129},{385,257},{130,2},{2... | collective-permute-start | bytes 294920 | tf_op jit(solution)/shard_map/ppermute | solution.py:27
  14.8 2.9 %collective-permute-start.5 = (f32[10,1,256]{2,0,1:T(8,128)S(1)}, f32[10,1,256]{2,0,1:T(8,128)S(1)}, u32[]{:S(2)}, u32[]{:S(2)}) collective-permute-start(f32[10,1,256]{2,0,1:T(8,128)S(1)} %copy.65), channel_id=1, source_target_pairs={{8,0},{16,8},{24,16},{32,24},{40,32},{48,40},{56,48},{64,56},{72,6... | collective-permute-start | bytes 30728 | tf_op jit(solution)/shard_map/ppermute | solution.py:27
  17.7 4.1 %collective-permute-start.7 = (f32[10,1,256]{2,0,1:T(8,128)S(1)}, f32[10,1,256]{2,0,1:T(8,128)S(1)}, u32[]{:S(2)}, u32[]{:S(2)}) collective-permute-start(f32[10,1,256]{2,0,1:T(8,128)S(1)} %copy.67), channel_id=1, source_target_pairs={{0,8},{8,16},{16,24},{24,32},{32,40},{40,48},{48,56},{56,64},{64,7... | collective-permute-start | bytes 30728 | tf_op jit(solution)/shard_map/ppermute | solution.py:26
  22.0 1.9 %collective-permute-start.4 = (f32[10,1,256]{2,0,1:T(8,128)S(1)}, f32[10,1,256]{2,0,1:T(8,128)S(1)}, u32[]{:S(2)}, u32[]{:S(2)}) collective-permute-start(f32[10,1,256]{2,0,1:T(8,128)S(1)} %copy.64), channel_id=1, source_target_pairs={{8,0},{16,8},{24,16},{32,24},{40,32},{48,40},{56,48},{64,56},{72,6... | collective-permute-start | bytes 30728 | tf_op jit(solution)/shard_map/ppermute | solution.py:27
  23.9 5.1 %collective-permute-start.6 = (f32[10,1,256]{2,0,1:T(8,128)S(1)}, f32[10,1,256]{2,0,1:T(8,128)S(1)}, u32[]{:S(2)}, u32[]{:S(2)}) collective-permute-start(f32[10,1,256]{2,0,1:T(8,128)S(1)} %copy.66), channel_id=1, source_target_pairs={{0,8},{8,16},{16,24},{24,32},{32,40},{40,48},{48,56},{56,64},{64,7... | collective-permute-start | bytes 30728 | tf_op jit(solution)/shard_map/ppermute | solution.py:26
  30.3 4.3 %collective-permute-start.11 = (f32[10,98,1]{1,0,2:T(8,128)S(1)}, f32[10,98,1]{1,0,2:T(8,128)S(1)}, u32[]{:S(2)}, u32[]{:S(2)}) collective-permute-start(f32[10,98,1]{1,0,2:T(8,128)S(1)} %copy.52), channel_id=1, source_target_pairs={{0,1},{1,2},{2,3},{3,4},{4,5},{5,6},{6,7},{8,9},{9,10},{10,11},{11... | collective-permute-start | bytes 11768 | tf_op jit(solution)/shard_map/ppermute | solution.py:26
  34.7 3.0 %collective-permute-start.9 = (f32[10,98,1]{1,0,2:T(8,128)S(1)}, f32[10,98,1]{1,0,2:T(8,128)S(1)}, u32[]{:S(2)}, u32[]{:S(2)}) collective-permute-start(f32[10,98,1]{1,0,2:T(8,128)S(1)} %copy.48), channel_id=1, source_target_pairs={{1,0},{2,1},{3,2},{4,3},{5,4},{6,5},{7,6},{9,8},{10,9},{11,10},{12... | collective-permute-start | bytes 11768 | tf_op jit(solution)/shard_map/ppermute | solution.py:27
  38.6 4.2 %collective-permute-start.8 = (f32[10,98,1]{1,0,2:T(8,128)S(1)}, f32[10,98,1]{1,0,2:T(8,128)S(1)}, u32[]{:S(2)}, u32[]{:S(2)}) collective-permute-start(f32[10,98,1]{1,0,2:T(8,128)S(1)} %copy.44), channel_id=1, source_target_pairs={{1,0},{2,1},{3,2},{4,3},{5,4},{6,5},{7,6},{9,8},{10,9},{11,10},{12... | collective-permute-start | bytes 11768 | tf_op jit(solution)/shard_map/ppermute | solution.py:27
  43.2 4.0 %collective-permute-start.10 = (f32[10,98,1]{1,0,2:T(8,128)S(1)}, f32[10,98,1]{1,0,2:T(8,128)S(1)}, u32[]{:S(2)}, u32[]{:S(2)}) collective-permute-start(f32[10,98,1]{1,0,2:T(8,128)S(1)} %copy.50), channel_id=1, source_target_pairs={{0,1},{1,2},{2,3},{3,4},{4,5},{5,6},{6,7},{8,9},{9,10},{10,11},{11... | collective-permute-start | bytes 11768 | tf_op jit(solution)/shard_map/ppermute | solution.py:26
  47.2 1.1 copy.49
  50.4 1.1 copy.51
  51.5 7.5 %fusion.55 = (f32[8,96,256]{2,1,0:T(8,128)S(1)}, f32[8,96,256]{2,1,0:T(8,128)}) fusion(f32[8,96,256]{2,1,0:T(8,128)S(1)} %copy-done, f32[10,1,256]{2,1,0:T(1,128)} %copy-done.13, f32[10,96,256]{2,1,0:T(8,128)} %copy-done.2, f32[10,1,256]{2,1,0:T(1,128)} %copy-done.14, f32[10,98,1]{2,1,0:T(8,128)} %copy.53, f32[8,96,256]{2,1,0:T(8,128)S(1)} %get-tuple-element.114, ...), kind=kLoop, calls=%fused_computation.128 | loop fusion | flops 16908288 | bytes 4578624 | tf_op jit(solution)/shard_map/add | solution.py:96
  59.0 1.9 %collective-permute-start.13 = (f32[1,96,256]{2,1,0:T(8,128)S(1)}, f32[1,96,256]{2,1,0:T(8,128)S(1)}, u32[]{:S(2)}, u32[]{:S(2)}) collective-permute-start(f32[1,96,256]{2,1,0:T(8,128)S(1)} %get-tuple-element.131), channel_id=1, source_target_pairs={{0,128},{128,256},{256,384},{1,129},{129,257},{257,385},{2,130},{1... | collective-permute-start | bytes 294920 | tf_op jit(solution)/shard_map/ppermute | solution.py:26
  60.9 3.6 %collective-permute-start.12 = (f32[1,96,256]{2,1,0:T(8,128)S(1)}, f32[1,96,256]{2,1,0:T(8,128)S(1)}, u32[]{:S(2)}, u32[]{:S(2)}) collective-permute-start(f32[1,96,256]{2,1,0:T(8,128)S(1)} %get-tuple-element.132), channel_id=1, source_target_pairs={{128,0},{256,128},{384,256},{129,1},{257,129},{385,257},{130,2},{2... | collective-permute-start | bytes 294920 | tf_op jit(solution)/shard_map/ppermute | solution.py:27
  68.0 1.9 %collective-permute-start.14 = (f32[10,1,256]{2,0,1:T(8,128)}, f32[10,1,256]{2,0,1:T(8,128)}, u32[]{:S(2)}, u32[]{:S(2)}) collective-permute-start(f32[10,1,256]{2,0,1:T(8,128)} %copy.68), channel_id=1, source_target_pairs={{8,0},{16,8},{24,16},{32,24},{40,32},{48,40},{56,48},{64,56},{72,6... | collective-permute-start | bytes 30728 | tf_op jit(solution)/shard_map/ppermute | solution.py:27
  70.0 5.1 %collective-permute-start.15 = (f32[10,1,256]{2,0,1:T(8,128)}, f32[10,1,256]{2,0,1:T(8,128)}, u32[]{:S(2)}, u32[]{:S(2)}) collective-permute-start(f32[10,1,256]{2,0,1:T(8,128)} %copy.69), channel_id=1, source_target_pairs={{0,8},{8,16},{16,24},{24,32},{32,40},{40,48},{48,56},{56,64},{64,7... | collective-permute-start | bytes 30728 | tf_op jit(solution)/shard_map/ppermute | solution.py:26
  75.1 6.6 %all_gather.3 = f32[4,96,256]{2,1,0:T(8,128)} all-gather(f32[1,96,256]{2,1,0:T(8,128)S(1)} %slice.178), channel_id=1, replica_groups=mesh['slab'=4,'mapx'=16,'mapy'=8] {'slab'}, dimensions={0}, use_global_device_ids=true | all-gather | bytes 491520 | tf_op jit(solution)/shard_map/all_gather | solution.py:34
  83.2 1.1 pad_maximum_fusion.2
  84.3 1.1 fusion.57
  85.4 1.9 %copy.60 = f32[10,98,1]{1,0,2:T(8,128)} copy(f32[10,98,1]{2,1,0:T(8,128)} %get-tuple-element.119) | data formatting | bytes 7840 | tf_op jit(solution)/shard_map/slice | solution.py:25
  87.4 1.9 %copy.62 = f32[10,98,1]{1,0,2:T(8,128)} copy(f32[10,98,1]{2,1,0:T(8,128)} %get-tuple-element.120) | data formatting | bytes 7840 | tf_op jit(solution)/shard_map/slice | solution.py:24
  89.3 4.7 %collective-permute-start.17 = (f32[10,98,1]{1,0,2:T(8,128)}, f32[10,98,1]{1,0,2:T(8,128)}, u32[]{:S(2)}, u32[]{:S(2)}) collective-permute-start(f32[10,98,1]{1,0,2:T(8,128)} %copy.62), channel_id=1, source_target_pairs={{0,1},{1,2},{2,3},{3,4},{4,5},{5,6},{6,7},{8,9},{9,10},{10,11},{11... | collective-permute-start | bytes 11768 | tf_op jit(solution)/shard_map/ppermute | solution.py:26
  94.0 2.6 %collective-permute-start.16 = (f32[10,98,1]{1,0,2:T(8,128)}, f32[10,98,1]{1,0,2:T(8,128)}, u32[]{:S(2)}, u32[]{:S(2)}) collective-permute-start(f32[10,98,1]{1,0,2:T(8,128)} %copy.60), channel_id=1, source_target_pairs={{1,0},{2,1},{3,2},{4,3},{5,4},{6,5},{7,6},{9,8},{10,9},{11,10},{12... | collective-permute-start | bytes 11768 | tf_op jit(solution)/shard_map/ppermute | solution.py:27
  96.6 2.8 %while.14 = (s32[]{:T(128)}, f32[96,256]{1,0:T(8,128)S(1)}, s32[]{:T(128)}, f32[4,96,256]{2,1,0:T(8,128)}, s32[]{:T(128)}, /*index=5*/s32[]{:T(128)}) while((s32[]{:T(128)}, f32[96,256]{1,0:T(8,128)S(1)}, s32[]{:T(128)}, f32[4,96,256]{2,1,0:T(8,128)}, s32[]{:T(128)}, /*index=5*/s32[]{:T(128)}) %tuple.53), condition=%wide.region_2.3_spmd.clone, body=%wide.region_1.2_spmd.clone.sunk | while | flops 73732 | bytes 295013 | solution.py:41
  99.5 2.8 %collective-permute-done.16 = f32[10,98,1]{1,0,2:T(8,128)} collective-permute-done((f32[10,98,1]{1,0,2:T(8,128)}, f32[10,98,1]{1,0,2:T(8,128)}, u32[]{:S(2)}, u32[]{:S(2)}) %collective-permute-start.16) | collective-permute-done | bytes 3952 | tf_op jit(solution)/shard_map/ppermute | solution.py:27
  102.3 1.8 %copy.61 = f32[10,98,1]{2,1,0:T(8,128)} copy(f32[10,98,1]{1,0,2:T(8,128)} %collective-permute-done.16) | data formatting | bytes 7840 | tf_op jit(solution)/shard_map/ppermute | solution.py:27
  104.1 1.8 %copy.63 = f32[10,98,1]{2,1,0:T(8,128)} copy(f32[10,98,1]{1,0,2:T(8,128)} %collective-permute-done.17) | data formatting | bytes 7840 | tf_op jit(solution)/shard_map/ppermute | solution.py:26
  105.8 8.4 %subtract_divide_fusion = (f32[8,96,256]{2,1,0:T(8,128)}, f32[8,96,256]{2,1,0:T(8,128)}, f32[8,96,256]{2,1,0:T(8,128)}) fusion(f32[8]{0:T(128)S(1)} %copy-done.17, f32[8,96,256]{2,1,0:T(8,128)S(1)} %copy-done.1, pred[8,96,256]{2,1,0:T(8,128)(4,1)} %get-tuple-element.118, pred[8,96,256]{2,1,0:T(8,128)(4,1)} %get-tuple-element.117, ...), kind=kLoop, calls=%fused_computation.109 | loop fusion | flops 26148864 | bytes 8412512 | tf_op jit(solution)/shard_map/div | solution.py:110
  (90 shorter events, 13.3 us)
Async XLA Ops:
  1.6 13.1 %collective-permute-start.1 = (f32[1,96,256]{2,1,0:T(8,128)S(1)}, f32[1,96,256]{2,1,0:T(8,128)S(1)}, u32[]{:S(2)}, u32[]{:S(2)}) collective-permute-start(f32[1,96,256]{2,1,0:T(8,128)S(1)} %get-tuple-element.135), channel_id=1, source_target_pairs={{128,0},{256,128},{384,256},{129,1},{257,129},{385,257},{130,2},{2... | collective-permute-start | bytes 294920 | tf_op jit(solution)/shard_map/ppermute | solution.py:27
  3.8 10.8 %collective-permute-start.3 = (f32[1,96,256]{2,1,0:T(8,128)S(1)}, f32[1,96,256]{2,1,0:T(8,128)S(1)}, u32[]{:S(2)}, u32[]{:S(2)}) collective-permute-start(f32[1,96,256]{2,1,0:T(8,128)S(1)} %get-tuple-element.136), channel_id=1, source_target_pairs={{0,128},{128,256},{256,384},{1,129},{129,257},{257,385},{2,130},{1... | collective-permute-start | bytes 294920 | tf_op jit(solution)/shard_map/ppermute | solution.py:26
  5.9 8.7 %copy-start = (f32[8,96,256]{2,1,0:T(8,128)S(1)}, f32[8,96,256]{2,1,0:T(8,128)}, u32[]{:S(2)}) copy-start(f32[8,96,256]{2,1,0:T(8,128)} %param.6) | copy-start | bytes 2359300
  9.0 12.9 %collective-permute-start.2 = (f32[1,96,256]{2,1,0:T(8,128)S(1)}, f32[1,96,256]{2,1,0:T(8,128)S(1)}, u32[]{:S(2)}, u32[]{:S(2)}) collective-permute-start(f32[1,96,256]{2,1,0:T(8,128)S(1)} %get-tuple-element.133), channel_id=1, source_target_pairs={{0,128},{128,256},{256,384},{1,129},{129,257},{257,385},{2,130},{1... | collective-permute-start | bytes 294920 | tf_op jit(solution)/shard_map/ppermute | solution.py:26
  10.9 10.9 %collective-permute-start = (f32[1,96,256]{2,1,0:T(8,128)S(1)}, f32[1,96,256]{2,1,0:T(8,128)S(1)}, u32[]{:S(2)}, u32[]{:S(2)}) collective-permute-start(f32[1,96,256]{2,1,0:T(8,128)S(1)} %get-tuple-element.134), channel_id=1, source_target_pairs={{128,0},{256,128},{384,256},{129,1},{257,129},{385,257},{130,2},{2... | collective-permute-start | bytes 294920 | tf_op jit(solution)/shard_map/ppermute | solution.py:27
  14.6 7.3 %copy-start.11 = (f32[1,96,256]{2,1,0:T(8,128)}, f32[1,96,256]{2,1,0:T(8,128)S(1)}, u32[]{:S(2)}) copy-start(f32[1,96,256]{2,1,0:T(8,128)S(1)} %collective-permute-done.3) | copy-start | bytes 294916
  14.7 14.4 %copy-start.10 = (f32[1,96,256]{2,1,0:T(8,128)}, f32[1,96,256]{2,1,0:T(8,128)S(1)}, u32[]{:S(2)}) copy-start(f32[1,96,256]{2,1,0:T(8,128)S(1)} %collective-permute-done.1) | copy-start | bytes 294916
  14.7 14.5 %copy-start.2 = (f32[10,96,256]{2,1,0:T(8,128)}, f32[10,96,256]{2,1,0:T(8,128)S(1)}, u32[]{:S(2)}) copy-start(f32[10,96,256]{2,1,0:T(8,128)S(1)} %constant_dynamic-update-slice_fusion) | copy-start | bytes 2949124
  14.8 14.2 %collective-permute-start.5 = (f32[10,1,256]{2,0,1:T(8,128)S(1)}, f32[10,1,256]{2,0,1:T(8,128)S(1)}, u32[]{:S(2)}, u32[]{:S(2)}) collective-permute-start(f32[10,1,256]{2,0,1:T(8,128)S(1)} %copy.65), channel_id=1, source_target_pairs={{8,0},{16,8},{24,16},{32,24},{40,32},{48,40},{56,48},{64,56},{72,6... | collective-permute-start | bytes 30728 | tf_op jit(solution)/shard_map/ppermute | solution.py:27
  17.7 11.3 %collective-permute-start.7 = (f32[10,1,256]{2,0,1:T(8,128)S(1)}, f32[10,1,256]{2,0,1:T(8,128)S(1)}, u32[]{:S(2)}, u32[]{:S(2)}) collective-permute-start(f32[10,1,256]{2,0,1:T(8,128)S(1)} %copy.67), channel_id=1, source_target_pairs={{0,8},{8,16},{16,24},{24,32},{32,40},{40,48},{48,56},{56,64},{64,7... | collective-permute-start | bytes 30728 | tf_op jit(solution)/shard_map/ppermute | solution.py:26
  21.9 29.6 %copy-start.7 = (f32[1,96,256]{2,1,0:T(8,128)}, f32[1,96,256]{2,1,0:T(8,128)S(1)}, u32[]{:S(2)}) copy-start(f32[1,96,256]{2,1,0:T(8,128)S(1)} %collective-permute-done) | copy-start | bytes 294916
  22.0 15.7 %collective-permute-start.4 = (f32[10,1,256]{2,0,1:T(8,128)S(1)}, f32[10,1,256]{2,0,1:T(8,128)S(1)}, u32[]{:S(2)}, u32[]{:S(2)}) collective-permute-start(f32[10,1,256]{2,0,1:T(8,128)S(1)} %copy.64), channel_id=1, source_target_pairs={{8,0},{16,8},{24,16},{32,24},{40,32},{48,40},{56,48},{64,56},{72,6... | collective-permute-start | bytes 30728 | tf_op jit(solution)/shard_map/ppermute | solution.py:27
  23.9 13.8 %collective-permute-start.6 = (f32[10,1,256]{2,0,1:T(8,128)S(1)}, f32[10,1,256]{2,0,1:T(8,128)S(1)}, u32[]{:S(2)}, u32[]{:S(2)}) collective-permute-start(f32[10,1,256]{2,0,1:T(8,128)S(1)} %copy.66), channel_id=1, source_target_pairs={{0,8},{8,16},{16,24},{24,32},{32,40},{40,48},{48,56},{56,64},{64,7... | collective-permute-start | bytes 30728 | tf_op jit(solution)/shard_map/ppermute | solution.py:26
  30.3 18.0 %collective-permute-start.11 = (f32[10,98,1]{1,0,2:T(8,128)S(1)}, f32[10,98,1]{1,0,2:T(8,128)S(1)}, u32[]{:S(2)}, u32[]{:S(2)}) collective-permute-start(f32[10,98,1]{1,0,2:T(8,128)S(1)} %copy.52), channel_id=1, source_target_pairs={{0,1},{1,2},{2,3},{3,4},{4,5},{5,6},{6,7},{8,9},{9,10},{10,11},{11... | collective-permute-start | bytes 11768 | tf_op jit(solution)/shard_map/ppermute | solution.py:26
  34.7 12.5 %collective-permute-start.9 = (f32[10,98,1]{1,0,2:T(8,128)S(1)}, f32[10,98,1]{1,0,2:T(8,128)S(1)}, u32[]{:S(2)}, u32[]{:S(2)}) collective-permute-start(f32[10,98,1]{1,0,2:T(8,128)S(1)} %copy.48), channel_id=1, source_target_pairs={{1,0},{2,1},{3,2},{4,3},{5,4},{6,5},{7,6},{9,8},{10,9},{11,10},{12... | collective-permute-start | bytes 11768 | tf_op jit(solution)/shard_map/ppermute | solution.py:27
  38.6 10.7 %collective-permute-start.8 = (f32[10,98,1]{1,0,2:T(8,128)S(1)}, f32[10,98,1]{1,0,2:T(8,128)S(1)}, u32[]{:S(2)}, u32[]{:S(2)}) collective-permute-start(f32[10,98,1]{1,0,2:T(8,128)S(1)} %copy.44), channel_id=1, source_target_pairs={{1,0},{2,1},{3,2},{4,3},{5,4},{6,5},{7,6},{9,8},{10,9},{11,10},{12... | collective-permute-start | bytes 11768 | tf_op jit(solution)/shard_map/ppermute | solution.py:27
  43.2 7.2 %collective-permute-start.10 = (f32[10,98,1]{1,0,2:T(8,128)S(1)}, f32[10,98,1]{1,0,2:T(8,128)S(1)}, u32[]{:S(2)}, u32[]{:S(2)}) collective-permute-start(f32[10,98,1]{1,0,2:T(8,128)S(1)} %copy.50), channel_id=1, source_target_pairs={{0,1},{1,2},{2,3},{3,4},{4,5},{5,6},{6,7},{8,9},{9,10},{10,11},{11... | collective-permute-start | bytes 11768 | tf_op jit(solution)/shard_map/ppermute | solution.py:26
  51.4 13.1 %copy-start.1 = (f32[8,96,256]{2,1,0:T(8,128)S(1)}, f32[8,96,256]{2,1,0:T(8,128)}, u32[]{:S(2)}) copy-start(f32[8,96,256]{2,1,0:T(8,128)} %param.7) | copy-start | bytes 2359300
  51.5 13.2 %copy-start.4 = (pred[8,96,256]{2,1,0:T(8,128)(4,1)S(1)}, pred[8,96,256]{2,1,0:T(8,128)(4,1)}, u32[]{:S(2)}) copy-start(pred[8,96,256]{2,1,0:T(8,128)(4,1)} %get-tuple-element.116) | copy-start | bytes 589828
  51.5 13.2 %copy-start.5 = (pred[8,96,256]{2,1,0:T(8,128)(4,1)S(1)}, pred[8,96,256]{2,1,0:T(8,128)(4,1)}, u32[]{:S(2)}) copy-start(pred[8,96,256]{2,1,0:T(8,128)(4,1)} %get-tuple-element.117) | copy-start | bytes 589828
  51.5 13.2 %copy-start.6 = (pred[8,96,256]{2,1,0:T(8,128)(4,1)S(1)}, pred[8,96,256]{2,1,0:T(8,128)(4,1)}, u32[]{:S(2)}) copy-start(pred[8,96,256]{2,1,0:T(8,128)(4,1)} %get-tuple-element.118) | copy-start | bytes 589828
  51.5 13.2 %copy-start.17 = (f32[8]{0:T(128)S(1)}, f32[8]{0:T(128)}, u32[]{:S(2)}) copy-start(f32[8]{0:T(128)} %param.9) | copy-start | bytes 100
  59.0 7.1 %collective-permute-start.13 = (f32[1,96,256]{2,1,0:T(8,128)S(1)}, f32[1,96,256]{2,1,0:T(8,128)S(1)}, u32[]{:S(2)}, u32[]{:S(2)}) collective-permute-start(f32[1,96,256]{2,1,0:T(8,128)S(1)} %get-tuple-element.131), channel_id=1, source_target_pairs={{0,128},{128,256},{256,384},{1,129},{129,257},{257,385},{2,130},{1... | collective-permute-start | bytes 294920 | tf_op jit(solution)/shard_map/ppermute | solution.py:26
  60.9 5.8 %collective-permute-start.12 = (f32[1,96,256]{2,1,0:T(8,128)S(1)}, f32[1,96,256]{2,1,0:T(8,128)S(1)}, u32[]{:S(2)}, u32[]{:S(2)}) collective-permute-start(f32[1,96,256]{2,1,0:T(8,128)S(1)} %get-tuple-element.132), channel_id=1, source_target_pairs={{128,0},{256,128},{384,256},{129,1},{257,129},{385,257},{130,2},{2... | collective-permute-start | bytes 294920 | tf_op jit(solution)/shard_map/ppermute | solution.py:27
  66.1 15.6 %copy-start.8 = (f32[1,96,256]{2,1,0:T(8,128)}, f32[1,96,256]{2,1,0:T(8,128)S(1)}, u32[]{:S(2)}) copy-start(f32[1,96,256]{2,1,0:T(8,128)S(1)} %collective-permute-done.13) | copy-start | bytes 294916
  66.8 14.9 %copy-start.9 = (f32[1,96,256]{2,1,0:T(8,128)}, f32[1,96,256]{2,1,0:T(8,128)S(1)}, u32[]{:S(2)}) copy-start(f32[1,96,256]{2,1,0:T(8,128)S(1)} %collective-permute-done.12) | copy-start | bytes 294916
  68.0 13.7 %collective-permute-start.14 = (f32[10,1,256]{2,0,1:T(8,128)}, f32[10,1,256]{2,0,1:T(8,128)}, u32[]{:S(2)}, u32[]{:S(2)}) collective-permute-start(f32[10,1,256]{2,0,1:T(8,128)} %copy.68), channel_id=1, source_target_pairs={{8,0},{16,8},{24,16},{32,24},{40,32},{48,40},{56,48},{64,56},{72,6... | collective-permute-start | bytes 30728 | tf_op jit(solution)/shard_map/ppermute | solution.py:27
  70.0 12.5 %collective-permute-start.15 = (f32[10,1,256]{2,0,1:T(8,128)}, f32[10,1,256]{2,0,1:T(8,128)}, u32[]{:S(2)}, u32[]{:S(2)}) collective-permute-start(f32[10,1,256]{2,0,1:T(8,128)} %copy.69), channel_id=1, source_target_pairs={{0,8},{8,16},{16,24},{24,32},{32,40},{40,48},{48,56},{56,64},{64,7... | collective-permute-start | bytes 30728 | tf_op jit(solution)/shard_map/ppermute | solution.py:26
  82.4 3.0 %copy-start.15 = (f32[10,1,256]{2,1,0:T(1,128)}, f32[10,1,256]{2,1,0:T(1,128)S(1)}, u32[]{:S(2)}) copy-start(f32[10,1,256]{2,1,0:T(1,128)S(1)} %copy.55) | copy-start | bytes 30724
  83.2 2.2 %copy-start.16 = (f32[10,1,256]{2,1,0:T(1,128)}, f32[10,1,256]{2,1,0:T(1,128)S(1)}, u32[]{:S(2)}) copy-start(f32[10,1,256]{2,1,0:T(1,128)S(1)} %copy.57) | copy-start | bytes 30724
  89.3 14.8 %collective-permute-start.17 = (f32[10,98,1]{1,0,2:T(8,128)}, f32[10,98,1]{1,0,2:T(8,128)}, u32[]{:S(2)}, u32[]{:S(2)}) collective-permute-start(f32[10,98,1]{1,0,2:T(8,128)} %copy.62), channel_id=1, source_target_pairs={{0,1},{1,2},{2,3},{3,4},{4,5},{5,6},{6,7},{8,9},{9,10},{10,11},{11... | collective-permute-start | bytes 11768 | tf_op jit(solution)/shard_map/ppermute | solution.py:26
  94.0 8.3 %collective-permute-start.16 = (f32[10,98,1]{1,0,2:T(8,128)}, f32[10,98,1]{1,0,2:T(8,128)}, u32[]{:S(2)}, u32[]{:S(2)}) collective-permute-start(f32[10,98,1]{1,0,2:T(8,128)} %copy.60), channel_id=1, source_target_pairs={{1,0},{2,1},{3,2},{4,3},{5,4},{6,5},{7,6},{9,8},{10,9},{11,10},{12... | collective-permute-start | bytes 11768 | tf_op jit(solution)/shard_map/ppermute | solution.py:27
  (4 other events, 2.7 us)
where the time goes:
time: 115 us; the launch traced here: 114 us
  starting transfers between devices  59.5 us (52%)
  other arithmetic  23.6 us (21%)
  local copies, waits for them, and re-layouts  19.6 us (17%)
  blocking collectives  6.6 us (6%)
  waiting for transfers between devices  3.51 us (3%)
  between operations  1.23 us (1%)
    ppermute x9, starting transfers between devices, padded_2(): before = lax.ppermute(last, axis, up)  33.5 us
    ppermute x9, starting transfers between devices, padded_2(): after = lax.ppermute(leading, axis, down)  26 us
    div x1, other arithmetic, body(): thickness_new = solid / (1.0 - porosity_new)  8.37 us
    add x1, other arithmetic, body(): middle = pressure + first_step  7.51 us
    all_gather x1, blocking collectives, carried_in(): pieces = lax.all_gather(value, axis)  6.6 us
    slice x7, local copies, waits for them, and re-layouts, padded_2(): leading = lax.slice_in_dim(array, 0, width, axis=dim)  5.02 us
    ppermute x6, local copies, waits for them, and re-layouts, padded_2(): before = lax.ppermute(last, axis, up)  4.63 us
    ppermute x6, local copies, waits for them, and re-layouts, padded_2(): after = lax.ppermute(leading, axis, down)  4.62 us
  transfers between devices with their start and end apart: 18, of which 2 were waited for; matrix products, arithmetic and copies ran while one was open for 12% of the time, Pallas kernels for 0%

commit v1 on v0

v1 whole, which is shorter than its diff:
```python
import math

import jax
import jax.numpy as jnp
from jax import lax
from jax.experimental import pallas as pl
from jax.experimental.pallas import tpu as pltpu
from jax.sharding import PartitionSpec as P

PHI_SURFACE = (0.45, 0.55, 0.65, 0.4)
ATHY_RATE = (0.25, 0.45, 0.8, 0.35)
MOB_BASE = (1.0, 0.0, -1.5, -0.5)
MOB_SLOPE = (6.0, 5.0, 8.0, 4.0)
GRAIN_DENSITY = (2.65, 2.68, 2.72, 2.71)
WATER_DENSITY = 1.03
SPECTRUM_MID = 1.0
SPECTRUM_HALF = 0.95
SIGMA_RATIO = SPECTRUM_MID / SPECTRUM_HALF
RHO_FIRST = 1.0 / SIGMA_RATIO
RHO_SECOND = 1.0 / (2.0 * SIGMA_RATIO - RHO_FIRST)

H_BASE = tuple(math.log(0.5) - b + 0.35 * s for b, s in zip(MOB_BASE, MOB_SLOPE))
H_SLOPE = tuple(-s for s in MOB_SLOPE)
ABSENT = 1e38

F32 = jnp.float32
L, R, C = 8, 96, 256
GR = 32
VMEM_LIMIT = 40 * 1024 * 1024


def recip(x):
    r = pl.reciprocal(x, approx=True)
    return r * (2.0 - x * r)


def present(h):
    return jnp.where(h == 0.0, ABSENT, h)


def classes(lith):
    return (lith & 1) == 1, lith >= 2


def pick(odd, upper, t):
    return jnp.where(upper, jnp.where(odd, t[3], t[2]), jnp.where(odd, t[1], t[0]))


def iota(shape, dim):
    return lax.broadcasted_iota(jnp.int32, shape, dim)


def roll(x, shift, axis):
    return pltpu.roll(x, shift % x.shape[axis], axis)


def start_kernel(par, solid, p, poro, lith, h, over, first, second):
    def chunk(i, carry):
        rows = pl.ds(pl.multiple_of(i * 32, 32), 32)
        total = jnp.zeros((32, C), F32)
        for z in range(L):
            odd, upper = classes(lith[z, rows, :])
            phi = poro[z, rows, :]
            h[z, rows, :] = jnp.exp(pick(odd, upper, H_BASE) + pick(odd, upper, H_SLOPE) * phi)
            load = (pick(odd, upper, GRAIN_DENSITY) + WATER_DENSITY * phi * recip(1.0 - phi)) * solid[z]
            over[z, rows, :] = total + 0.5 * load
            total = total + load
        first[pl.ds(pl.multiple_of(4 * R + i * 32, 32), 32), :] = total
        return carry

    lax.fori_loop(0, R // 32, chunk, 0)
    is_odd = par[0] == 1
    for ref, o, i in (
        (first, jnp.where(is_odd, 0, L - 1), jnp.where(is_odd, 1, L - 2)),
        (second, jnp.where(is_odd, L - 1, 0), jnp.where(is_odd, L - 2, 1)),
    ):
        ref[0:R, :] = h[o]
        ref[R : 2 * R, :] = p[o]
        ref[2 * R : 3 * R, :] = h[i]
        ref[3 * R : 4 * R, :] = p[i]


def pack_y_kernel(par, h, p, first, second, lo, hi):
    is_odd = par[0] == 1
    lane = iota((GR, 128), 1)

    def plane(arr, z, g, cols):
        rows = slice(GR * g, GR * g + GR)
        if 0 <= z < L:
            return (h, p)[arr][z, rows, cols]
        at = slice(R * arr + GR * g, R * arr + GR * g + GR)
        a, b = first[at, cols], second[at, cols]
        return jnp.where(is_odd, a, b) if z < 0 else jnp.where(is_odd, b, a)

    acc_lo = jnp.zeros((GR, 128), F32)
    acc_hi = jnp.zeros((GR, 128), F32)
    for g in range(3):
        for z in range(-1, L + 1):
            for arr in range(2):
                base = 40 * g + 4 * (z + 1) + 2 * arr
                here = (lane >= base) & (lane < base + 2)
                acc_lo = jnp.where(here, roll(plane(arr, z, g, slice(0, 128)), base, 1), acc_lo)
                acc_hi = jnp.where(here, roll(plane(arr, z, g, slice(C - 128, C)), base + 2, 1), acc_hi)
    lo[...] = acc_lo
    hi[...] = acc_hi


def pack_x_kernel(par, h, p, first, second, ylo, yhi, lo, hi):
    is_odd = par[0] == 1
    for ref, o, i, yrow in ((lo, 0, 1, 0), (hi, R - 1, R - 2, GR - 1)):
        for arr, own in ((0, h), (1, p)):
            at = slice(R * arr + o, R * arr + o + 1)
            a, b = first[at, :], second[at, :]
            top = 10 * arr
            ref[top : top + 1, :] = jnp.where(is_odd, a, b)
            for z in range(L):
                ref[top + 1 + z : top + 2 + z, :] = own[z, o : o + 1, :]
                ref[20 + L * arr + z : 21 + L * arr + z, :] = own[z, i : i + 1, :]
            ref[top + 9 : top + 10, :] = jnp.where(is_odd, b, a)
        ref[36:37, 0:128] = ylo[yrow : yrow + 1, :]
        ref[36:37, 128:256] = yhi[yrow : yrow + 1, :]
        ref[37:40, :] = jnp.zeros((3, C), F32)


def step(h, p, beside):
    total, flow = None, None
    weights = []
    for hn, pn in beside:
        t = recip(h + hn)
        weights.append(t)
        total = 1.0 + t if total is None else total + t
        flow = t * (pn - p) if flow is None else flow + t * (pn - p)
    inv = recip(total)
    return p + flow * inv, weights, inv


def main_kernel(
    par, solid, h, p, over, lith, first, second, above,
    ylo, yhi, wlo, whi, xlo, xhi, vlo, vhi,
    p_out, poro_out, thick_out,
    hs, ps, p1s, txl, txh, tyl, tyh, tz, inv,
    xh, xp, xq, yh, yp, yq,
):
    is_odd = par[0] == 1
    for z in range(L):
        hs[z + 2] = h[z]
        ps[z + 2] = p[z]
    for k, zl, zh in ((0, 1, 10), (1, 0, 11)):
        ha, hb = first[2 * k * R : (2 * k + 1) * R, :], second[2 * k * R : (2 * k + 1) * R, :]
        pa, pb = first[(2 * k + 1) * R : (2 * k + 2) * R, :], second[(2 * k + 1) * R : (2 * k + 2) * R, :]
        hs[zl] = present(jnp.where(is_odd, ha, hb))
        hs[zh] = present(jnp.where(is_odd, hb, ha))
        ps[zl] = jnp.where(is_odd, pa, pb)
        ps[zh] = jnp.where(is_odd, pb, pa)

    sub = iota((16, C), 0)
    lane = iota((16, C), 1)
    lane_x = iota((16, 128), 1)
    sub_x = iota((16, 128), 0)
    for s, msg, own, row_lane in ((0, xlo, vlo, 80), (1, xhi, vhi, 0)):
        def rows10(ref, at):
            return jnp.concatenate([ref[at : at + 10, :], jnp.zeros((6, C), F32)], axis=0)

        def rows8(ref, at):
            return jnp.concatenate([jnp.zeros((1, C), F32), ref[at : at + 8, :], jnp.zeros((7, C), F32)], axis=0)

        ho, po = present(rows10(msg, 0)), rows10(msg, 10)
        hi_, pi_ = present(rows8(msg, 20)), rows8(msg, 28)
        hw, pw = present(rows10(own, 0)), rows10(own, 10)

        def corner(cols, k):
            row = jnp.broadcast_to(msg[36:37, cols], (16, 128))
            return jnp.sum(jnp.where(lane_x == row_lane + 4 * sub_x + k, row, 0.0), axis=1, keepdims=True)

        left, right = slice(0, 128), slice(128, 256)
        hl = jnp.where(lane == 0, present(corner(left, 1)), roll(ho, 1, 1))
        pl_ = jnp.where(lane == 0, corner(left, 3), roll(po, 1, 1))
        hr = jnp.where(lane == C - 1, present(corner(right, 0)), roll(ho, -1, 1))
        pr = jnp.where(lane == C - 1, corner(right, 2), roll(po, -1, 1))
        beside = (
            (hi_, pi_), (hw, pw), (hl, pl_), (hr, pr),
            (roll(ho, 1, 0), roll(po, 1, 0)), (roll(ho, -1, 0), roll(po, -1, 0)),
        )
        q, _, _ = step(ho, po, beside)
        xh[s] = ho
        xp[s] = po
        xq[s] = q

    lane = iota((GR, 128), 1)
    sub = iota((GR, 128), 0)
    for s, msg, own, o, i, w, cols in (
        (0, ylo, wlo, 1, 0, 0, slice(0, 128)),
        (1, yhi, whi, 0, 1, 1, slice(128, 256)),
    ):
        m, v = msg[...], own[...]
        ho, po = present(roll(m, -o, 1)), roll(m, -o - 2, 1)
        hi_, pi_ = present(roll(m, -i, 1)), roll(m, -i - 2, 1)
        hw, pw = present(roll(v, -w, 1)), roll(v, -w - 2, 1)

        def along_x(f, k, fix):
            low = jnp.broadcast_to(fix(xlo[36:37, cols]), (GR, 128))
            high = jnp.broadcast_to(fix(xhi[36:37, cols]), (GR, 128))
            u = roll(f, 1, 0)
            u = jnp.where(sub == 0, jnp.where(lane < 40, roll(low, -80 - k, 1), roll(u, 40, 1)), u)
            d = roll(f, -1, 0)
            d = jnp.where(sub == GR - 1, jnp.where(lane >= 80, roll(high, 80 - k, 1), roll(d, -40, 1)), d)
            return u, d

        hu, hd = along_x(ho, o, present)
        pu, pd = along_x(po, o + 2, lambda t: t)
        beside = (
            (hi_, pi_), (hw, pw), (hu, pu), (hd, pd),
            (roll(ho, 4, 1), roll(po, 4, 1)), (roll(ho, -4, 1), roll(po, -4, 1)),
        )
        q, _, _ = step(ho, po, beside)
        yh[s] = ho
        yp[s] = po
        yq[s] = q

    row = iota((R, C), 0)
    col = iota((R, C), 1)

    def column(ref, s, z):
        f = ref[s]
        pieces = [roll(f, 128 - 40 * g - 4 * z, 1)[:, 0:1] for g in range(3)]
        return jnp.concatenate(pieces, axis=0)

    def lateral(f, z, rows_ref, cols_ref):
        up = jnp.where(row == 0, rows_ref[0, pl.ds(z, 1), :], roll(f, 1, 0))
        down = jnp.where(row == R - 1, rows_ref[1, pl.ds(z, 1), :], roll(f, -1, 0))
        left = jnp.where(col == 0, column(cols_ref, 0, z), roll(f, 1, 1))
        right = jnp.where(col == C - 1, column(cols_ref, 1, z), roll(f, -1, 1))
        return up, down, left, right

    def first_step(z, carry):
        hc, pc = hs[z + 1], ps[z + 1]
        hn = lateral(hc, z, xh, yh) + (hs[z], hs[z + 2])
        pn = lateral(pc, z, xp, yp) + (ps[z], ps[z + 2])
        q, weights, d = step(hc, pc, tuple(zip(hn, pn)))
        p1s[z] = q
        for ref, t in zip((txl, txh, tyl, tyh, tz), weights):
            ref[z] = t
        inv[z] = d
        return carry

    lax.fori_loop(0, L + 2, first_step, 0)

    base = above[...] + jnp.where(is_odd, first[4 * R : 5 * R, :], 0.0)

    def second_step(z, carry):
        k = z + 1
        q = p1s[k]
        pc = ps[k + 1]
        up, down, left, right = lateral(q, k, xq, yq)
        flow = txl[k] * (up - q) + txh[k] * (down - q)
        flow = flow + tyl[k] * (left - q) + tyh[k] * (right - q)
        flow = flow + tz[k] * (p1s[k - 1] - q) + tz[k + 1] * (p1s[k + 1] - q)
        d0 = q - pc
        pn = q + RHO_SECOND * RHO_FIRST * d0 + (2.0 * RHO_SECOND / SPECTRUM_HALF) * (flow - d0) * inv[k]
        p_out[z] = pn
        stress = jnp.maximum(base + over[z] - pn, 0.0)
        odd, upper = classes(lith[z])
        new = pick(odd, upper, PHI_SURFACE) * jnp.exp(-pick(odd, upper, ATHY_RATE) * stress)
        poro_out[z] = new
        thick_out[z] = solid[z] * recip(1.0 - new)
        return carry

    lax.fori_loop(0, L, second_step, 0)


def call(kernel, outs, n_smem, n_in, scratch=(), name=None):
    smem = pl.BlockSpec(memory_space=pltpu.SMEM)
    vmem = pl.BlockSpec(memory_space=pltpu.VMEM)
    return pl.pallas_call(
        kernel,
        out_shape=[jax.ShapeDtypeStruct(s, F32) for s in outs],
        in_specs=[smem] * n_smem + [vmem] * n_in,
        out_specs=[vmem] * len(outs),
        scratch_shapes=[pltpu.VMEM(s, F32) for s in scratch],
        compiler_params=pltpu.CompilerParams(vmem_limit_bytes=VMEM_LIMIT),
        name=name,
    )


def pair(axis, lo, hi):
    n = lax.axis_size(axis)
    up = [(i, i + 1) for i in range(n - 1)]
    down = [(j, i) for i, j in up]
    return lax.ppermute(hi, axis, up), lax.ppermute(lo, axis, down)


def body(p, poro, lith, solid):
    par = (lax.axis_index("slab") % 2).astype(jnp.int32).reshape(1)
    block = (L, R, C)
    h, over, first, second = call(
        start_kernel, [block, block, (5 * R, C), (4 * R, C)], 2, 3, name="start"
    )(par, solid, p, poro, lith)
    from_second = lax.ppermute(second, "slab", [(1, 2), (2, 1)])
    from_first = lax.ppermute(first, "slab", [(0, 1), (1, 0), (2, 3), (3, 2)])
    both = first[4 * R :] + from_first[4 * R :]
    above = lax.ppermute(both, "slab", [(1, 2), (0, 3)])
    wlo, whi = call(pack_y_kernel, [(GR, 128)] * 2, 1, 4, name="pack_y")(
        par, h, p, from_first, from_second
    )
    ylo, yhi = pair("mapy", wlo, whi)
    vlo, vhi = call(pack_x_kernel, [(40, C)] * 2, 1, 6, name="pack_x")(
        par, h, p, from_first, from_second, ylo, yhi
    )
    xlo, xhi = pair("mapx", vlo, vhi)
    plane = (10, R, C)
    scratch = [(12, R, C)] * 2 + [plane] * 7 + [(2, 16, C)] * 3 + [(2, GR, 128)] * 3
    return tuple(
        call(main_kernel, [block] * 3, 2, 15, scratch, name="main")(
            par, solid, h, p, over, lith, from_first, from_second, above,
            ylo, yhi, wlo, whi, xlo, xhi, vlo, vhi,
        )
    )


def solution(mesh):
    spec = P("slab", "mapx", "mapy")
    return jax.shard_map(
        body, mesh=mesh, in_specs=(spec, spec, spec, P("slab")), out_specs=(spec,) * 3, check_vma=False
    )
```

time: 115 us -> 52 us (0.45)
  the two profiles are of different devices: /device:TPU:366 before, /device:TPU:238 now
where the time goes in v1:
time: 52 us; the launch traced here: 51.6 us
  starting transfers between devices  20.4 us (39%)
  waiting for transfers between devices  16.1 us (31%)
  Pallas kernels  10.3 us (20%)
  local copies, waits for them, and re-layouts  4.05 us (8%)
  between operations  0.76 us (1%)
    ppermute x4, starting transfers between devices, pair(): return (lax.ppermute(hi, axis, up), lax.ppermute(lo, axis, down))  14.3 us
    ppermute x4, waiting for transfers between devices, pair(): return (lax.ppermute(hi, axis, up), lax.ppermute(lo, axis, down))  10.2 us
    pallas_call x1, Pallas kernels, body(): call(main_kernel, [block] * 3, 2, 15, scratch, name='main')  8.33 us
    ppermute x1, waiting for transfers between devices, body(): from_second = lax.ppermute(second, 'slab', [(1, 2), (2, 1)])  5.97 us
    unnamed x10, local copies, waits for them, and re-layouts  4.05 us
    ppermute x1, starting transfers between devices, body(): from_second = lax.ppermute(second, 'slab', [(1, 2), (2, 1)])  2.84 us
    ppermute x1, starting transfers between devices, body(): from_first = lax.ppermute(first, 'slab', [(0, 1), (1, 0), (2, 3), (3, 2)])  1.92 us
    pallas_call x1, Pallas kernels, body(): call(start_kernel, [block, block, (5 * R, C), (4 * R, C)], 2, 3, name='st...  1.33 us
  transfers between devices with their start and end apart: 7, of which 3 were waited for; matrix products, arithmetic and copies ran while one was open for 0% of the time, Pallas kernels for 1%

profile of v1, /device:TPU:238, one launch (start us, length us, event | category | flops | bytes accessed | tf_op | source)
XLA Modules:
  0.0 51.6 jit_solution(15257641674599846921)
XLA Ops:
  0.6 0.0 copy-start.4
  0.7 0.6 %copy-done.4 = f32[8]{0:T(128)S(1)} copy-done((f32[8]{0:T(128)S(1)}, f32[8]{0:T(128)}, u32[]{:S(2)}) %copy-start.4) | copy-done | bytes 56
  1.3 0.0 copy-start
  1.3 1.1 %copy-done = f32[8,96,256]{2,1,0:T(8,128)S(1)} copy-done((f32[8,96,256]{2,1,0:T(8,128)S(1)}, f32[8,96,256]{2,1,0:T(8,128)}, u32[]{:S(2)}) %copy-start) | copy-done | bytes 786456
  2.4 0.0 copy-start.2
  2.4 1.1 %copy-done.2 = s32[8,96,256]{2,1,0:T(8,128)S(1)} copy-done((s32[8,96,256]{2,1,0:T(8,128)S(1)}, s32[8,96,256]{2,1,0:T(8,128)}, u32[]{:S(2)}) %copy-start.2) | copy-done | bytes 786456
  3.6 0.0 copy-start.3
  3.6 1.1 %copy-done.3 = f32[8,96,256]{2,1,0:T(8,128)S(1)} copy-done((f32[8,96,256]{2,1,0:T(8,128)S(1)}, f32[8,96,256]{2,1,0:T(8,128)}, u32[]{:S(2)}) %copy-start.3) | copy-done | bytes 786456
  4.7 0.0 copy-start.1
  4.7 1.3 %start.1 = (f32[8,96,256]{2,1,0:T(8,128)S(1)}, f32[8,96,256]{2,1,0:T(8,128)S(1)}, f32[480,256]{1,0:T(8,128)S(1)}, f32[384,256]{1,0:T(8,128)S(1)}) custom-call(s32[1]{0:T(128)} %bitcast.par, f32[8]{0:T(128)S(1)} %copy-done.4, f32[8,96,256]{2,1,0:T(8,128)S(1)} %copy-done, f32[8,96,256]{2,1,0:T(8,128)S(1)} %copy-done.3, s32[8,96,256]{2,1,0:T(8,128)S(1)} %copy-done.2), custom_call_target="tpu_custom_call" | custom-call | tf_op jit(solution)/shard_map/start/pallas_call | solution.py:295
  6.0 1.9 %collective-permute-start = (f32[480,256]{1,0:T(8,128)S(1)}, f32[480,256]{1,0:T(8,128)S(1)}, u32[]{:S(2)}, u32[]{:S(2)}) collective-permute-start(f32[480,256]{1,0:T(8,128)S(1)} %get-tuple-element.13), channel_id=1, source_target_pairs={{0,128},{128,0},{256,384},{384,256},{1,129},{129,1},{257,385},{385... | collective-permute-start | bytes 1474568 | tf_op jit(solution)/shard_map/ppermute | solution.py:299
  8.0 2.8 %collective-permute-start.1 = (f32[384,256]{1,0:T(8,128)S(1)}, f32[384,256]{1,0:T(8,128)S(1)}, u32[]{:S(2)}, u32[]{:S(2)}) collective-permute-start(f32[384,256]{1,0:T(8,128)S(1)} %get-tuple-element.14), channel_id=1, source_target_pairs={{128,256},{256,128},{129,257},{257,129},{130,258},{258,130},{131,2... | collective-permute-start | bytes 1179656 | tf_op jit(solution)/shard_map/ppermute | solution.py:298
  10.8 0.0 collective-permute-done.first
  10.8 1.3 %collective-permute-start.2 = (f32[96,256]{1,0:T(8,128)S(1)}, f32[96,256]{1,0:T(8,128)S(1)}, u32[]{:S(2)}, u32[]{:S(2)}) collective-permute-start(f32[96,256]{1,0:T(8,128)S(1)} %slice_add_fusion), channel_id=1, source_target_pairs={{128,256},{0,384},{129,257},{1,385},{130,258},{2,386},{131,259},{3... | collective-permute-start | bytes 294920 | tf_op jit(solution)/shard_map/ppermute | solution.py:301
  12.1 6.0 %collective-permute-done.1.second = f32[384,256]{1,0:T(8,128)S(1)} collective-permute-done((f32[384,256]{1,0:T(8,128)S(1)}, f32[384,256]{1,0:T(8,128)S(1)}, u32[]{:S(2)}, u32[]{:S(2)}) %collective-permute-start.1) | collective-permute-done | bytes 393248 | tf_op jit(solution)/shard_map/ppermute | solution.py:298
  18.1 0.0 copy-done.1
  18.1 0.6 %pack_y.1 = (f32[32,128]{1,0:T(8,128)S(1)}, f32[32,128]{1,0:T(8,128)S(1)}) custom-call(s32[1]{0:T(128)} %bitcast.par, f32[8,96,256]{2,1,0:T(8,128)S(1)} %get-tuple-element.11.h, f32[8,96,256]{2,1,0:T(8,128)S(1)} %copy-done.1, f32[480,256]{1,0:T(8,128)S(1)} %collective-permute-done.first, f32[384,256]{1,0:T(8,128)S(1)} %collective-permute-done.1.second), custom_call_target="tpu_custom_call" | custom-call | tf_op jit(solution)/shard_map/pack_y/pallas_call | solution.py:302
  18.7 4.3 %collective-permute-start.3 = (f32[32,128]{1,0:T(8,128)S(1)}, f32[32,128]{1,0:T(8,128)S(1)}, u32[]{:S(2)}, u32[]{:S(2)}) collective-permute-start(f32[32,128]{1,0:T(8,128)S(1)} %get-tuple-element.15.whi), channel_id=1, source_target_pairs={{0,1},{1,2},{2,3},{3,4},{4,5},{5,6},{6,7},{8,9},{9,10},{10,11},{11... | collective-permute-start | bytes 49160 | tf_op jit(solution)/shard_map/ppermute | solution.py:289
  23.1 3.0 %collective-permute-start.4 = (f32[32,128]{1,0:T(8,128)S(1)}, f32[32,128]{1,0:T(8,128)S(1)}, u32[]{:S(2)}, u32[]{:S(2)}) collective-permute-start(f32[32,128]{1,0:T(8,128)S(1)} %get-tuple-element.16.wlo), channel_id=1, source_target_pairs={{1,0},{2,1},{3,2},{4,3},{5,4},{6,5},{7,6},{9,8},{10,9},{11,10},{12... | collective-permute-start | bytes 49160 | tf_op jit(solution)/shard_map/ppermute | solution.py:289
  26.1 0.0 collective-permute-done.3.ylo
  26.1 5.0 %collective-permute-done.4.yhi = f32[32,128]{1,0:T(8,128)S(1)} collective-permute-done((f32[32,128]{1,0:T(8,128)S(1)}, f32[32,128]{1,0:T(8,128)S(1)}, u32[]{:S(2)}, u32[]{:S(2)}) %collective-permute-start.4) | collective-permute-done | bytes 16416 | tf_op jit(solution)/shard_map/ppermute | solution.py:289
  31.1 5.0 %collective-permute-start.5 = (f32[40,256]{1,0:T(8,128)S(1)}, f32[40,256]{1,0:T(8,128)S(1)}, u32[]{:S(2)}, u32[]{:S(2)}) collective-permute-start(f32[40,256]{1,0:T(8,128)S(1)} %get-tuple-element.17.vhi), channel_id=1, source_target_pairs={{0,8},{8,16},{16,24},{24,32},{32,40},{40,48},{48,56},{56,64},{64,7... | collective-permute-start | bytes 122888 | tf_op jit(solution)/shard_map/ppermute | solution.py:289
  36.2 1.9 %collective-permute-start.6 = (f32[40,256]{1,0:T(8,128)S(1)}, f32[40,256]{1,0:T(8,128)S(1)}, u32[]{:S(2)}, u32[]{:S(2)}) collective-permute-start(f32[40,256]{1,0:T(8,128)S(1)} %get-tuple-element.18.vlo), channel_id=1, source_target_pairs={{8,0},{16,8},{24,16},{32,24},{40,32},{48,40},{56,48},{64,56},{72,6... | collective-permute-start | bytes 122888 | tf_op jit(solution)/shard_map/ppermute | solution.py:289
  38.1 0.0 collective-permute-done.5.xlo
  38.1 5.2 %collective-permute-done.6.xhi = f32[40,256]{1,0:T(8,128)S(1)} collective-permute-done((f32[40,256]{1,0:T(8,128)S(1)}, f32[40,256]{1,0:T(8,128)S(1)}, u32[]{:S(2)}, u32[]{:S(2)}) %collective-permute-start.6) | collective-permute-done | bytes 40992 | tf_op jit(solution)/shard_map/ppermute | solution.py:289
  43.3 0.0 collective-permute-done.2.above
  43.3 8.3 %main.1 = (f32[8,96,256]{2,1,0:T(8,128)}, f32[8,96,256]{2,1,0:T(8,128)}, f32[8,96,256]{2,1,0:T(8,128)}) custom-call(s32[1]{0:T(128)} %bitcast.par, f32[8]{0:T(128)S(1)} %copy-done.4, f32[8,96,256]{2,1,0:T(8,128)S(1)} %get-tuple-element.11.h, f32[8,96,256]{2,1,0:T(8,128)S(1)} %copy-done.1, f32[8,96,256]{2,1,0:T(8,128)S(1)} %get-tuple-element.12.over, ...), custom_call_target="tpu_custom_call" | custom-call | tf_op jit(solution)/shard_map/main/pallas_call | solution.py:313
  (2 shorter events, 0.1 us)
Async XLA Ops:
  0.6 0.7 %copy-start.4 = (f32[8]{0:T(128)S(1)}, f32[8]{0:T(128)}, u32[]{:S(2)}) copy-start(f32[8]{0:T(128)} %solid.3) | copy-start | bytes 100
  1.3 1.1 %copy-start = (f32[8,96,256]{2,1,0:T(8,128)S(1)}, f32[8,96,256]{2,1,0:T(8,128)}, u32[]{:S(2)}) copy-start(f32[8,96,256]{2,1,0:T(8,128)} %p.7) | copy-start | bytes 2359300
  2.4 1.1 %copy-start.2 = (s32[8,96,256]{2,1,0:T(8,128)S(1)}, s32[8,96,256]{2,1,0:T(8,128)}, u32[]{:S(2)}) copy-start(s32[8,96,256]{2,1,0:T(8,128)} %lith.3) | copy-start | bytes 2359300
  3.6 1.1 %copy-start.3 = (f32[8,96,256]{2,1,0:T(8,128)S(1)}, f32[8,96,256]{2,1,0:T(8,128)}, u32[]{:S(2)}) copy-start(f32[8,96,256]{2,1,0:T(8,128)} %poro.1) | copy-start | bytes 2359300
  4.7 13.4 %copy-start.1 = (f32[8,96,256]{2,1,0:T(8,128)S(1)}, f32[8,96,256]{2,1,0:T(8,128)}, u32[]{:S(2)}) copy-start(f32[8,96,256]{2,1,0:T(8,128)} %p.7) | copy-start | bytes 2359300
  6.0 4.8 %collective-permute-start = (f32[480,256]{1,0:T(8,128)S(1)}, f32[480,256]{1,0:T(8,128)S(1)}, u32[]{:S(2)}, u32[]{:S(2)}) collective-permute-start(f32[480,256]{1,0:T(8,128)S(1)} %get-tuple-element.13), channel_id=1, source_target_pairs={{0,128},{128,0},{256,384},{384,256},{1,129},{129,1},{257,385},{385... | collective-permute-start | bytes 1474568 | tf_op jit(solution)/shard_map/ppermute | solution.py:299
  8.0 10.1 %collective-permute-start.1 = (f32[384,256]{1,0:T(8,128)S(1)}, f32[384,256]{1,0:T(8,128)S(1)}, u32[]{:S(2)}, u32[]{:S(2)}) collective-permute-start(f32[384,256]{1,0:T(8,128)S(1)} %get-tuple-element.14), channel_id=1, source_target_pairs={{128,256},{256,128},{129,257},{257,129},{130,258},{258,130},{131,2... | collective-permute-start | bytes 1179656 | tf_op jit(solution)/shard_map/ppermute | solution.py:298
  10.8 32.4 %collective-permute-start.2 = (f32[96,256]{1,0:T(8,128)S(1)}, f32[96,256]{1,0:T(8,128)S(1)}, u32[]{:S(2)}, u32[]{:S(2)}) collective-permute-start(f32[96,256]{1,0:T(8,128)S(1)} %slice_add_fusion), channel_id=1, source_target_pairs={{128,256},{0,384},{129,257},{1,385},{130,258},{2,386},{131,259},{3... | collective-permute-start | bytes 294920 | tf_op jit(solution)/shard_map/ppermute | solution.py:301
  18.7 7.4 %collective-permute-start.3 = (f32[32,128]{1,0:T(8,128)S(1)}, f32[32,128]{1,0:T(8,128)S(1)}, u32[]{:S(2)}, u32[]{:S(2)}) collective-permute-start(f32[32,128]{1,0:T(8,128)S(1)} %get-tuple-element.15.whi), channel_id=1, source_target_pairs={{0,1},{1,2},{2,3},{3,4},{4,5},{5,6},{6,7},{8,9},{9,10},{10,11},{11... | collective-permute-start | bytes 49160 | tf_op jit(solution)/shard_map/ppermute | solution.py:289
  23.1 8.0 %collective-permute-start.4 = (f32[32,128]{1,0:T(8,128)S(1)}, f32[32,128]{1,0:T(8,128)S(1)}, u32[]{:S(2)}, u32[]{:S(2)}) collective-permute-start(f32[32,128]{1,0:T(8,128)S(1)} %get-tuple-element.16.wlo), channel_id=1, source_target_pairs={{1,0},{2,1},{3,2},{4,3},{5,4},{6,5},{7,6},{9,8},{10,9},{11,10},{12... | collective-permute-start | bytes 49160 | tf_op jit(solution)/shard_map/ppermute | solution.py:289
  31.1 7.0 %collective-permute-start.5 = (f32[40,256]{1,0:T(8,128)S(1)}, f32[40,256]{1,0:T(8,128)S(1)}, u32[]{:S(2)}, u32[]{:S(2)}) collective-permute-start(f32[40,256]{1,0:T(8,128)S(1)} %get-tuple-element.17.vhi), channel_id=1, source_target_pairs={{0,8},{8,16},{16,24},{24,32},{32,40},{40,48},{48,56},{56,64},{64,7... | collective-permute-start | bytes 122888 | tf_op jit(solution)/shard_map/ppermute | solution.py:289
  36.2 7.1 %collective-permute-start.6 = (f32[40,256]{1,0:T(8,128)S(1)}, f32[40,256]{1,0:T(8,128)S(1)}, u32[]{:S(2)}, u32[]{:S(2)}) collective-permute-start(f32[40,256]{1,0:T(8,128)S(1)} %get-tuple-element.18.vlo), channel_id=1, source_target_pairs={{8,0},{16,8},{24,16},{32,24},{40,32},{48,40},{56,48},{64,56},{72,6... | collective-permute-start | bytes 122888 | tf_op jit(solution)/shard_map/ppermute | solution.py:289

commit v2 on v1

v2 whole, which is shorter than its diff:
```python
import math

import jax
import jax.numpy as jnp
from jax import lax
from jax.experimental import pallas as pl
from jax.experimental.pallas import tpu as pltpu
from jax.sharding import PartitionSpec as P

PHI_SURFACE = (0.45, 0.55, 0.65, 0.4)
ATHY_RATE = (0.25, 0.45, 0.8, 0.35)
MOB_BASE = (1.0, 0.0, -1.5, -0.5)
MOB_SLOPE = (6.0, 5.0, 8.0, 4.0)
GRAIN_DENSITY = (2.65, 2.68, 2.72, 2.71)
WATER_DENSITY = 1.03
SPECTRUM_MID = 1.0
SPECTRUM_HALF = 0.95
SIGMA_RATIO = SPECTRUM_MID / SPECTRUM_HALF
RHO_FIRST = 1.0 / SIGMA_RATIO
RHO_SECOND = 1.0 / (2.0 * SIGMA_RATIO - RHO_FIRST)

H_BASE = tuple(math.log(0.5) - b + 0.35 * s for b, s in zip(MOB_BASE, MOB_SLOPE))
H_SLOPE = tuple(-s for s in MOB_SLOPE)
ABSENT = 1e38

F32 = jnp.float32
L, R, C = 8, 96, 256
GR = 32
VMEM_LIMIT = 40 * 1024 * 1024


def recip(x):
    r = pl.reciprocal(x, approx=True)
    return r * (2.0 - x * r)


def present(h):
    return jnp.where(h == 0.0, ABSENT, h)


def classes(lith):
    return (lith & 1) == 1, lith >= 2


def pick(odd, upper, t):
    return jnp.where(upper, jnp.where(odd, t[3], t[2]), jnp.where(odd, t[1], t[0]))


def iota(shape, dim):
    return lax.broadcasted_iota(jnp.int32, shape, dim)


def roll(x, shift, axis):
    return pltpu.roll(x, shift % x.shape[axis], axis)


def start_kernel(slab, p_in, poro_in, lith_in, solid_in, p, lith, h, over, first, second, poro, solid, sems, solid_sem):
    copies = []
    solid_copy = pltpu.make_async_copy(solid_in, solid, solid_sem)
    solid_copy.start()
    for z in range(L):
        row = []
        for k, (src, dst) in enumerate(((poro_in, poro), (lith_in, lith), (p_in, p))):
            copy = pltpu.make_async_copy(src.at[z], dst.at[z], sems.at[k, z])
            copy.start()
            row.append(copy)
        copies.append(row)
    solid_copy.wait()
    for z in range(L):
        copies[z][0].wait()
        copies[z][1].wait()

        def chunk(i, carry, z=z):
            rows = pl.ds(pl.multiple_of(i * 32, 32), 32)
            at = pl.ds(pl.multiple_of(4 * R + i * 32, 32), 32)
            odd, upper = classes(lith[z, rows, :])
            phi = poro[z, rows, :]
            h[z, rows, :] = jnp.exp(pick(odd, upper, H_BASE) + pick(odd, upper, H_SLOPE) * phi)
            load = (pick(odd, upper, GRAIN_DENSITY) + WATER_DENSITY * phi * recip(1.0 - phi)) * solid[z]
            if z == 0:
                over[z, rows, :] = 0.5 * load
                first[at, :] = load
            else:
                total = first[at, :]
                over[z, rows, :] = total + 0.5 * load
                first[at, :] = total + load
            return carry

        lax.fori_loop(0, R // 32, chunk, 0)
    for z in range(L):
        copies[z][2].wait()
    is_odd = (slab[0] & 1) == 1
    o, i = jnp.where(is_odd, 0, L - 1), jnp.where(is_odd, 1, L - 2)
    first[0:R, :] = h[o]
    first[R : 2 * R, :] = p[o]
    first[2 * R : 3 * R, :] = h[i]
    first[3 * R : 4 * R, :] = p[i]
    o = jnp.where(is_odd, L - 1, 0)
    second[0:R, :] = h[o]
    second[R : 2 * R, :] = p[o]


def pack_y_kernel(slab, h, p, mine, first, second, lo, hi, third):
    is_odd = (slab[0] & 1) == 1
    lane = iota((GR, 128), 1)

    def plane(arr, z, g, cols):
        rows = slice(GR * g, GR * g + GR)
        if 0 <= z < L:
            return (h, p)[arr][z, rows, cols]
        at = slice(R * arr + GR * g, R * arr + GR * g + GR)
        a, b = first[at, cols], second[at, cols]
        return jnp.where(is_odd, a, b) if z < 0 else jnp.where(is_odd, b, a)

    acc_lo = jnp.zeros((GR, 128), F32)
    acc_hi = jnp.zeros((GR, 128), F32)
    for g in range(3):
        for z in range(-1, L + 1):
            for arr in range(2):
                base = 40 * g + 4 * (z + 1) + 2 * arr
                here = (lane >= base) & (lane < base + 2)
                acc_lo = jnp.where(here, roll(plane(arr, z, g, slice(0, 128)), base, 1), acc_lo)
                acc_hi = jnp.where(here, roll(plane(arr, z, g, slice(C - 128, C)), base + 2, 1), acc_hi)
    lo[...] = acc_lo
    hi[...] = acc_hi
    i = jnp.where(is_odd, L - 2, 1)
    third[0:R, :] = h[i]
    third[R : 2 * R, :] = p[i]
    third[2 * R : 3 * R, :] = mine[4 * R : 5 * R, :] + first[4 * R : 5 * R, :]


def pack_x_kernel(slab, h, p, first, second, ylo, yhi, lo, hi):
    is_odd = (slab[0] & 1) == 1
    for ref, o, i, yrow in ((lo, 0, 1, 0), (hi, R - 1, R - 2, GR - 1)):
        for arr, own in ((0, h), (1, p)):
            at = slice(R * arr + o, R * arr + o + 1)
            a, b = first[at, :], second[at, :]
            top = 10 * arr
            ref[top : top + 1, :] = jnp.where(is_odd, a, b)
            for z in range(L):
                ref[top + 1 + z : top + 2 + z, :] = own[z, o : o + 1, :]
                ref[20 + L * arr + z : 21 + L * arr + z, :] = own[z, i : i + 1, :]
            ref[top + 9 : top + 10, :] = jnp.where(is_odd, b, a)
        ref[36:37, 0:128] = ylo[yrow : yrow + 1, :]
        ref[36:37, 128:256] = yhi[yrow : yrow + 1, :]
        ref[37:40, :] = jnp.zeros((3, C), F32)


def step(h, p, beside):
    total, flow = None, None
    for hn, pn in beside:
        t = recip(h + hn)
        total = 1.0 + t if total is None else total + t
        flow = t * (pn - p) if flow is None else flow + t * (pn - p)
    return p + flow * recip(total)


def beside_y(msgs, owns, corners):
    lane = iota((GR, 128), 1)
    sub = iota((GR, 128), 0)
    result = []
    for msg, own, o, i, w, cols in (
        (msgs[0], owns[0], 1, 0, 0, slice(0, 128)),
        (msgs[1], owns[1], 0, 1, 1, slice(128, 256)),
    ):
        m, v = msg[...], own[...]
        ho, po = present(roll(m, -o, 1)), roll(m, -o - 2, 1)
        hi_, pi_ = present(roll(m, -i, 1)), roll(m, -i - 2, 1)
        hw, pw = present(roll(v, -w, 1)), roll(v, -w - 2, 1)

        def along_x(f, k, fix):
            u = roll(f, 1, 0)
            u = jnp.where(sub == 0, roll(u, 40, 1), u)
            d = roll(f, -1, 0)
            d = jnp.where(sub == GR - 1, roll(d, -40, 1), d)
            if corners is not None:
                low = jnp.broadcast_to(fix(corners[0][36:37, cols]), (GR, 128))
                high = jnp.broadcast_to(fix(corners[1][36:37, cols]), (GR, 128))
                u = jnp.where((sub == 0) & (lane < 40), roll(low, -80 - k, 1), u)
                d = jnp.where((sub == GR - 1) & (lane >= 80), roll(high, 80 - k, 1), d)
            return u, d

        hu, hd = along_x(ho, o, present)
        pu, pd = along_x(po, o + 2, lambda t: t)
        q = step(ho, po, (
            (hi_, pi_), (hw, pw), (hu, pu), (hd, pd),
            (roll(ho, 4, 1), roll(po, 4, 1)), (roll(ho, -4, 1), roll(po, -4, 1)),
        ))
        result.append((ho, po, q))
    return result


def beside_x(msgs, owns, xh, xp, xq):
    lane = iota((16, C), 1)
    lane_x = iota((16, 128), 1)
    sub_x = iota((16, 128), 0)
    for s, row_lane in ((0, 80), (1, 0)):
        msg, own = msgs[s], owns[s]

        def rows10(ref, at):
            return jnp.concatenate([ref[at : at + 10, :], jnp.zeros((6, C), F32)], axis=0)

        def rows8(ref, at):
            return jnp.concatenate([jnp.zeros((1, C), F32), ref[at : at + 8, :], jnp.zeros((7, C), F32)], axis=0)

        ho, po = present(rows10(msg, 0)), rows10(msg, 10)
        hi_, pi_ = present(rows8(msg, 20)), rows8(msg, 28)
        hw, pw = present(rows10(own, 0)), rows10(own, 10)

        def corner(cols, k):
            row = jnp.broadcast_to(msg[36:37, cols], (16, 128))
            return jnp.sum(jnp.where(lane_x == row_lane + 4 * sub_x + k, row, 0.0), axis=1, keepdims=True)

        left, right = slice(0, 128), slice(128, 256)
        hl = jnp.where(lane == 0, present(corner(left, 1)), roll(ho, 1, 1))
        pl_ = jnp.where(lane == 0, corner(left, 3), roll(po, 1, 1))
        hr = jnp.where(lane == C - 1, present(corner(right, 0)), roll(ho, -1, 1))
        pr = jnp.where(lane == C - 1, corner(right, 2), roll(po, -1, 1))
        xh[s] = ho
        xp[s] = po
        xq[s] = step(ho, po, (
            (hi_, pi_), (hw, pw), (hl, pl_), (hr, pr),
            (roll(ho, 1, 0), roll(po, 1, 0)), (roll(ho, -1, 0), roll(po, -1, 0)),
        ))


def edge_columns(lo, hi, z, g):
    lane = iota((GR, 128), 1)
    at = 40 * g + 4 * (z + 1)
    return jnp.where(lane == 0, roll(lo, -at, 1), roll(hi, 127 - at, 1))


def around(before, here, after, edge):
    sub = iota((8, C), 0)
    lane = iota((8, 128), 1)
    up = roll(jnp.where(sub == 7, before, here), 1, 0)
    down = roll(jnp.where(sub == 0, after, here), -1, 0)
    a, b = here[:, :128], here[:, 128:]
    ra, rb = roll(a, 1, 1), roll(b, 1, 1)
    left = jnp.concatenate([jnp.where(lane == 0, edge, ra), jnp.where(lane == 0, ra, rb)], axis=1)
    ra, rb = roll(a, -1, 1), roll(b, -1, 1)
    right = jnp.concatenate([jnp.where(lane == 127, rb, ra), jnp.where(lane == 127, edge, rb)], axis=1)
    return up, down, left, right


def first_chunk(hval, pval, hedge, pedge, put):
    hc, pc = hval(-1), pval(-1)
    t = recip(hc[1] + hval(-2)[1])
    flow = t * (pc[1] - pval(-2)[1])
    for z in range(-1, L + 1):
        hn, pn = hval(z + 1), pval(z + 1)
        t2 = recip(hc[1] + hn[1])
        flow2 = t2 * (pn[1] - pc[1])
        h, p = hc[1], pc[1]
        total, change = 1.0 + (t + t2), flow2 - flow
        weights = []
        for hb, pb in zip(around(*hc, hedge(z)), around(*pc, pedge(z))):
            w = recip(h + hb)
            weights.append(w)
            total = total + w
            change = change + w * (pb - p)
        inv = recip(total)
        put(z, p + change * inv, weights, t, inv)
        hc, pc, t, flow = hn, pn, t2, flow2


def second_chunk(qval, qedge, weight, pval, base, over, lith, solid, put):
    low = qval(-1)[1]
    qc = qval(0)
    flow = weight(0, 4) * (qc[1] - low)
    for z in range(L):
        qn = qval(z + 1)
        flow2 = weight(z + 1, 4) * (qn[1] - qc[1])
        q = qc[1]
        change = flow2 - flow
        for k, qb in enumerate(around(*qc, qedge(z))):
            change = change + weight(z, k) * (qb - q)
        d0 = q - pval(z)
        pn = q + RHO_SECOND * RHO_FIRST * d0 + (2.0 * RHO_SECOND / SPECTRUM_HALF) * (change - d0) * weight(z, 5)
        stress = jnp.maximum(base + over(z) - pn, 0.0)
        odd, upper = classes(lith(z))
        new = pick(odd, upper, PHI_SURFACE) * jnp.exp(-pick(odd, upper, ATHY_RATE) * stress)
        put(z, pn, new, solid[z] * recip(1.0 - new))
        qc, flow = qn, flow2


def above_rows(slab, first, third, rows):
    base = jnp.where((slab[0] & 1) == 1, first[rows(4 * R), :], 0.0)
    return base + jnp.where(slab[0] >= 2, third[rows(2 * R), :], 0.0)


def inner_kernel(
    slab, solid, h, p, over, lith, first, second, third, ylo, yhi, wlo, whi,
    hz, pz, eh, ep, p1, out0, out1, out2,
    eq, wt, o0, o1, o2, sems,
):
    is_odd = (slab[0] & 1) == 1
    for k, (a, b) in enumerate(((first, second), (first, third))):
        at = 2 * R * k
        ha, hb = a[at : at + R, :], b[0:R, :]
        pa, pb = a[at + R : at + 2 * R, :], b[R : 2 * R, :]
        hz[2 * k] = present(jnp.where(is_odd, ha, hb))
        hz[2 * k + 1] = present(jnp.where(is_odd, hb, ha))
        pz[2 * k] = jnp.where(is_odd, pa, pb)
        pz[2 * k + 1] = jnp.where(is_odd, pb, pa)
    lo, hi = beside_y((ylo, yhi), (wlo, whi), None)
    for z in range(-1, L + 1):
        for g in range(3):
            rows = slice(GR * g, GR * g + GR)
            eh[z + 1, rows, :] = edge_columns(lo[0], hi[0], z, g)
            ep[z + 1, rows, :] = edge_columns(lo[1], hi[1], z, g)
            if 0 <= z < L:
                eq[z, rows, :] = edge_columns(lo[2], hi[2], z, g)

    def at8(i):
        return pl.ds(pl.multiple_of(8 * i, 8), 8)

    def triple(own, halo, i):
        here = (at8(jnp.maximum(i - 1, 0)), at8(i), at8(jnp.minimum(i + 1, R // 8 - 1)))

        def value(z):
            ref, k = (own, z) if 0 <= z < L else (halo, {-1: 0, L: 1, -2: 2, L + 1: 3}[z])
            return tuple(ref[k, rows, :] for rows in here)

        return value

    def chunk1(i, carry):
        rows = at8(i)

        def put(z, q, weights, t, inv):
            p1[z + 1, rows, :] = q
            if 0 <= z <= L:
                wt[4, z, rows, :] = t
            if 0 <= z < L:
                for k, w in enumerate(weights):
                    wt[k, z, rows, :] = w
                wt[5, z, rows, :] = inv

        first_chunk(
            triple(h, hz, i), triple(p, pz, i),
            lambda z: eh[z + 1, rows, :], lambda z: ep[z + 1, rows, :], put,
        )
        return carry

    lax.fori_loop(0, R // 8, chunk1, 0)

    def chunk2(i, carry):
        rows = at8(i)
        here = (at8(i - 1), rows, at8(i + 1))

        def put(z, a, b, c):
            o0[z, rows, :] = a
            o1[z, rows, :] = b
            o2[z, rows, :] = c

        second_chunk(
            lambda z: tuple(p1[z + 1, r, :] for r in here),
            lambda z: eq[z, rows, :],
            lambda z, k: wt[k, z, rows, :],
            lambda z: p[z, rows, :],
            above_rows(slab, first, third, lambda top: pl.ds(pl.multiple_of(top + 8 * i, 8), 8)),
            lambda z: over[z, rows, :],
            lambda z: lith[z, rows, :],
            solid, put,
        )
        return carry

    lax.fori_loop(1, R // 8 - 1, chunk2, 0)
    rows = pl.ds(8, R - 16)
    copies = [
        pltpu.make_async_copy(src.at[:, rows, :], dst.at[:, rows, :], sems.at[k])
        for k, (src, dst) in enumerate(((o0, out0), (o1, out1), (o2, out2)))
    ]
    for copy in copies:
        copy.start()
    for copy in copies:
        copy.wait()


def outer_kernel(
    slab, solid, h, p, over, lith, first, third, ylo, yhi, wlo, whi, xlo, xhi, vlo, vhi,
    hz, pz, eh, ep, p1, in0, in1, in2,
    out0, out1, out2,
    xh, xp, xq, q1, wt, o0, o1, o2, sems,
):
    beside_x((xlo, xhi), (vlo, vhi), xh, xp, xq)
    lo, hi = beside_y((ylo, yhi), (wlo, whi), (xlo, xhi))
    copies = []
    for s, top, g, part in ((0, 0, 0, slice(0, 8)), (1, R - 8, 2, slice(GR - 8, GR))):
        rows = slice(top, top + 8)
        near = slice(8, 16) if s == 0 else slice(R - 16, R - 8)

        def triple(own, halo, strip, s=s, rows=rows, near=near):
            def value(z):
                ref, k = (own, z) if 0 <= z < L else (halo, {-1: 0, L: 1, -2: 2, L + 1: 3}[z])
                here, inside = ref[k, rows, :], ref[k, near, :]
                if z < -1 or z > L:
                    return here, here, here
                row = jnp.broadcast_to(strip[s, z + 1 : z + 2, :], (8, C))
                return (row, here, inside) if s == 0 else (inside, here, row)

            return value

        def put(z, q, weights, t, inv, s=s):
            q1[s, z + 1] = q
            if 0 <= z <= L:
                wt[s, 4, z] = t
            if 0 <= z < L:
                for k, w in enumerate(weights):
                    wt[s, k, z] = w
                wt[s, 5, z] = inv

        first_chunk(
            triple(h, hz, xh), triple(p, pz, xp),
            lambda z: eh[z + 1, rows, :], lambda z: ep[z + 1, rows, :], put,
        )

        def q_triple(z, s=s, near=near):
            here = q1[s, z + 1]
            if z < 0 or z >= L:
                return here, here, here
            row = jnp.broadcast_to(xq[s, z + 1 : z + 2, :], (8, C))
            inside = p1[z + 1, near, :]
            return (row, here, inside) if s == 0 else (inside, here, row)

        def put2(z, a, b, c, s=s):
            o0[s, z] = a
            o1[s, z] = b
            o2[s, z] = c

        second_chunk(
            q_triple,
            lambda z: edge_columns(lo[2], hi[2], z, g)[part],
            lambda z, k: wt[s, k, z],
            lambda z: p[z, rows, :],
            above_rows(slab, first, third, lambda t: slice(t + top, t + top + 8)),
            lambda z: over[z, rows, :],
            lambda z: lith[z, rows, :],
            solid, put2,
        )
        for k, (src, dst) in enumerate(((o0, out0), (o1, out1), (o2, out2))):
            copy = pltpu.make_async_copy(src.at[s], dst.at[:, rows, :], sems.at[s, k])
            copy.start()
            copies.append(copy)
    for copy in copies:
        copy.wait()


SMEM, VMEM, HBM = pltpu.SMEM, pltpu.VMEM, pltpu.HBM


def call(kernel, name, ins, outs, scratch=(), aliases=None):
    return pl.pallas_call(
        kernel,
        out_shape=[jax.ShapeDtypeStruct(s, t) for s, t, _ in outs],
        in_specs=[pl.BlockSpec(memory_space=m) for m in ins],
        out_specs=[pl.BlockSpec(memory_space=m) for _, _, m in outs],
        scratch_shapes=list(scratch),
        input_output_aliases=aliases or {},
        compiler_params=pltpu.CompilerParams(vmem_limit_bytes=VMEM_LIMIT),
        name=name,
    )


def pair(axis, lo, hi):
    n = lax.axis_size(axis)
    up = [(i, i + 1) for i in range(n - 1)]
    down = [(j, i) for i, j in up]
    return lax.ppermute(hi, axis, up), lax.ppermute(lo, axis, down)


def vm(*shape):
    return (shape, F32, VMEM)


def body(p_in, poro, lith_in, solid):
    p_in, poro, lith_in, solid_in = (pltpu.with_memory_space_constraint(a, HBM) for a in (p_in, poro, lith_in, solid))
    slab = lax.axis_index("slab").astype(jnp.int32).reshape(1)
    block = (L, R, C)
    dma = pltpu.SemaphoreType.DMA
    p, lith, h, over, first, second = call(
        start_kernel, "start", [SMEM] + [HBM] * 4,
        [vm(*block), (block, jnp.int32, VMEM), vm(*block), vm(*block), vm(5 * R, C), vm(2 * R, C)],
        [VMEM(block, F32), SMEM((L,), F32), dma((3, L)), dma(())],
    )(slab, p_in, poro, lith_in, solid_in)
    second_in = lax.ppermute(second, "slab", [(1, 2), (2, 1)])
    first_in = lax.ppermute(first, "slab", [(0, 1), (1, 0), (2, 3), (3, 2)])
    wlo, whi, third = call(
        pack_y_kernel, "pack_y", [SMEM] + [VMEM] * 5, [vm(GR, 128), vm(GR, 128), vm(3 * R, C)]
    )(slab, h, p, first, first_in, second_in)
    ylo, yhi = pair("mapy", wlo, whi)
    third_in = lax.ppermute(third, "slab", [(1, 2), (2, 1), (0, 3)])
    vlo, vhi = call(pack_x_kernel, "pack_x", [SMEM] + [VMEM] * 6, [vm(40, C)] * 2)(
        slab, h, p, first_in, second_in, ylo, yhi
    )
    xlo, xhi = pair("mapx", vlo, vhi)
    hbm = (block, F32, HBM)
    hz, pz, eh, ep, p1, *outs = call(
        inner_kernel, "inner", [SMEM] * 2 + [VMEM] * 11,
        [vm(4, R, C)] * 2 + [vm(L + 2, R, 128)] * 2 + [vm(L + 2, R, C)] + [hbm] * 3,
        [VMEM((L, R, 128), F32), VMEM((6, L + 1, R, C), F32)] + [VMEM(block, F32)] * 3 + [dma((3,))],
    )(slab, solid, h, p, over, lith, first_in, second_in, third_in, ylo, yhi, wlo, whi)
    return tuple(
        call(
            outer_kernel, "outer", [SMEM] * 2 + [VMEM] * 19 + [HBM] * 3, [hbm] * 3,
            [VMEM((2, 16, C), F32)] * 3
            + [VMEM((2, L + 2, 8, C), F32), VMEM((2, 6, L + 1, 8, C), F32)]
            + [VMEM((2, L, 8, C), F32)] * 3 + [dma((2, 3))],
            {21: 0, 22: 1, 23: 2},
        )(
            slab, solid, h, p, over, lith, first_in, third_in, ylo, yhi, wlo, whi, xlo, xhi, vlo, vhi,
            hz, pz, eh, ep, p1, *outs,
        )
    )


def solution(mesh):
    spec = P("slab", "mapx", "mapy")
    return jax.shard_map(
        body, mesh=mesh, in_specs=(spec, spec, spec, P("slab")), out_specs=(spec,) * 3, check_vma=False
    )
```

time: 52 us -> 44.4 us (0.85)
  the two profiles are of different devices: /device:TPU:238 before, /device:TPU:262 now
where the time goes in v2:
time: 44.4 us; the launch traced here: 44.1 us
  starting transfers between devices  22 us (50%)
  Pallas kernels  11.9 us (27%)
  waiting for transfers between devices  8.86 us (20%)
  between operations  0.76 us (2%)
  local copies, waits for them, and re-layouts  0.65 us (1%)
    ppermute x4, starting transfers between devices, pair(): return (lax.ppermute(hi, axis, up), lax.ppermute(lo, axis, down))  14.4 us
    pallas_call x1, Pallas kernels, body(): call(inner_kernel, 'inner', [SMEM] * 2 + [VMEM] * 11, [vm(4, R, C)] * 2 +...  6.73 us
    ppermute x4, waiting for transfers between devices, pair(): return (lax.ppermute(hi, axis, up), lax.ppermute(lo, axis, down))  4.72 us
    ppermute x1, waiting for transfers between devices, body(): second_in = lax.ppermute(second, 'slab', [(1, 2), (2, 1)])  4.14 us
    ppermute x1, starting transfers between devices, body(): second_in = lax.ppermute(second, 'slab', [(1, 2), (2, 1)])  2.84 us
    ppermute x1, starting transfers between devices, body(): third_in = lax.ppermute(third, 'slab', [(1, 2), (2, 1), (0, 3)])  2.84 us
    pallas_call x1, Pallas kernels, body(): call(outer_kernel, 'outer', [SMEM] * 2 + [VMEM] * 19 + [HBM] * 3, [hbm] *...  2.29 us
    pallas_call x1, Pallas kernels, body(): call(start_kernel, 'start', [SMEM] + [HBM] * 4, [vm(*block), (block, jnp....  2.18 us
  transfers between devices with their start and end apart: 7, of which 2 were waited for; matrix products, arithmetic and copies ran while one was open for 0% of the time, Pallas kernels for 15%

profile of v2, /device:TPU:262, one launch (start us, length us, event | category | flops | bytes accessed | tf_op | source)
XLA Modules:
  0.0 44.1 jit_solution(16020325642456322755)
XLA Ops:
  0.6 2.2 %start.1 = (f32[8,96,256]{2,1,0:T(8,128)S(1)}, s32[8,96,256]{2,1,0:T(8,128)S(1)}, f32[8,96,256]{2,1,0:T(8,128)S(1)}, f32[8,96,256]{2,1,0:T(8,128)S(1)}, f32[480,256]{1,0:T(8,128)S(1)}, /*index=5*/f32[192,256]{1,0:T(8,128)S(1)}) custom-call(s32[1]{0:T(128)} %bitcast.slab, f32[8,96,256]{2,1,0:T(8,128)} %p_in.1, f32[8,96,256]{2,1,0:T(8,128)} %poro_in.1, ...), custom_call_target="tpu_custom_call" | custom-call | tf_op jit(solution)/shard_map/start/pallas_call | solution.py:481
  2.8 1.9 %collective-permute-start = (f32[480,256]{1,0:T(8,128)S(1)}, f32[480,256]{1,0:T(8,128)S(1)}, u32[]{:S(2)}, u32[]{:S(2)}) collective-permute-start(f32[480,256]{1,0:T(8,128)S(1)} %get-tuple-element.26.mine), channel_id=1, source_target_pairs={{0,128},{128,0},{256,384},{384,256},{1,129},{129,1},{257,385},{385... | collective-permute-start | bytes 1474568 | tf_op jit(solution)/shard_map/ppermute | solution.py:487
  4.7 2.8 %collective-permute-start.1 = (f32[192,256]{1,0:T(8,128)S(1)}, f32[192,256]{1,0:T(8,128)S(1)}, u32[]{:S(2)}, u32[]{:S(2)}) collective-permute-start(f32[192,256]{1,0:T(8,128)S(1)} %get-tuple-element.27), channel_id=1, source_target_pairs={{128,256},{256,128},{129,257},{257,129},{130,258},{258,130},{131,2... | collective-permute-start | bytes 589832 | tf_op jit(solution)/shard_map/ppermute | solution.py:486
  7.6 4.1 %collective-permute-done.1.second = f32[192,256]{1,0:T(8,128)S(1)} collective-permute-done((f32[192,256]{1,0:T(8,128)S(1)}, f32[192,256]{1,0:T(8,128)S(1)}, u32[]{:S(2)}, u32[]{:S(2)}) %collective-permute-start.1) | collective-permute-done | bytes 196640 | tf_op jit(solution)/shard_map/ppermute | solution.py:486
  11.7 0.0 collective-permute-done.first
  11.7 0.6 %pack_y.1 = (f32[32,128]{1,0:T(8,128)S(1)}, f32[32,128]{1,0:T(8,128)S(1)}, f32[288,256]{1,0:T(8,128)S(1)}) custom-call(s32[1]{0:T(128)} %bitcast.slab, f32[8,96,256]{2,1,0:T(8,128)S(1)} %get-tuple-element.22.h, f32[8,96,256]{2,1,0:T(8,128)S(1)} %get-tuple-element.23.p, f32[480,256]{1,0:T(8,128)S(1)} %get-tuple-element.26.mine, ...), custom_call_target="tpu_custom_call" | custom-call | tf_op jit(solution)/shard_map/pack_y/pallas_call | solution.py:488
  12.4 2.8 %collective-permute-start.2 = (f32[288,256]{1,0:T(8,128)S(1)}, f32[288,256]{1,0:T(8,128)S(1)}, u32[]{:S(2)}, u32[]{:S(2)}) collective-permute-start(f32[288,256]{1,0:T(8,128)S(1)} %get-tuple-element.28), channel_id=1, source_target_pairs={{128,256},{256,128},{0,384},{129,257},{257,129},{1,385},{130,258},... | collective-permute-start | bytes 884744 | tf_op jit(solution)/shard_map/ppermute | solution.py:492
  15.2 4.0 %collective-permute-start.3 = (f32[32,128]{1,0:T(8,128)S(1)}, f32[32,128]{1,0:T(8,128)S(1)}, u32[]{:S(2)}, u32[]{:S(2)}) collective-permute-start(f32[32,128]{1,0:T(8,128)S(1)} %get-tuple-element.29.whi), channel_id=1, source_target_pairs={{0,1},{1,2},{2,3},{3,4},{4,5},{5,6},{6,7},{8,9},{9,10},{10,11},{11... | collective-permute-start | bytes 49160 | tf_op jit(solution)/shard_map/ppermute | solution.py:469
  19.2 3.3 %collective-permute-start.4 = (f32[32,128]{1,0:T(8,128)S(1)}, f32[32,128]{1,0:T(8,128)S(1)}, u32[]{:S(2)}, u32[]{:S(2)}) collective-permute-start(f32[32,128]{1,0:T(8,128)S(1)} %get-tuple-element.30.wlo), channel_id=1, source_target_pairs={{1,0},{2,1},{3,2},{4,3},{5,4},{6,5},{7,6},{9,8},{10,9},{11,10},{12... | collective-permute-start | bytes 49160 | tf_op jit(solution)/shard_map/ppermute | solution.py:469
  22.6 0.0 collective-permute-done.3.ylo
  22.6 4.7 %collective-permute-done.4.yhi = f32[32,128]{1,0:T(8,128)S(1)} collective-permute-done((f32[32,128]{1,0:T(8,128)S(1)}, f32[32,128]{1,0:T(8,128)S(1)}, u32[]{:S(2)}, u32[]{:S(2)}) %collective-permute-start.4) | collective-permute-done | bytes 16416 | tf_op jit(solution)/shard_map/ppermute | solution.py:469
  27.3 2.9 %collective-permute-start.5 = (f32[40,256]{1,0:T(8,128)S(1)}, f32[40,256]{1,0:T(8,128)S(1)}, u32[]{:S(2)}, u32[]{:S(2)}) collective-permute-start(f32[40,256]{1,0:T(8,128)S(1)} %get-tuple-element.31.vhi), channel_id=1, source_target_pairs={{0,8},{8,16},{16,24},{24,32},{32,40},{40,48},{48,56},{56,64},{64,7... | collective-permute-start | bytes 122888 | tf_op jit(solution)/shard_map/ppermute | solution.py:469
  30.3 4.1 %collective-permute-start.6 = (f32[40,256]{1,0:T(8,128)S(1)}, f32[40,256]{1,0:T(8,128)S(1)}, u32[]{:S(2)}, u32[]{:S(2)}) collective-permute-start(f32[40,256]{1,0:T(8,128)S(1)} %get-tuple-element.32.vlo), channel_id=1, source_target_pairs={{8,0},{16,8},{24,16},{32,24},{40,32},{48,40},{56,48},{64,56},{72,6... | collective-permute-start | bytes 122888 | tf_op jit(solution)/shard_map/ppermute | solution.py:469
  34.4 0.0 collective-permute-done.2.third
  34.4 0.0 copy-start
  34.4 0.6 %copy-done = f32[8]{0:T(128)S(1)} copy-done((f32[8]{0:T(128)S(1)}, f32[8]{0:T(128)}, u32[]{:S(2)}) %copy-start) | copy-done | bytes 56
  35.1 6.7 %inner.1 = (f32[4,96,256]{2,1,0:T(8,128)S(1)}, f32[4,96,256]{2,1,0:T(8,128)S(1)}, f32[10,96,128]{2,1,0:T(8,128)S(1)}, f32[10,96,128]{2,1,0:T(8,128)S(1)}, f32[10...) custom-call(s32[1]{0:T(128)} %bitcast.slab, f32[8]{0:T(128)S(1)} %copy-done, ...), custom_call_target="tpu_custom_call" | custom-call | tf_op jit(solution)/shard_map/inner/pallas_call | solution.py:498
  41.8 0.0 collective-permute-done.5.xlo
  41.8 0.0 collective-permute-done.6.xhi
  41.8 2.3 %outer.1 = (f32[8,96,256]{2,1,0:T(8,128)}, f32[8,96,256]{2,1,0:T(8,128)}, f32[8,96,256]{2,1,0:T(8,128)}) custom-call(s32[1]{0:T(128)} %bitcast.slab, f32[8]{0:T(128)S(1)} %copy-done, f32[8,96,256]{2,1,0:T(8,128)S(1)} %get-tuple-element.22.h, f32[8,96,256]{2,1,0:T(8,128)S(1)} %get-tuple-element.23.p, ...), custom_call_target="tpu_custom_call", output_to_operand_aliasing={{0}: (21, {}), {1}: (22, {}), {2}: (23, {})} | custom-call | tf_op jit(solution)/shard_map/outer/pallas_call | solution.py:504
  (1 shorter events, 0.0 us)
Async XLA Ops:
  2.8 8.9 %collective-permute-start = (f32[480,256]{1,0:T(8,128)S(1)}, f32[480,256]{1,0:T(8,128)S(1)}, u32[]{:S(2)}, u32[]{:S(2)}) collective-permute-start(f32[480,256]{1,0:T(8,128)S(1)} %get-tuple-element.26.mine), channel_id=1, source_target_pairs={{0,128},{128,0},{256,384},{384,256},{1,129},{129,1},{257,385},{385... | collective-permute-start | bytes 1474568 | tf_op jit(solution)/shard_map/ppermute | solution.py:487
  4.7 7.0 %collective-permute-start.1 = (f32[192,256]{1,0:T(8,128)S(1)}, f32[192,256]{1,0:T(8,128)S(1)}, u32[]{:S(2)}, u32[]{:S(2)}) collective-permute-start(f32[192,256]{1,0:T(8,128)S(1)} %get-tuple-element.27), channel_id=1, source_target_pairs={{128,256},{256,128},{129,257},{257,129},{130,258},{258,130},{131,2... | collective-permute-start | bytes 589832 | tf_op jit(solution)/shard_map/ppermute | solution.py:486
  12.4 22.0 %collective-permute-start.2 = (f32[288,256]{1,0:T(8,128)S(1)}, f32[288,256]{1,0:T(8,128)S(1)}, u32[]{:S(2)}, u32[]{:S(2)}) collective-permute-start(f32[288,256]{1,0:T(8,128)S(1)} %get-tuple-element.28), channel_id=1, source_target_pairs={{128,256},{256,128},{0,384},{129,257},{257,129},{1,385},{130,258},... | collective-permute-start | bytes 884744 | tf_op jit(solution)/shard_map/ppermute | solution.py:492
  15.2 7.4 %collective-permute-start.3 = (f32[32,128]{1,0:T(8,128)S(1)}, f32[32,128]{1,0:T(8,128)S(1)}, u32[]{:S(2)}, u32[]{:S(2)}) collective-permute-start(f32[32,128]{1,0:T(8,128)S(1)} %get-tuple-element.29.whi), channel_id=1, source_target_pairs={{0,1},{1,2},{2,3},{3,4},{4,5},{5,6},{6,7},{8,9},{9,10},{10,11},{11... | collective-permute-start | bytes 49160 | tf_op jit(solution)/shard_map/ppermute | solution.py:469
  19.2 8.0 %collective-permute-start.4 = (f32[32,128]{1,0:T(8,128)S(1)}, f32[32,128]{1,0:T(8,128)S(1)}, u32[]{:S(2)}, u32[]{:S(2)}) collective-permute-start(f32[32,128]{1,0:T(8,128)S(1)} %get-tuple-element.30.wlo), channel_id=1, source_target_pairs={{1,0},{2,1},{3,2},{4,3},{5,4},{6,5},{7,6},{9,8},{10,9},{11,10},{12... | collective-permute-start | bytes 49160 | tf_op jit(solution)/shard_map/ppermute | solution.py:469
  27.3 14.5 %collective-permute-start.5 = (f32[40,256]{1,0:T(8,128)S(1)}, f32[40,256]{1,0:T(8,128)S(1)}, u32[]{:S(2)}, u32[]{:S(2)}) collective-permute-start(f32[40,256]{1,0:T(8,128)S(1)} %get-tuple-element.31.vhi), channel_id=1, source_target_pairs={{0,8},{8,16},{16,24},{24,32},{32,40},{40,48},{48,56},{56,64},{64,7... | collective-permute-start | bytes 122888 | tf_op jit(solution)/shard_map/ppermute | solution.py:469
  30.3 11.6 %collective-permute-start.6 = (f32[40,256]{1,0:T(8,128)S(1)}, f32[40,256]{1,0:T(8,128)S(1)}, u32[]{:S(2)}, u32[]{:S(2)}) collective-permute-start(f32[40,256]{1,0:T(8,128)S(1)} %get-tuple-element.32.vlo), channel_id=1, source_target_pairs={{8,0},{16,8},{24,16},{32,24},{40,32},{48,40},{56,48},{64,56},{72,6... | collective-permute-start | bytes 122888 | tf_op jit(solution)/shard_map/ppermute | solution.py:469
  34.4 0.7 %copy-start = (f32[8]{0:T(128)S(1)}, f32[8]{0:T(128)}, u32[]{:S(2)}) copy-start(f32[8]{0:T(128)} %solid.3) | copy-start | bytes 100

commit v3 on v2

v3 whole, which is shorter than its diff:
```python
import math

import jax
import jax.numpy as jnp
from jax import lax
from jax.experimental import pallas as pl
from jax.experimental.pallas import tpu as pltpu
from jax.sharding import PartitionSpec as P

PHI_SURFACE = (0.45, 0.55, 0.65, 0.4)
ATHY_RATE = (0.25, 0.45, 0.8, 0.35)
MOB_BASE = (1.0, 0.0, -1.5, -0.5)
MOB_SLOPE = (6.0, 5.0, 8.0, 4.0)
GRAIN_DENSITY = (2.65, 2.68, 2.72, 2.71)
WATER_DENSITY = 1.03
SPECTRUM_MID = 1.0
SPECTRUM_HALF = 0.95
SIGMA_RATIO = SPECTRUM_MID / SPECTRUM_HALF
RHO_FIRST = 1.0 / SIGMA_RATIO
RHO_SECOND = 1.0 / (2.0 * SIGMA_RATIO - RHO_FIRST)

H_BASE = tuple(math.log(0.5) - b + 0.35 * s for b, s in zip(MOB_BASE, MOB_SLOPE))
H_SLOPE = tuple(-s for s in MOB_SLOPE)
ABSENT = 1e38

F32 = jnp.float32
L, R, C = 8, 96, 256
GR = 32
VMEM_LIMIT = 40 * 1024 * 1024


def recip(x):
    r = pl.reciprocal(x, approx=True)
    return r * (2.0 - x * r)


def present(h):
    return jnp.where(h == 0.0, ABSENT, h)


def classes(lith):
    return (lith & 1) == 1, lith >= 2


def pick(odd, upper, t):
    return jnp.where(upper, jnp.where(odd, t[3], t[2]), jnp.where(odd, t[1], t[0]))


def iota(shape, dim):
    return lax.broadcasted_iota(jnp.int32, shape, dim)


def roll(x, shift, axis):
    return pltpu.roll(x, shift % x.shape[axis], axis)


def start_kernel(slab, p_in, poro_in, lith_in, solid_in, p, lith, h, over, first, second, shade, poro, solid, sems, solid_sem):
    copies = []
    solid_copy = pltpu.make_async_copy(solid_in, solid, solid_sem)
    solid_copy.start()
    for z in range(L):
        row = []
        for k, (src, dst) in enumerate(((poro_in, poro), (lith_in, lith), (p_in, p))):
            copy = pltpu.make_async_copy(src.at[z], dst.at[z], sems.at[k, z])
            copy.start()
            row.append(copy)
        copies.append(row)
    solid_copy.wait()
    for z in range(L):
        shade[z : z + 1, :] = jnp.full((1, C), solid[z], F32)
    for z in range(L):
        copies[z][0].wait()
        copies[z][1].wait()

        def chunk(i, carry, z=z):
            rows = pl.ds(pl.multiple_of(i * 32, 32), 32)
            at = pl.ds(pl.multiple_of(4 * R + i * 32, 32), 32)
            odd, upper = classes(lith[z, rows, :])
            phi = poro[z, rows, :]
            h[z, rows, :] = jnp.exp(pick(odd, upper, H_BASE) + pick(odd, upper, H_SLOPE) * phi)
            load = (pick(odd, upper, GRAIN_DENSITY) + WATER_DENSITY * phi * recip(1.0 - phi)) * solid[z]
            if z == 0:
                over[z, rows, :] = 0.5 * load
                first[at, :] = load
            else:
                total = first[at, :]
                over[z, rows, :] = total + 0.5 * load
                first[at, :] = total + load
            return carry

        lax.fori_loop(0, R // 32, chunk, 0)
    for z in range(L):
        copies[z][2].wait()
    is_odd = (slab[0] & 1) == 1
    o, i = jnp.where(is_odd, 0, L - 1), jnp.where(is_odd, 1, L - 2)
    first[0:R, :] = h[o]
    first[R : 2 * R, :] = p[o]
    first[2 * R : 3 * R, :] = h[i]
    first[3 * R : 4 * R, :] = p[i]
    o, i = jnp.where(is_odd, L - 1, 0), jnp.where(is_odd, L - 2, 1)
    second[0:R, :] = h[o]
    second[R : 2 * R, :] = p[o]
    second[2 * R : 3 * R, :] = h[i]


def packed(plane, layers, acc_lo, acc_hi):
    lane = iota((GR, 128), 1)
    for g in range(3):
        for z in layers:
            for arr in range(2):
                base = 40 * g + 4 * (z + 1) + 2 * arr
                here = (lane >= base) & (lane < base + 2)
                acc_lo = jnp.where(here, roll(plane(arr, z, g, slice(0, 128)), base, 1), acc_lo)
                acc_hi = jnp.where(here, roll(plane(arr, z, g, slice(C - 128, C)), base + 2, 1), acc_hi)
    return acc_lo, acc_hi


def pack_y_kernel(slab, first, second, own_lo, own_hi, lo, hi):
    is_odd = (slab[0] & 1) == 1

    def plane(arr, z, g, cols):
        at = slice(R * arr + GR * g, R * arr + GR * g + GR)
        a, b = first[at, cols], second[at, cols]
        return jnp.where(is_odd, a, b) if z < 0 else jnp.where(is_odd, b, a)

    lo[...], hi[...] = packed(plane, (-1, L), own_lo[...], own_hi[...])


def pack_x_kernel(slab, h, p, first, second, ylo, yhi, lo, hi):
    is_odd = (slab[0] & 1) == 1
    for ref, o, i, yrow in ((lo, 0, 1, 0), (hi, R - 1, R - 2, GR - 1)):
        for arr, own in ((0, h), (1, p)):
            at = slice(R * arr + o, R * arr + o + 1)
            a, b = first[at, :], second[at, :]
            top = 10 * arr
            ref[top : top + 1, :] = jnp.where(is_odd, a, b)
            for z in range(L):
                ref[top + 1 + z : top + 2 + z, :] = own[z, o : o + 1, :]
                ref[20 + L * arr + z : 21 + L * arr + z, :] = own[z, i : i + 1, :]
            ref[top + 9 : top + 10, :] = jnp.where(is_odd, b, a)
        ref[36:37, 0:128] = ylo[yrow : yrow + 1, :]
        ref[36:37, 128:256] = yhi[yrow : yrow + 1, :]
        ref[37:40, :] = jnp.zeros((3, C), F32)


def sums(h, p, beside):
    total, flow = None, None
    for hn, pn in beside:
        t = recip(h + hn)
        total = 1.0 + t if total is None else total + t
        flow = t * (pn - p) if flow is None else flow + t * (pn - p)
    return total, flow


def beside_y(msgs, owns):
    lane = iota((GR, 128), 1)
    sub = iota((GR, 128), 0)
    result = []
    for msg, own, o, i, w in ((msgs[0], owns[0], 1, 0, 0), (msgs[1], owns[1], 0, 1, 1)):
        m, v = msg[...], own[...]
        ho, po = present(roll(m, -o, 1)), roll(m, -o - 2, 1)
        hi_, pi_ = present(roll(m, -i, 1)), roll(m, -i - 2, 1)
        hw, pw = present(roll(v, -w, 1)), roll(v, -w - 2, 1)

        def along_x(f):
            u = roll(f, 1, 0)
            u = jnp.where(sub == 0, roll(u, 40, 1), u)
            d = roll(f, -1, 0)
            d = jnp.where(sub == GR - 1, roll(d, -40, 1), d)
            return u, d

        hu, hd = along_x(ho)
        pu, pd = along_x(po)
        hu = jnp.where((sub == 0) & (lane < 40), ABSENT, hu)
        hd = jnp.where((sub == GR - 1) & (lane >= 80), ABSENT, hd)
        total, flow = sums(ho, po, (
            (hi_, pi_), (hw, pw), (hu, pu), (hd, pd),
            (roll(ho, 4, 1), roll(po, 4, 1)), (roll(ho, -4, 1), roll(po, -4, 1)),
        ))
        result.append((ho, po, total, flow))
    return result


def beside_y_corners(msgs, yst):
    lane = iota((GR, 128), 1)
    sub = iota((GR, 128), 0)
    at_low = (sub == 0) & (lane < 40)
    at_high = (sub == GR - 1) & (lane >= 80)
    result = []
    for s, o, cols in ((0, 1, slice(0, 128)), (1, 0, slice(128, 256))):
        ho, po, total, flow = (yst[s, k] for k in range(4))

        def corner(k):
            low = jnp.broadcast_to(msgs[0][36:37, cols], (GR, 128))
            high = jnp.broadcast_to(msgs[1][36:37, cols], (GR, 128))
            return jnp.where(sub == 0, roll(low, -80 - k, 1), roll(high, 80 - k, 1))

        t = jnp.where(at_low | at_high, recip(ho + present(corner(o))), 0.0)
        result.append(po + (flow + t * (corner(o + 2) - po)) * recip(total + t))
    return result


def beside_x(msgs, owns, xh, xp, xq):
    lane = iota((16, C), 1)
    lane_x = iota((16, 128), 1)
    sub_x = iota((16, 128), 0)
    for s, row_lane in ((0, 80), (1, 0)):
        msg, own = msgs[s], owns[s]

        def rows10(ref, at):
            return jnp.concatenate([ref[at : at + 10, :], jnp.zeros((6, C), F32)], axis=0)

        def rows8(ref, at):
            return jnp.concatenate([jnp.zeros((1, C), F32), ref[at : at + 8, :], jnp.zeros((7, C), F32)], axis=0)

        ho, po = present(rows10(msg, 0)), rows10(msg, 10)
        hi_, pi_ = present(rows8(msg, 20)), rows8(msg, 28)
        hw, pw = present(rows10(own, 0)), rows10(own, 10)

        def corner(cols, k):
            row = jnp.broadcast_to(msg[36:37, cols], (16, 128))
            return jnp.sum(jnp.where(lane_x == row_lane + 4 * sub_x + k, row, 0.0), axis=1, keepdims=True)

        left, right = slice(0, 128), slice(128, 256)
        hl = jnp.where(lane == 0, present(corner(left, 1)), roll(ho, 1, 1))
        pl_ = jnp.where(lane == 0, corner(left, 3), roll(po, 1, 1))
        hr = jnp.where(lane == C - 1, present(corner(right, 0)), roll(ho, -1, 1))
        pr = jnp.where(lane == C - 1, corner(right, 2), roll(po, -1, 1))
        xh[s] = ho
        xp[s] = po
        total, flow = sums(ho, po, (
            (hi_, pi_), (hw, pw), (hl, pl_), (hr, pr),
            (roll(ho, 1, 0), roll(po, 1, 0)), (roll(ho, -1, 0), roll(po, -1, 0)),
        ))
        xq[s] = po + flow * recip(total)


def edge_columns(lo, hi, z, g):
    lane = iota((GR, 128), 1)
    at = 40 * g + 4 * (z + 1)
    return jnp.where(lane == 0, roll(lo, -at, 1), roll(hi, 127 - at, 1))


def around_x(before, here, after):
    sub = iota((8, C), 0)
    return roll(jnp.where(sub == 7, before, here), 1, 0), roll(jnp.where(sub == 0, after, here), -1, 0)


def around_y(here, edge):
    lane = iota((8, 128), 1)
    a, b = here[:, :128], here[:, 128:]
    ra, rb = roll(a, 1, 1), roll(b, 1, 1)
    left = jnp.concatenate([jnp.where(lane == 0, edge, ra), jnp.where(lane == 0, ra, rb)], axis=1)
    ra, rb = roll(a, -1, 1), roll(b, -1, 1)
    right = jnp.concatenate([jnp.where(lane == 127, rb, ra), jnp.where(lane == 127, edge, rb)], axis=1)
    return left, right


def second_chunk(qval, qedge, weight, pval, base, over, lith, shade, put):
    low = qval(-1)[1]
    qc = qval(0)
    flow = weight(0, 4) * (qc[1] - low)
    for z in range(L):
        qn = qval(z + 1)
        flow2 = weight(z + 1, 4) * (qn[1] - qc[1])
        q = qc[1]
        change = flow2 - flow
        for k, qb in enumerate(around_x(*qc) + around_y(q, qedge(z))):
            change = change + weight(z, k) * (qb - q)
        d0 = q - pval(z)
        pn = q + RHO_SECOND * RHO_FIRST * d0 + (2.0 * RHO_SECOND / SPECTRUM_HALF) * (change - d0) * weight(z, 5)
        stress = jnp.maximum(base + over(z) - pn, 0.0)
        odd, upper = classes(lith(z))
        new = pick(odd, upper, PHI_SURFACE) * jnp.exp(-pick(odd, upper, ATHY_RATE) * stress)
        put(z, pn, new, jnp.broadcast_to(shade[z : z + 1, :], (8, C)) * recip(1.0 - new))
        qc, flow = qn, flow2


def above_rows(slab, first, third, rows):
    base = jnp.where((slab[0] & 1) == 1, first[rows(4 * R), :], 0.0)
    return base + jnp.where(slab[0] >= 2, third[rows(R), :], 0.0)


def at8(i):
    return pl.ds(pl.multiple_of(8 * i, 8), 8)


LAST = R // 8 - 1


def triples(h, p, hz, pz, i):
    here = (at8(jnp.maximum(i - 1, 0)), at8(i), at8(jnp.minimum(i + 1, LAST)))

    def at(z):
        return (h, p, z) if 0 <= z < L else (hz, pz, {-1: 0, L: 1, -2: 2, L + 1: 3}[z])

    def hval(z):
        ref, _, k = at(z)
        a, b, c = (ref[k, rows, :] for rows in here)
        return jnp.where(i == 0, ABSENT, a), b, jnp.where(i == LAST, ABSENT, c)

    def pval(z):
        _, ref, k = at(z)
        return tuple(ref[k, rows, :] for rows in here)

    return hval, pval


def pack_own_kernel(slab, h, p, mine, first, third, lo, hi):
    zero = jnp.zeros((GR, 128), F32)
    lo[...], hi[...] = packed(
        lambda arr, z, g, cols: (h, p)[arr][z, GR * g : GR * g + GR, cols], range(L), zero, zero
    )
    i = jnp.where((slab[0] & 1) == 1, L - 2, 1)
    third[0:R, :] = p[i]
    third[R : 2 * R, :] = mine[4 * R : 5 * R, :] + first[4 * R : 5 * R, :]


def pre_kernel(slab, h, p, first, second, w, hz, pz):
    is_odd = (slab[0] & 1) == 1
    for ref, at, fix in ((hz, 0, present), (pz, R, lambda t: t)):
        a, b = first[at : at + R, :], second[at : at + R, :]
        ref[0] = fix(jnp.where(is_odd, a, b))
        ref[1] = fix(jnp.where(is_odd, b, a))

    def chunk(i, carry):
        rows = at8(i)
        hval, pval = triples(h, p, hz, pz, i)
        hc, pc = hval(0), pval(0)
        t = recip(hc[1] + hz[0, rows, :])
        flow = t * (pc[1] - pz[0, rows, :])
        w[2, 0, rows, :] = t
        for z in range(L):
            hn, pn = hval(z + 1), pval(z + 1)
            t2 = recip(hc[1] + hn[1])
            flow2 = t2 * (pn[1] - pc[1])
            w[2, z + 1, rows, :] = t2
            total, change = (1.0 + t) + t2, flow2 - flow
            for k, (hb, pb) in enumerate(zip(around_x(*hc), around_x(*pc))):
                u = recip(hc[1] + hb)
                w[k, z, rows, :] = u
                total = total + u
                change = change + u * (pb - pc[1])
            w[3, z, rows, :] = total
            w[4, z, rows, :] = change
            hc, pc, t, flow = hn, pn, t2, flow2
        return carry

    lax.fori_loop(0, R // 8, chunk, 0)


def inner_kernel(
    slab, shade, h, p, over, lith, first, second, third, w, hz1, pz1, ylo, yhi, wlo, whi,
    yst, wy, p1, dd, rr, out0, out1, out2,
    hz, pz, eh, ep, eq, o0, o1, o2, sems,
):
    is_odd = (slab[0] & 1) == 1
    for k in range(2):
        hz[k] = hz1[k]
        pz[k] = pz1[k]
    for ref, a, b, fix in (
        (hz, first[2 * R : 3 * R, :], second[2 * R : 3 * R, :], present),
        (pz, first[3 * R : 4 * R, :], third[0:R, :], lambda t: t),
    ):
        ref[2] = fix(jnp.where(is_odd, a, b))
        ref[3] = fix(jnp.where(is_odd, b, a))
    lo, hi = beside_y((ylo, yhi), (wlo, whi))
    for s, values in enumerate((lo, hi)):
        for k in range(4):
            yst[s, k] = values[k]
    qlo, qhi = (v[1] + v[3] * recip(v[2]) for v in (lo, hi))
    for z in range(-1, L + 1):
        for g in range(3):
            rows = slice(GR * g, GR * g + GR)
            eh[z + 1, rows, :] = edge_columns(lo[0], hi[0], z, g)
            ep[z + 1, rows, :] = edge_columns(lo[1], hi[1], z, g)
            if 0 <= z < L:
                eq[z, rows, :] = edge_columns(qlo, qhi, z, g)

    def chunk1(i, carry):
        rows = at8(i)
        hval, pval = triples(h, p, hz, pz, i)

        def finish(z, hc, pc, total, change):
            for k, (hb, pb) in enumerate(zip(around_y(hc, eh[z + 1, rows, :]), around_y(pc, ep[z + 1, rows, :]))):
                u = recip(hc + hb)
                if 0 <= z < L:
                    wy[k, z, rows, :] = u
                total = total + u
                change = change + u * (pb - pc)
            inv = recip(total)
            if 0 <= z < L:
                wy[2, z, rows, :] = inv
            p1[z + 1, rows, :] = pc + change * inv
            at = pl.ds(pl.multiple_of(jnp.where(i == LAST, 8, jnp.where(i == 0, 0, 16)), 8), 8)
            dd[z + 1, at, :] = total
            rr[z + 1, at, :] = change

        for z, out, own in ((-1, -2, 0), (L, L + 1, L - 1)):
            hc, pc = hval(z), pval(z)
            beside = [(hval(out)[1], pval(out)[1]), (hval(own)[1], pval(own)[1])]
            beside += list(zip(around_x(*hc), around_x(*pc)))
            finish(z, hc[1], pc[1], *sums(hc[1], pc[1], beside))
        for z in range(L):
            finish(z, h[z, rows, :], p[z, rows, :], w[3, z, rows, :], w[4, z, rows, :])
        return carry

    lax.fori_loop(0, R // 8, chunk1, 0)

    def moved(i):
        return [
            pltpu.make_async_copy(src.at[:, at8(i), :], dst.at[:, at8(i), :], sems.at[k, i])
            for k, (src, dst) in enumerate(((o0, out0), (o1, out1), (o2, out2)))
        ]

    def chunk2(i, carry):
        rows = at8(i)
        here = (at8(i - 1), rows, at8(i + 1))

        def put(z, a, b, c):
            o0[z, rows, :] = a
            o1[z, rows, :] = b
            o2[z, rows, :] = c

        second_chunk(
            lambda z: tuple(p1[z + 1, r, :] for r in here),
            lambda z: eq[z, rows, :],
            lambda z, k: (w, w, wy, wy, w, wy)[k][(0, 1, 0, 1, 2, 2)[k], z, rows, :],
            lambda z: p[z, rows, :],
            above_rows(slab, first, third, lambda top: pl.ds(pl.multiple_of(top + 8 * i, 8), 8)),
            lambda z: over[z, rows, :],
            lambda z: lith[z, rows, :],
            shade, put,
        )
        for copy in moved(i):
            copy.start()
        return carry

    lax.fori_loop(1, LAST, chunk2, 0)

    def arrive(i, carry):
        for copy in moved(i):
            copy.wait()
        return carry

    lax.fori_loop(1, LAST, arrive, 0)


def outer_kernel(
    slab, shade, h, p, over, lith, first, third, xlo, xhi, vlo, vhi,
    hz, pz, w, yst, wy, p1, dd, rr, in0, in1, in2,
    out0, out1, out2,
    xh, xp, xq, q1, wt, o0, o1, o2, sems,
):
    beside_x((xlo, xhi), (vlo, vhi), xh, xp, xq)
    lo, hi = beside_y_corners((xlo, xhi), yst)
    sub = iota((8, C), 0)
    copies = []
    for s, top, g, part in ((0, 0, 0, slice(0, 8)), (1, R - 8, 2, slice(GR - 8, GR))):
        rows = slice(top, top + 8)
        near = slice(8, 16) if s == 0 else slice(R - 16, R - 8)
        edge = sub == (0 if s == 0 else 7)

        def strip(ref, z, s=s):
            return jnp.broadcast_to(ref[s, z + 1 : z + 2, :], (8, C))

        for z in range(-1, L + 1):
            if 0 <= z < L:
                hc, pc = h[z, rows, :], p[z, rows, :]
            else:
                k = 0 if z < 0 else 1
                hc, pc = hz[k, rows, :], pz[k, rows, :]
            total, change = dd[z + 1, 8 * s : 8 * s + 8, :], rr[z + 1, 8 * s : 8 * s + 8, :]
            t = jnp.where(edge, recip(hc + strip(xh, z)), 0.0)
            inv = recip(total + t)
            q1[s, z + 1] = pc + (change + t * (strip(xp, z) - pc)) * inv
            if 0 <= z < L:
                wt[s, 0, z] = w[s, z, rows, :] + t
                wt[s, 1, z] = inv

        def q_triple(z, s=s, near=near):
            here = q1[s, z + 1]
            if z < 0 or z >= L:
                return here, here, here
            inside = p1[z + 1, near, :]
            return (strip(xq, z), here, inside) if s == 0 else (inside, here, strip(xq, z))

        def weight(z, k, s=s, rows=rows):
            if k == s:
                return wt[s, 0, z]
            if k == 5:
                return wt[s, 1, z]
            return (w, w, wy, wy, w)[k][(0, 1, 0, 1, 2)[k], z, rows, :]

        def put(z, a, b, c, s=s):
            o0[s, z] = a
            o1[s, z] = b
            o2[s, z] = c

        second_chunk(
            q_triple,
            lambda z: edge_columns(lo, hi, z, g)[part],
            weight,
            lambda z: p[z, rows, :],
            above_rows(slab, first, third, lambda t: slice(t + top, t + top + 8)),
            lambda z: over[z, rows, :],
            lambda z: lith[z, rows, :],
            shade, put,
        )
        for k, (src, dst) in enumerate(((o0, out0), (o1, out1), (o2, out2))):
            copy = pltpu.make_async_copy(src.at[s], dst.at[:, rows, :], sems.at[s, k])
            copy.start()
            copies.append(copy)
    for copy in copies:
        copy.wait()


SMEM, VMEM, HBM = pltpu.SMEM, pltpu.VMEM, pltpu.HBM


def call(kernel, name, ins, outs, scratch=(), aliases=None):
    return pl.pallas_call(
        kernel,
        out_shape=[jax.ShapeDtypeStruct(s, t) for s, t, _ in outs],
        in_specs=[pl.BlockSpec(memory_space=m) for m in ins],
        out_specs=[pl.BlockSpec(memory_space=m) for _, _, m in outs],
        scratch_shapes=list(scratch),
        input_output_aliases=aliases or {},
        compiler_params=pltpu.CompilerParams(vmem_limit_bytes=VMEM_LIMIT),
        name=name,
    )


def pair(axis, lo, hi):
    n = lax.axis_size(axis)
    up = [(i, i + 1) for i in range(n - 1)]
    down = [(j, i) for i, j in up]
    return lax.ppermute(hi, axis, up), lax.ppermute(lo, axis, down)


def vm(*shape):
    return (shape, F32, VMEM)


def body(p_in, poro, lith_in, solid):
    p_in, poro, lith_in, solid = (
        pltpu.with_memory_space_constraint(a, HBM) for a in (p_in, poro, lith_in, solid)
    )
    slab = lax.axis_index("slab").astype(jnp.int32).reshape(1)
    block = (L, R, C)
    dma = pltpu.SemaphoreType.DMA
    p, lith, h, over, first, second, shade = call(
        start_kernel, "start", [SMEM] + [HBM] * 4,
        [vm(*block), (block, jnp.int32, VMEM), vm(*block), vm(*block), vm(5 * R, C), vm(3 * R, C), vm(L, C)],
        [VMEM(block, F32), SMEM((L,), F32), dma((3, L)), dma(())],
    )(slab, p_in, poro, lith_in, solid)
    second_in = lax.ppermute(second, "slab", [(1, 2), (2, 1)])
    first_in = lax.ppermute(first, "slab", [(0, 1), (1, 0), (2, 3), (3, 2)])
    third, *own_y = call(
        pack_own_kernel, "pack_own", [SMEM] + [VMEM] * 4, [vm(2 * R, C), vm(GR, 128), vm(GR, 128)]
    )(slab, h, p, first, first_in)
    third_in = lax.ppermute(third, "slab", [(1, 2), (2, 1), (0, 3)])
    wlo, whi = call(pack_y_kernel, "pack_y", [SMEM] + [VMEM] * 4, [vm(GR, 128)] * 2)(
        slab, first_in, second_in, *own_y
    )
    ylo, yhi = pair("mapy", wlo, whi)
    h2, wlo2 = lax.optimization_barrier((h, wlo))
    w, hz, pz = call(
        pre_kernel, "pre", [SMEM] + [VMEM] * 4, [vm(5, L + 1, R, C), vm(2, R, C), vm(2, R, C)]
    )(slab, h2, p, first_in, second_in)
    ylo, yhi, hz = lax.optimization_barrier((ylo, yhi, hz))
    vlo, vhi = call(pack_x_kernel, "pack_x", [SMEM] + [VMEM] * 6, [vm(40, C)] * 2)(
        slab, h, p, first_in, second_in, ylo, yhi
    )
    xlo, xhi = pair("mapx", vlo, vhi)
    hbm = (block, F32, HBM)
    plane = VMEM((4, R, C), F32)
    edges = VMEM((L + 2, R, 128), F32)
    yst, wy, p1, dd, rr, *outs = call(
        inner_kernel, "inner", [SMEM] + [VMEM] * 15,
        [vm(2, 4, GR, 128), vm(3, L, R, C), vm(L + 2, R, C)] + [vm(L + 2, 24, C)] * 2 + [hbm] * 3,
        [plane, plane, edges, edges, VMEM((L, R, 128), F32)] + [VMEM(block, F32)] * 3 + [dma((3, R // 8))],
    )(slab, shade, h, p, over, lith, first_in, second_in, third_in, w, hz, pz, ylo, yhi, wlo, whi)
    return tuple(
        call(
            outer_kernel, "outer", [SMEM] + [VMEM] * 19 + [HBM] * 3, [hbm] * 3,
            [VMEM((2, 16, C), F32)] * 3
            + [VMEM((2, L + 2, 8, C), F32), VMEM((2, 2, L, 8, C), F32)]
            + [VMEM((2, L, 8, C), F32)] * 3 + [dma((2, 3))],
            {20: 0, 21: 1, 22: 2},
        )(
            slab, shade, h, p, over, lith, first_in, third_in, xlo, xhi, vlo, vhi,
            hz, pz, w, yst, wy, p1, dd, rr, *outs,
        )
    )


def solution(mesh):
    spec = P("slab", "mapx", "mapy")
    return jax.shard_map(
        body, mesh=mesh, in_specs=(spec, spec, spec, P("slab")), out_specs=(spec,) * 3, check_vma=False
    )
```

time: 44.4 us -> 40 us (0.901)
  the two profiles are of different devices: /device:TPU:262 before, /device:TPU:270 now
where the time goes in v3:
time: 40 us; the launch traced here: 39.7 us
  starting transfers between devices  21.9 us (55%)
  Pallas kernels  10.8 us (27%)
  waiting for transfers between devices  6.23 us (16%)
  between operations  0.77 us (2%)
    ppermute x4, starting transfers between devices, pair(): return (lax.ppermute(hi, axis, up), lax.ppermute(lo, axis, down))  14.4 us
    pallas_call x1, Pallas kernels, body(): call(inner_kernel, 'inner', [SMEM] + [VMEM] * 15, [vm(2, 4, GR, 128), vm(...  5.48 us
    ppermute x4, waiting for transfers between devices, pair(): return (lax.ppermute(hi, axis, up), lax.ppermute(lo, axis, down))  3.82 us
    ppermute x1, starting transfers between devices, body(): second_in = lax.ppermute(second, 'slab', [(1, 2), (2, 1)])  2.84 us
    ppermute x1, starting transfers between devices, body(): third_in = lax.ppermute(third, 'slab', [(1, 2), (2, 1), (0, 3)])  2.72 us
    ppermute x1, waiting for transfers between devices, body(): second_in = lax.ppermute(second, 'slab', [(1, 2), (2, 1)])  2.4 us
    pallas_call x1, Pallas kernels, body(): call(start_kernel, 'start', [SMEM] + [HBM] * 4, [vm(*block), (block, jnp....  2.18 us
    ppermute x1, starting transfers between devices, body(): first_in = lax.ppermute(first, 'slab', [(0, 1), (1, 0), (2, 3), (3, 2)])  1.92 us
  transfers between devices with their start and end apart: 7, of which 2 were waited for; matrix products, arithmetic and copies ran while one was open for 0% of the time, Pallas kernels for 19%

profile of v3, /device:TPU:270, one launch (start us, length us, event | category | flops | bytes accessed | tf_op | source)
XLA Modules:
  0.0 39.7 jit_solution(2502963205934348315)
XLA Ops:
  0.6 2.2 %start.1 = (f32[8,96,256]{2,1,0:T(8,128)S(1)}, s32[8,96,256]{2,1,0:T(8,128)S(1)}, f32[8,96,256]{2,1,0:T(8,128)S(1)}, f32[8,96,256]{2,1,0:T(8,128)S(1)}, f32[480,...) custom-call(s32[1]{0:T(128)} %bitcast.slab, f32[8,96,256]{2,1,0:T(8,128)} %p_in.1, ...), custom_call_target="tpu_custom_call" | custom-call | tf_op jit(solution)/shard_map/start/pallas_call | solution.py:552
  2.8 1.9 %collective-permute-start = (f32[480,256]{1,0:T(8,128)S(1)}, f32[480,256]{1,0:T(8,128)S(1)}, u32[]{:S(2)}, u32[]{:S(2)}) collective-permute-start(f32[480,256]{1,0:T(8,128)S(1)} %get-tuple-element.37.mine), channel_id=1, source_target_pairs={{0,128},{128,0},{256,384},{384,256},{1,129},{129,1},{257,385},{385... | collective-permute-start | bytes 1474568 | tf_op jit(solution)/shard_map/ppermute | solution.py:558
  4.8 2.8 %collective-permute-start.2 = (f32[288,256]{1,0:T(8,128)S(1)}, f32[288,256]{1,0:T(8,128)S(1)}, u32[]{:S(2)}, u32[]{:S(2)}) collective-permute-start(f32[288,256]{1,0:T(8,128)S(1)} %get-tuple-element.39), channel_id=1, source_target_pairs={{128,256},{256,128},{129,257},{257,129},{130,258},{258,130},{131,2... | collective-permute-start | bytes 884744 | tf_op jit(solution)/shard_map/ppermute | solution.py:557
  7.6 0.0 collective-permute-done.first
  7.6 0.5 %pack_own.1 = (f32[192,256]{1,0:T(8,128)S(1)}, f32[32,128]{1,0:T(8,128)S(1)}, f32[32,128]{1,0:T(8,128)S(1)}) custom-call(s32[1]{0:T(128)} %bitcast.slab, f32[8,96,256]{2,1,0:T(8,128)S(1)} %get-tuple-element.44.h, f32[8,96,256]{2,1,0:T(8,128)S(1)} %get-tuple-element.34.p, f32[480,256]{1,0:T(8,128)S(1)} %get-tuple-element.37.mine, ...), custom_call_target="tpu_custom_call" | custom-call | tf_op jit(solution)/shard_map/pack_own/pallas_call | solution.py:559
  8.1 2.7 %collective-permute-start.1 = (f32[192,256]{1,0:T(8,128)S(1)}, f32[192,256]{1,0:T(8,128)S(1)}, u32[]{:S(2)}, u32[]{:S(2)}) collective-permute-start(f32[192,256]{1,0:T(8,128)S(1)} %get-tuple-element.38), channel_id=1, source_target_pairs={{128,256},{256,128},{0,384},{129,257},{257,129},{1,385},{130,258},... | collective-permute-start | bytes 589832 | tf_op jit(solution)/shard_map/ppermute | solution.py:562
  10.8 2.4 %collective-permute-done.2.second = f32[288,256]{1,0:T(8,128)S(1)} collective-permute-done((f32[288,256]{1,0:T(8,128)S(1)}, f32[288,256]{1,0:T(8,128)S(1)}, u32[]{:S(2)}, u32[]{:S(2)}) %collective-permute-start.2) | collective-permute-done | bytes 294944 | tf_op jit(solution)/shard_map/ppermute | solution.py:557
  13.2 0.2 pack_y.1
  13.4 4.3 %collective-permute-start.3 = (f32[32,128]{1,0:T(8,128)S(1)}, f32[32,128]{1,0:T(8,128)S(1)}, u32[]{:S(2)}, u32[]{:S(2)}) collective-permute-start(f32[32,128]{1,0:T(8,128)S(1)} %get-tuple-element.42.whi), channel_id=1, source_target_pairs={{0,1},{1,2},{2,3},{3,4},{4,5},{5,6},{6,7},{8,9},{9,10},{10,11},{11... | collective-permute-start | bytes 49160 | tf_op jit(solution)/shard_map/ppermute | solution.py:538
  17.8 3.0 %collective-permute-start.4 = (f32[32,128]{1,0:T(8,128)S(1)}, f32[32,128]{1,0:T(8,128)S(1)}, u32[]{:S(2)}, u32[]{:S(2)}) collective-permute-start(f32[32,128]{1,0:T(8,128)S(1)} %get-tuple-element.43.wlo), channel_id=1, source_target_pairs={{1,0},{2,1},{3,2},{4,3},{5,4},{6,5},{7,6},{9,8},{10,9},{11,10},{12... | collective-permute-start | bytes 49160 | tf_op jit(solution)/shard_map/ppermute | solution.py:538
  20.8 1.2 %pre.1 = (f32[5,9,96,256]{3,2,1,0:T(8,128)S(1)}, f32[2,96,256]{2,1,0:T(8,128)S(1)}, f32[2,96,256]{2,1,0:T(8,128)S(1)}) custom-call(s32[1]{0:T(128)} %bitcast.slab, f32[8,96,256]{2,1,0:T(8,128)S(1)} %get-tuple-element.44.h, f32[8,96,256]{2,1,0:T(8,128)S(1)} %get-tuple-element.34.p, f32[480,256]{1,0:T(8,128)S(1)} %collective-permute-done.first, ...), custom_call_target="tpu_custom_call" | custom-call | tf_op jit(solution)/shard_map/pre/pallas_call | solution.py:568
  22.0 0.0 collective-permute-done.3.ylo
  22.0 3.8 %collective-permute-done.4.yhi = f32[32,128]{1,0:T(8,128)S(1)} collective-permute-done((f32[32,128]{1,0:T(8,128)S(1)}, f32[32,128]{1,0:T(8,128)S(1)}, u32[]{:S(2)}, u32[]{:S(2)}) %collective-permute-start.4) | collective-permute-done | bytes 16416 | tf_op jit(solution)/shard_map/ppermute | solution.py:538
  25.8 2.9 %collective-permute-start.5 = (f32[40,256]{1,0:T(8,128)S(1)}, f32[40,256]{1,0:T(8,128)S(1)}, u32[]{:S(2)}, u32[]{:S(2)}) collective-permute-start(f32[40,256]{1,0:T(8,128)S(1)} %get-tuple-element.48.vhi), channel_id=1, source_target_pairs={{0,8},{8,16},{16,24},{24,32},{32,40},{40,48},{48,56},{56,64},{64,7... | collective-permute-start | bytes 122888 | tf_op jit(solution)/shard_map/ppermute | solution.py:538
  28.8 4.1 %collective-permute-start.6 = (f32[40,256]{1,0:T(8,128)S(1)}, f32[40,256]{1,0:T(8,128)S(1)}, u32[]{:S(2)}, u32[]{:S(2)}) collective-permute-start(f32[40,256]{1,0:T(8,128)S(1)} %get-tuple-element.49.vlo), channel_id=1, source_target_pairs={{8,0},{16,8},{24,16},{32,24},{40,32},{48,40},{56,48},{64,56},{72,6... | collective-permute-start | bytes 122888 | tf_op jit(solution)/shard_map/ppermute | solution.py:538
  32.9 0.0 collective-permute-done.1.third
  32.9 5.5 %inner.1 = (f32[2,4,32,128]{3,2,1,0:T(8,128)S(1)}, f32[3,8,96,256]{3,2,1,0:T(8,128)S(1)}, f32[10,96,256]{2,1,0:T(8,128)S(1)}, f32[10,24,256]{2,1,0:T(8,128)S(1)}...) custom-call(s32[1]{0:T(128)} %bitcast.slab, ...), custom_call_target="tpu_custom_call" | custom-call | tf_op jit(solution)/shard_map/inner/pallas_call | solution.py:579
  38.4 0.0 collective-permute-done.5.xlo
  38.4 0.0 collective-permute-done.6.xhi
  38.4 1.3 %outer.1 = (f32[8,96,256]{2,1,0:T(8,128)}, f32[8,96,256]{2,1,0:T(8,128)}, f32[8,96,256]{2,1,0:T(8,128)}) custom-call(s32[1]{0:T(128)} %bitcast.slab, f32[8,256]{1,0:T(8,128)S(1)} %get-tuple-element.32.shade, f32[8,96,256]{2,1,0:T(8,128)S(1)} %get-tuple-element.44.h, ...), custom_call_target="tpu_custom_call", output_to_operand_aliasing={{0}: (20, {}), {1}: (21, {}), {2}: (22, {})} | custom-call | tf_op jit(solution)/shard_map/outer/pallas_call | solution.py:585
  (1 shorter events, 0.0 us)
Async XLA Ops:
  2.8 4.8 %collective-permute-start = (f32[480,256]{1,0:T(8,128)S(1)}, f32[480,256]{1,0:T(8,128)S(1)}, u32[]{:S(2)}, u32[]{:S(2)}) collective-permute-start(f32[480,256]{1,0:T(8,128)S(1)} %get-tuple-element.37.mine), channel_id=1, source_target_pairs={{0,128},{128,0},{256,384},{384,256},{1,129},{129,1},{257,385},{385... | collective-permute-start | bytes 1474568 | tf_op jit(solution)/shard_map/ppermute | solution.py:558
  4.8 8.5 %collective-permute-start.2 = (f32[288,256]{1,0:T(8,128)S(1)}, f32[288,256]{1,0:T(8,128)S(1)}, u32[]{:S(2)}, u32[]{:S(2)}) collective-permute-start(f32[288,256]{1,0:T(8,128)S(1)} %get-tuple-element.39), channel_id=1, source_target_pairs={{128,256},{256,128},{129,257},{257,129},{130,258},{258,130},{131,2... | collective-permute-start | bytes 884744 | tf_op jit(solution)/shard_map/ppermute | solution.py:557
  8.1 24.8 %collective-permute-start.1 = (f32[192,256]{1,0:T(8,128)S(1)}, f32[192,256]{1,0:T(8,128)S(1)}, u32[]{:S(2)}, u32[]{:S(2)}) collective-permute-start(f32[192,256]{1,0:T(8,128)S(1)} %get-tuple-element.38), channel_id=1, source_target_pairs={{128,256},{256,128},{0,384},{129,257},{257,129},{1,385},{130,258},... | collective-permute-start | bytes 589832 | tf_op jit(solution)/shard_map/ppermute | solution.py:562
  13.4 8.5 %collective-permute-start.3 = (f32[32,128]{1,0:T(8,128)S(1)}, f32[32,128]{1,0:T(8,128)S(1)}, u32[]{:S(2)}, u32[]{:S(2)}) collective-permute-start(f32[32,128]{1,0:T(8,128)S(1)} %get-tuple-element.42.whi), channel_id=1, source_target_pairs={{0,1},{1,2},{2,3},{3,4},{4,5},{5,6},{6,7},{8,9},{9,10},{10,11},{11... | collective-permute-start | bytes 49160 | tf_op jit(solution)/shard_map/ppermute | solution.py:538
  17.8 8.0 %collective-permute-start.4 = (f32[32,128]{1,0:T(8,128)S(1)}, f32[32,128]{1,0:T(8,128)S(1)}, u32[]{:S(2)}, u32[]{:S(2)}) collective-permute-start(f32[32,128]{1,0:T(8,128)S(1)} %get-tuple-element.43.wlo), channel_id=1, source_target_pairs={{1,0},{2,1},{3,2},{4,3},{5,4},{6,5},{7,6},{9,8},{10,9},{11,10},{12... | collective-permute-start | bytes 49160 | tf_op jit(solution)/shard_map/ppermute | solution.py:538
  25.8 12.6 %collective-permute-start.5 = (f32[40,256]{1,0:T(8,128)S(1)}, f32[40,256]{1,0:T(8,128)S(1)}, u32[]{:S(2)}, u32[]{:S(2)}) collective-permute-start(f32[40,256]{1,0:T(8,128)S(1)} %get-tuple-element.48.vhi), channel_id=1, source_target_pairs={{0,8},{8,16},{16,24},{24,32},{32,40},{40,48},{48,56},{56,64},{64,7... | collective-permute-start | bytes 122888 | tf_op jit(solution)/shard_map/ppermute | solution.py:538
  28.8 9.6 %collective-permute-start.6 = (f32[40,256]{1,0:T(8,128)S(1)}, f32[40,256]{1,0:T(8,128)S(1)}, u32[]{:S(2)}, u32[]{:S(2)}) collective-permute-start(f32[40,256]{1,0:T(8,128)S(1)} %get-tuple-element.49.vlo), channel_id=1, source_target_pairs={{8,0},{16,8},{24,16},{32,24},{40,32},{48,40},{56,48},{64,56},{72,6... | collective-permute-start | bytes 122888 | tf_op jit(solution)/shard_map/ppermute | solution.py:538

commit v4 on v3

--- a/solution.py
+++ b/solution.py
@@ -26,6 +26,7 @@
 F32 = jnp.float32
 L, R, C = 8, 96, 256
 GR = 32
+STEPS = 3
 VMEM_LIMIT = 40 * 1024 * 1024
 
 
@@ -54,43 +55,60 @@
     return pltpu.roll(x, shift % x.shape[axis], axis)
 
 
+class Later:
+    def __init__(self, every):
+        self.every, self.count, self.kept = every, 0, []
+
+    def put(self, *stores):
+        self.kept.extend(stores)
+        self.count += 1
+        if self.count % self.every == 0:
+            self.flush()
+
+    def flush(self):
+        for ref, at, value in self.kept:
+            ref[at] = value
+        self.kept = []
+
+
 def start_kernel(slab, p_in, poro_in, lith_in, solid_in, p, lith, h, over, first, second, shade, poro, solid, sems, solid_sem):
+    step = R // STEPS
     copies = []
     solid_copy = pltpu.make_async_copy(solid_in, solid, solid_sem)
     solid_copy.start()
-    for z in range(L):
-        row = []
-        for k, (src, dst) in enumerate(((poro_in, poro), (lith_in, lith), (p_in, p))):
-            copy = pltpu.make_async_copy(src.at[z], dst.at[z], sems.at[k, z])
+    for k in range(STEPS):
+        rows = slice(k * step, (k + 1) * step)
+        group = [
+            pltpu.make_async_copy(src.at[:, rows, :], dst.at[:, rows, :], sems.at[j, k])
+            for j, (src, dst) in enumerate(((poro_in, poro), (lith_in, lith), (p_in, p)))
+        ]
+        for copy in group:
             copy.start()
-            row.append(copy)
-        copies.append(row)
+        copies.append(group)
     solid_copy.wait()
     for z in range(L):
         shade[z : z + 1, :] = jnp.full((1, C), solid[z], F32)
-    for z in range(L):
-        copies[z][0].wait()
-        copies[z][1].wait()
-
-        def chunk(i, carry, z=z):
-            rows = pl.ds(pl.multiple_of(i * 32, 32), 32)
-            at = pl.ds(pl.multiple_of(4 * R + i * 32, 32), 32)
-            odd, upper = classes(lith[z, rows, :])
-            phi = poro[z, rows, :]
-            h[z, rows, :] = jnp.exp(pick(odd, upper, H_BASE) + pick(odd, upper, H_SLOPE) * phi)
-            load = (pick(odd, upper, GRAIN_DENSITY) + WATER_DENSITY * phi * recip(1.0 - phi)) * solid[z]
-            if z == 0:
-                over[z, rows, :] = 0.5 * load
-                first[at, :] = load
-            else:
-                total = first[at, :]
-                over[z, rows, :] = total + 0.5 * load
-                first[at, :] = total + load
+    for k in range(STEPS):
+        copies[k][0].wait()
+        copies[k][1].wait()
+
+        def chunk(i, carry, k=k):
+            rows = pl.ds(pl.multiple_of(k * step + i * 16, 16), 16)
+            total = jnp.zeros((16, C), F32)
+            later = Later(4)
+            for z in range(L):
+                odd, upper = classes(lith[z, rows, :])
+                phi = poro[z, rows, :]
+                hz = jnp.exp(pick(odd, upper, H_BASE) + pick(odd, upper, H_SLOPE) * phi)
+                load = (pick(odd, upper, GRAIN_DENSITY) + WATER_DENSITY * phi * recip(1.0 - phi)) * solid[z]
+                later.put((h, (z, rows), hz), (over, (z, rows), total + 0.5 * load))
+                total = total + load
+            first[pl.ds(pl.multiple_of(4 * R + k * step + i * 16, 16), 16), :] = total
             return carry
 
-        lax.fori_loop(0, R // 32, chunk, 0)
-    for z in range(L):
-        copies[z][2].wait()
+        lax.fori_loop(0, step // 16, chunk, 0, unroll=True)
+    for k in range(STEPS):
+        copies[k][2].wait()
     is_odd = (slab[0] & 1) == 1
     o, i = jnp.where(is_odd, 0, L - 1), jnp.where(is_odd, 1, L - 2)
     first[0:R, :] = h[o]
@@ -235,10 +253,13 @@
         xq[s] = po + flow * recip(total)
 
 
-def edge_columns(lo, hi, z, g):
+def both_edges(lo, hi):
     lane = iota((GR, 128), 1)
-    at = 40 * g + 4 * (z + 1)
-    return jnp.where(lane == 0, roll(lo, -at, 1), roll(hi, 127 - at, 1))
+    return jnp.where((lane & 3) == 0, lo, roll(hi, -1, 1))
+
+
+def edge_columns(both, z, g):
+    return roll(both, -40 * g - 4 * (z + 1), 1)
 
 
 def around_x(before, here, after):
@@ -330,28 +351,29 @@
         t = recip(hc[1] + hz[0, rows, :])
         flow = t * (pc[1] - pz[0, rows, :])
         w[2, 0, rows, :] = t
+        later = Later(4)
         for z in range(L):
             hn, pn = hval(z + 1), pval(z + 1)
             t2 = recip(hc[1] + hn[1])
             flow2 = t2 * (pn[1] - pc[1])
-            w[2, z + 1, rows, :] = t2
             total, change = (1.0 + t) + t2, flow2 - flow
+            stores = [(w, (2, z + 1, rows), t2)]
             for k, (hb, pb) in enumerate(zip(around_x(*hc), around_x(*pc))):
                 u = recip(hc[1] + hb)
-                w[k, z, rows, :] = u
+                stores.append((w, (k, z, rows), u))
                 total = total + u
                 change = change + u * (pb - pc[1])
-            w[3, z, rows, :] = total
-            w[4, z, rows, :] = change
+            later.put(*stores, (w, (3, z, rows), total), (w, (4, z, rows), change))
             hc, pc, t, flow = hn, pn, t2, flow2
+        later.flush()
         return carry
 
-    lax.fori_loop(0, R // 8, chunk, 0)
+    lax.fori_loop(0, R // 8, chunk, 0, unroll=True)
 
 
 def inner_kernel(
     slab, shade, h, p, over, lith, first, second, third, w, hz1, pz1, ylo, yhi, wlo, whi,
-    yst, wy, p1, dd, rr, out0, out1, out2,
+    yst, wy, p1, iv, out0, out1, out2,
     hz, pz, eh, ep, eq, o0, o1, o2, sems,
 ):
     is_odd = (slab[0] & 1) == 1
@@ -369,32 +391,31 @@
         for k in range(4):
             yst[s, k] = values[k]
     qlo, qhi = (v[1] + v[3] * recip(v[2]) for v in (lo, hi))
+    hb, pb, qb = both_edges(lo[0], hi[0]), both_edges(lo[1], hi[1]), both_edges(qlo, qhi)
     for z in range(-1, L + 1):
         for g in range(3):
             rows = slice(GR * g, GR * g + GR)
-            eh[z + 1, rows, :] = edge_columns(lo[0], hi[0], z, g)
-            ep[z + 1, rows, :] = edge_columns(lo[1], hi[1], z, g)
+            eh[z + 1, rows, :] = edge_columns(hb, z, g)
+            ep[z + 1, rows, :] = edge_columns(pb, z, g)
             if 0 <= z < L:
-                eq[z, rows, :] = edge_columns(qlo, qhi, z, g)
+                eq[z, rows, :] = edge_columns(qb, z, g)
 
     def chunk1(i, carry):
         rows = at8(i)
         hval, pval = triples(h, p, hz, pz, i)
 
+        later = Later(4)
+
         def finish(z, hc, pc, total, change):
+            stores = []
             for k, (hb, pb) in enumerate(zip(around_y(hc, eh[z + 1, rows, :]), around_y(pc, ep[z + 1, rows, :]))):
                 u = recip(hc + hb)
                 if 0 <= z < L:
-                    wy[k, z, rows, :] = u
+                    stores.append((wy, (k, z, rows), u))
                 total = total + u
                 change = change + u * (pb - pc)
             inv = recip(total)
-            if 0 <= z < L:
-                wy[2, z, rows, :] = inv
-            p1[z + 1, rows, :] = pc + change * inv
-            at = pl.ds(pl.multiple_of(jnp.where(i == LAST, 8, jnp.where(i == 0, 0, 16)), 8), 8)
-            dd[z + 1, at, :] = total
-            rr[z + 1, at, :] = change
+            later.put(*stores, (iv, (z + 1, rows), inv), (p1, (z + 1, rows), pc + change * inv))
 
         for z, out, own in ((-1, -2, 0), (L, L + 1, L - 1)):
             hc, pc = hval(z), pval(z)
@@ -403,9 +424,10 @@
             finish(z, hc[1], pc[1], *sums(hc[1], pc[1], beside))
         for z in range(L):
             finish(z, h[z, rows, :], p[z, rows, :], w[3, z, rows, :], w[4, z, rows, :])
+        later.flush()
         return carry
 
-    lax.fori_loop(0, R // 8, chunk1, 0)
+    lax.fori_loop(0, R // 8, chunk1, 0, unroll=True)
 
     def moved(i):
         return [
@@ -417,26 +439,27 @@
         rows = at8(i)
         here = (at8(i - 1), rows, at8(i + 1))
 
+        later = Later(4)
+
         def put(z, a, b, c):
-            o0[z, rows, :] = a
-            o1[z, rows, :] = b
-            o2[z, rows, :] = c
+            later.put((o0, (z, rows), a), (o1, (z, rows), b), (o2, (z, rows), c))
 
         second_chunk(
             lambda z: tuple(p1[z + 1, r, :] for r in here),
             lambda z: eq[z, rows, :],
-            lambda z, k: (w, w, wy, wy, w, wy)[k][(0, 1, 0, 1, 2, 2)[k], z, rows, :],
+            lambda z, k: iv[z + 1, rows, :] if k == 5 else (w, w, wy, wy, w)[k][(0, 1, 0, 1, 2)[k], z, rows, :],
             lambda z: p[z, rows, :],
             above_rows(slab, first, third, lambda top: pl.ds(pl.multiple_of(top + 8 * i, 8), 8)),
             lambda z: over[z, rows, :],
             lambda z: lith[z, rows, :],
             shade, put,
         )
+        later.flush()
         for copy in moved(i):
             copy.start()
         return carry
 
-    lax.fori_loop(1, LAST, chunk2, 0)
+    lax.fori_loop(1, LAST, chunk2, 0, unroll=True)
 
     def arrive(i, carry):
         for copy in moved(i):
@@ -448,12 +471,12 @@
 
 def outer_kernel(
     slab, shade, h, p, over, lith, first, third, xlo, xhi, vlo, vhi,
-    hz, pz, w, yst, wy, p1, dd, rr, in0, in1, in2,
+    hz, pz, w, yst, wy, p1, iv, in0, in1, in2,
     out0, out1, out2,
     xh, xp, xq, q1, wt, o0, o1, o2, sems,
 ):
     beside_x((xlo, xhi), (vlo, vhi), xh, xp, xq)
-    lo, hi = beside_y_corners((xlo, xhi), yst)
+    columns = both_edges(*beside_y_corners((xlo, xhi), yst))
     sub = iota((8, C), 0)
     copies = []
     for s, top, g, part in ((0, 0, 0, slice(0, 8)), (1, R - 8, 2, slice(GR - 8, GR))):
@@ -464,19 +487,22 @@
         def strip(ref, z, s=s):
             return jnp.broadcast_to(ref[s, z + 1 : z + 2, :], (8, C))
 
+        later = Later(5)
         for z in range(-1, L + 1):
             if 0 <= z < L:
                 hc, pc = h[z, rows, :], p[z, rows, :]
             else:
                 k = 0 if z < 0 else 1
                 hc, pc = hz[k, rows, :], pz[k, rows, :]
-            total, change = dd[z + 1, 8 * s : 8 * s + 8, :], rr[z + 1, 8 * s : 8 * s + 8, :]
+            total = recip(iv[z + 1, rows, :])
+            change = (p1[z + 1, rows, :] - pc) * total
             t = jnp.where(edge, recip(hc + strip(xh, z)), 0.0)
             inv = recip(total + t)
-            q1[s, z + 1] = pc + (change + t * (strip(xp, z) - pc)) * inv
+            stores = [(q1, (s, z + 1), pc + (change + t * (strip(xp, z) - pc)) * inv)]
             if 0 <= z < L:
-                wt[s, 0, z] = w[s, z, rows, :] + t
-                wt[s, 1, z] = inv
+                stores += [(wt, (s, 0, z), w[s, z, rows, :] + t), (wt, (s, 1, z), inv)]
+            later.put(*stores)
+        later.flush()
 
         def q_triple(z, s=s, near=near):
             here = q1[s, z + 1]
@@ -492,14 +518,14 @@
                 return wt[s, 1, z]
             return (w, w, wy, wy, w)[k][(0, 1, 0, 1, 2)[k], z, rows, :]
 
-        def put(z, a, b, c, s=s):
-            o0[s, z] = a
-            o1[s, z] = b
-            o2[s, z] = c
+        later = Later(4)
+
+        def put(z, a, b, c, s=s, later=later):
+            later.put((o0, (s, z), a), (o1, (s, z), b), (o2, (s, z), c))
 
         second_chunk(
             q_triple,
-            lambda z: edge_columns(lo, hi, z, g)[part],
+            lambda z: edge_columns(columns[part], z, g),
             weight,
             lambda z: p[z, rows, :],
             above_rows(slab, first, third, lambda t: slice(t + top, t + top + 8)),
@@ -552,7 +578,7 @@
     p, lith, h, over, first, second, shade = call(
         start_kernel, "start", [SMEM] + [HBM] * 4,
         [vm(*block), (block, jnp.int32, VMEM), vm(*block), vm(*block), vm(5 * R, C), vm(3 * R, C), vm(L, C)],
-        [VMEM(block, F32), SMEM((L,), F32), dma((3, L)), dma(())],
+        [VMEM(block, F32), SMEM((L,), F32), dma((3, STEPS)), dma(())],
     )(slab, p_in, poro, lith_in, solid)
     second_in = lax.ppermute(second, "slab", [(1, 2), (2, 1)])
     first_in = lax.ppermute(first, "slab", [(0, 1), (1, 0), (2, 3), (3, 2)])
@@ -576,21 +602,21 @@
     hbm = (block, F32, HBM)
     plane = VMEM((4, R, C), F32)
     edges = VMEM((L + 2, R, 128), F32)
-    yst, wy, p1, dd, rr, *outs = call(
+    yst, wy, p1, iv, *outs = call(
         inner_kernel, "inner", [SMEM] + [VMEM] * 15,
-        [vm(2, 4, GR, 128), vm(3, L, R, C), vm(L + 2, R, C)] + [vm(L + 2, 24, C)] * 2 + [hbm] * 3,
+        [vm(2, 4, GR, 128), vm(2, L, R, C), vm(L + 2, R, C), vm(L + 2, R, C)] + [hbm] * 3,
         [plane, plane, edges, edges, VMEM((L, R, 128), F32)] + [VMEM(block, F32)] * 3 + [dma((3, R // 8))],
     )(slab, shade, h, p, over, lith, first_in, second_in, third_in, w, hz, pz, ylo, yhi, wlo, whi)
     return tuple(
         call(
-            outer_kernel, "outer", [SMEM] + [VMEM] * 19 + [HBM] * 3, [hbm] * 3,
+            outer_kernel, "outer", [SMEM] + [VMEM] * 18 + [HBM] * 3, [hbm] * 3,
             [VMEM((2, 16, C), F32)] * 3
             + [VMEM((2, L + 2, 8, C), F32), VMEM((2, 2, L, 8, C), F32)]
             + [VMEM((2, L, 8, C), F32)] * 3 + [dma((2, 3))],
-            {20: 0, 21: 1, 22: 2},
+            {19: 0, 20: 1, 21: 2},
         )(
             slab, shade, h, p, over, lith, first_in, third_in, xlo, xhi, vlo, vhi,
-            hz, pz, w, yst, wy, p1, dd, rr, *outs,
+            hz, pz, w, yst, wy, p1, iv, *outs,
         )
     )
 

time: 40 us -> 39.3 us (0.982)
  the two profiles are of different devices: /device:TPU:270 before, /device:TPU:238 now
where the time goes in v4:
time: 39.3 us; the launch traced here: 39 us
  starting transfers between devices  21.8 us (55%)
  Pallas kernels  8.92 us (23%)
  waiting for transfers between devices  7.56 us (19%)
  between operations  0.77 us (2%)
    ppermute x4, starting transfers between devices, pair(): return (lax.ppermute(hi, axis, up), lax.ppermute(lo, axis, down))  14.3 us
    ppermute x4, waiting for transfers between devices, pair(): return (lax.ppermute(hi, axis, up), lax.ppermute(lo, axis, down))  5.15 us
    pallas_call x1, Pallas kernels, body(): call(inner_kernel, 'inner', [SMEM] + [VMEM] * 15, [vm(2, 4, GR, 128), vm(...  3.99 us
    ppermute x1, starting transfers between devices, body(): second_in = lax.ppermute(second, 'slab', [(1, 2), (2, 1)])  2.84 us
    ppermute x1, starting transfers between devices, body(): third_in = lax.ppermute(third, 'slab', [(1, 2), (2, 1), (0, 3)])  2.72 us
    ppermute x1, waiting for transfers between devices, body(): second_in = lax.ppermute(second, 'slab', [(1, 2), (2, 1)])  2.4 us
    ppermute x1, starting transfers between devices, body(): first_in = lax.ppermute(first, 'slab', [(0, 1), (1, 0), (2, 3), (3, 2)])  1.92 us
    pallas_call x1, Pallas kernels, body(): call(start_kernel, 'start', [SMEM] + [HBM] * 4, [vm(*block), (block, jnp....  1.92 us
  transfers between devices with their start and end apart: 7, of which 3 were waited for; matrix products, arithmetic and copies ran while one was open for 0% of the time, Pallas kernels for 15%

profile of v4, /device:TPU:238, one launch (start us, length us, event | category | flops | bytes accessed | tf_op | source)
XLA Modules:
  0.0 39.0 jit_solution(12808387112928868271)
XLA Ops:
  0.6 1.9 %start.1 = (f32[8,96,256]{2,1,0:T(8,128)S(1)}, s32[8,96,256]{2,1,0:T(8,128)S(1)}, f32[8,96,256]{2,1,0:T(8,128)S(1)}, f32[8,96,256]{2,1,0:T(8,128)S(1)}, f32[480,...) custom-call(s32[1]{0:T(128)} %bitcast.slab, f32[8,96,256]{2,1,0:T(8,128)} %p_in.1, ...), custom_call_target="tpu_custom_call" | custom-call | tf_op jit(solution)/shard_map/start/pallas_call | solution.py:578
  2.6 1.9 %collective-permute-start = (f32[480,256]{1,0:T(8,128)S(1)}, f32[480,256]{1,0:T(8,128)S(1)}, u32[]{:S(2)}, u32[]{:S(2)}) collective-permute-start(f32[480,256]{1,0:T(8,128)S(1)} %get-tuple-element.36.mine), channel_id=1, source_target_pairs={{0,128},{128,0},{256,384},{384,256},{1,129},{129,1},{257,385},{385... | collective-permute-start | bytes 1474568 | tf_op jit(solution)/shard_map/ppermute | solution.py:584
  4.5 2.8 %collective-permute-start.2 = (f32[288,256]{1,0:T(8,128)S(1)}, f32[288,256]{1,0:T(8,128)S(1)}, u32[]{:S(2)}, u32[]{:S(2)}) collective-permute-start(f32[288,256]{1,0:T(8,128)S(1)} %get-tuple-element.38), channel_id=1, source_target_pairs={{128,256},{256,128},{129,257},{257,129},{130,258},{258,130},{131,2... | collective-permute-start | bytes 884744 | tf_op jit(solution)/shard_map/ppermute | solution.py:583
  7.3 0.0 collective-permute-done.first
  7.3 0.5 %pack_own.1 = (f32[192,256]{1,0:T(8,128)S(1)}, f32[32,128]{1,0:T(8,128)S(1)}, f32[32,128]{1,0:T(8,128)S(1)}) custom-call(s32[1]{0:T(128)} %bitcast.slab, f32[8,96,256]{2,1,0:T(8,128)S(1)} %get-tuple-element.43.h, f32[8,96,256]{2,1,0:T(8,128)S(1)} %get-tuple-element.33.p, f32[480,256]{1,0:T(8,128)S(1)} %get-tuple-element.36.mine, ...), custom_call_target="tpu_custom_call" | custom-call | tf_op jit(solution)/shard_map/pack_own/pallas_call | solution.py:585
  7.8 2.7 %collective-permute-start.1 = (f32[192,256]{1,0:T(8,128)S(1)}, f32[192,256]{1,0:T(8,128)S(1)}, u32[]{:S(2)}, u32[]{:S(2)}) collective-permute-start(f32[192,256]{1,0:T(8,128)S(1)} %get-tuple-element.37), channel_id=1, source_target_pairs={{128,256},{256,128},{0,384},{129,257},{257,129},{1,385},{130,258},... | collective-permute-start | bytes 589832 | tf_op jit(solution)/shard_map/ppermute | solution.py:588
  10.6 2.4 %collective-permute-done.2.second = f32[288,256]{1,0:T(8,128)S(1)} collective-permute-done((f32[288,256]{1,0:T(8,128)S(1)}, f32[288,256]{1,0:T(8,128)S(1)}, u32[]{:S(2)}, u32[]{:S(2)}) %collective-permute-start.2) | collective-permute-done | bytes 294944 | tf_op jit(solution)/shard_map/ppermute | solution.py:583
  13.0 0.2 pack_y.1
  13.2 4.3 %collective-permute-start.3 = (f32[32,128]{1,0:T(8,128)S(1)}, f32[32,128]{1,0:T(8,128)S(1)}, u32[]{:S(2)}, u32[]{:S(2)}) collective-permute-start(f32[32,128]{1,0:T(8,128)S(1)} %get-tuple-element.41.whi), channel_id=1, source_target_pairs={{0,1},{1,2},{2,3},{3,4},{4,5},{5,6},{6,7},{8,9},{9,10},{10,11},{11... | collective-permute-start | bytes 49160 | tf_op jit(solution)/shard_map/ppermute | solution.py:564
  17.5 3.0 %collective-permute-start.4 = (f32[32,128]{1,0:T(8,128)S(1)}, f32[32,128]{1,0:T(8,128)S(1)}, u32[]{:S(2)}, u32[]{:S(2)}) collective-permute-start(f32[32,128]{1,0:T(8,128)S(1)} %get-tuple-element.42.wlo), channel_id=1, source_target_pairs={{1,0},{2,1},{3,2},{4,3},{5,4},{6,5},{7,6},{9,8},{10,9},{11,10},{12... | collective-permute-start | bytes 49160 | tf_op jit(solution)/shard_map/ppermute | solution.py:564
  20.5 1.0 %pre.1 = (f32[5,9,96,256]{3,2,1,0:T(8,128)S(1)}, f32[2,96,256]{2,1,0:T(8,128)S(1)}, f32[2,96,256]{2,1,0:T(8,128)S(1)}) custom-call(s32[1]{0:T(128)} %bitcast.slab, f32[8,96,256]{2,1,0:T(8,128)S(1)} %get-tuple-element.43.h, f32[8,96,256]{2,1,0:T(8,128)S(1)} %get-tuple-element.33.p, f32[480,256]{1,0:T(8,128)S(1)} %collective-permute-done.first, ...), custom_call_target="tpu_custom_call" | custom-call | tf_op jit(solution)/shard_map/pre/pallas_call | solution.py:594
  21.5 0.0 collective-permute-done.3.ylo
  21.5 4.0 %collective-permute-done.4.yhi = f32[32,128]{1,0:T(8,128)S(1)} collective-permute-done((f32[32,128]{1,0:T(8,128)S(1)}, f32[32,128]{1,0:T(8,128)S(1)}, u32[]{:S(2)}, u32[]{:S(2)}) %collective-permute-start.4) | collective-permute-done | bytes 16416 | tf_op jit(solution)/shard_map/ppermute | solution.py:564
  25.6 5.0 %collective-permute-start.5 = (f32[40,256]{1,0:T(8,128)S(1)}, f32[40,256]{1,0:T(8,128)S(1)}, u32[]{:S(2)}, u32[]{:S(2)}) collective-permute-start(f32[40,256]{1,0:T(8,128)S(1)} %get-tuple-element.47.vhi), channel_id=1, source_target_pairs={{0,8},{8,16},{16,24},{24,32},{32,40},{40,48},{48,56},{56,64},{64,7... | collective-permute-start | bytes 122888 | tf_op jit(solution)/shard_map/ppermute | solution.py:564
  30.6 1.9 %collective-permute-start.6 = (f32[40,256]{1,0:T(8,128)S(1)}, f32[40,256]{1,0:T(8,128)S(1)}, u32[]{:S(2)}, u32[]{:S(2)}) collective-permute-start(f32[40,256]{1,0:T(8,128)S(1)} %get-tuple-element.48.vlo), channel_id=1, source_target_pairs={{8,0},{16,8},{24,16},{32,24},{40,32},{48,40},{56,48},{64,56},{72,6... | collective-permute-start | bytes 122888 | tf_op jit(solution)/shard_map/ppermute | solution.py:564
  32.5 0.0 collective-permute-done.1.third
  32.6 4.0 %inner.1 = (f32[2,4,32,128]{3,2,1,0:T(8,128)S(1)}, f32[2,8,96,256]{3,2,1,0:T(8,128)S(1)}, f32[10,96,256]{2,1,0:T(8,128)S(1)}, f32[10,96,256]{2,1,0:T(8,128)S(1)}...) custom-call(s32[1]{0:T(128)} %bitcast.slab, f32[8,256]{1,0:T(8,128)S(1)} %get-tuple-element.31.shade, ...), custom_call_target="tpu_custom_call" | custom-call | tf_op jit(solution)/shard_map/inner/pallas_call | solution.py:605
  36.5 0.0 collective-permute-done.5.xlo
  36.6 1.2 %collective-permute-done.6.xhi = f32[40,256]{1,0:T(8,128)S(1)} collective-permute-done((f32[40,256]{1,0:T(8,128)S(1)}, f32[40,256]{1,0:T(8,128)S(1)}, u32[]{:S(2)}, u32[]{:S(2)}) %collective-permute-start.6) | collective-permute-done | bytes 40992 | tf_op jit(solution)/shard_map/ppermute | solution.py:564
  37.7 1.3 %outer.1 = (f32[8,96,256]{2,1,0:T(8,128)}, f32[8,96,256]{2,1,0:T(8,128)}, f32[8,96,256]{2,1,0:T(8,128)}) custom-call(s32[1]{0:T(128)} %bitcast.slab, f32[8,256]{1,0:T(8,128)S(1)} %get-tuple-element.31.shade, f32[8,96,256]{2,1,0:T(8,128)S(1)} %get-tuple-element.43.h, ...), custom_call_target="tpu_custom_call", output_to_operand_aliasing={{0}: (19, {}), {1}: (20, {}), {2}: (21, {})} | custom-call | tf_op jit(solution)/shard_map/outer/pallas_call | solution.py:611
  (1 shorter events, 0.0 us)
Async XLA Ops:
  2.6 4.8 %collective-permute-start = (f32[480,256]{1,0:T(8,128)S(1)}, f32[480,256]{1,0:T(8,128)S(1)}, u32[]{:S(2)}, u32[]{:S(2)}) collective-permute-start(f32[480,256]{1,0:T(8,128)S(1)} %get-tuple-element.36.mine), channel_id=1, source_target_pairs={{0,128},{128,0},{256,384},{384,256},{1,129},{129,1},{257,385},{385... | collective-permute-start | bytes 1474568 | tf_op jit(solution)/shard_map/ppermute | solution.py:584
  4.5 8.5 %collective-permute-start.2 = (f32[288,256]{1,0:T(8,128)S(1)}, f32[288,256]{1,0:T(8,128)S(1)}, u32[]{:S(2)}, u32[]{:S(2)}) collective-permute-start(f32[288,256]{1,0:T(8,128)S(1)} %get-tuple-element.38), channel_id=1, source_target_pairs={{128,256},{256,128},{129,257},{257,129},{130,258},{258,130},{131,2... | collective-permute-start | bytes 884744 | tf_op jit(solution)/shard_map/ppermute | solution.py:583
  7.8 24.7 %collective-permute-start.1 = (f32[192,256]{1,0:T(8,128)S(1)}, f32[192,256]{1,0:T(8,128)S(1)}, u32[]{:S(2)}, u32[]{:S(2)}) collective-permute-start(f32[192,256]{1,0:T(8,128)S(1)} %get-tuple-element.37), channel_id=1, source_target_pairs={{128,256},{256,128},{0,384},{129,257},{257,129},{1,385},{130,258},... | collective-permute-start | bytes 589832 | tf_op jit(solution)/shard_map/ppermute | solution.py:588
  13.2 8.4 %collective-permute-start.3 = (f32[32,128]{1,0:T(8,128)S(1)}, f32[32,128]{1,0:T(8,128)S(1)}, u32[]{:S(2)}, u32[]{:S(2)}) collective-permute-start(f32[32,128]{1,0:T(8,128)S(1)} %get-tuple-element.41.whi), channel_id=1, source_target_pairs={{0,1},{1,2},{2,3},{3,4},{4,5},{5,6},{6,7},{8,9},{9,10},{10,11},{11... | collective-permute-start | bytes 49160 | tf_op jit(solution)/shard_map/ppermute | solution.py:564
  17.5 8.0 %collective-permute-start.4 = (f32[32,128]{1,0:T(8,128)S(1)}, f32[32,128]{1,0:T(8,128)S(1)}, u32[]{:S(2)}, u32[]{:S(2)}) collective-permute-start(f32[32,128]{1,0:T(8,128)S(1)} %get-tuple-element.42.wlo), channel_id=1, source_target_pairs={{1,0},{2,1},{3,2},{4,3},{5,4},{6,5},{7,6},{9,8},{10,9},{11,10},{12... | collective-permute-start | bytes 49160 | tf_op jit(solution)/shard_map/ppermute | solution.py:564
  25.6 11.0 %collective-permute-start.5 = (f32[40,256]{1,0:T(8,128)S(1)}, f32[40,256]{1,0:T(8,128)S(1)}, u32[]{:S(2)}, u32[]{:S(2)}) collective-permute-start(f32[40,256]{1,0:T(8,128)S(1)} %get-tuple-element.47.vhi), channel_id=1, source_target_pairs={{0,8},{8,16},{16,24},{24,32},{32,40},{40,48},{48,56},{56,64},{64,7... | collective-permute-start | bytes 122888 | tf_op jit(solution)/shard_map/ppermute | solution.py:564
  30.6 7.1 %collective-permute-start.6 = (f32[40,256]{1,0:T(8,128)S(1)}, f32[40,256]{1,0:T(8,128)S(1)}, u32[]{:S(2)}, u32[]{:S(2)}) collective-permute-start(f32[40,256]{1,0:T(8,128)S(1)} %get-tuple-element.48.vlo), channel_id=1, source_target_pairs={{8,0},{16,8},{24,16},{32,24},{40,32},{48,40},{56,48},{64,56},{72,6... | collective-permute-start | bytes 122888 | tf_op jit(solution)/shard_map/ppermute | solution.py:564

commit v5 on v4

--- a/solution.py
+++ b/solution.py
@@ -69,6 +69,18 @@
         for ref, at, value in self.kept:
             ref[at] = value
         self.kept = []
+
+
+def packed(plane, layers, acc_lo, acc_hi):
+    lane = iota((GR, 128), 1)
+    for g in range(3):
+        for z in layers:
+            for arr in range(2):
+                base = 40 * g + 4 * (z + 1) + 2 * arr
+                here = (lane >= base) & (lane < base + 2)
+                acc_lo = jnp.where(here, roll(plane(arr, z, g, slice(0, 128)), base, 1), acc_lo)
+                acc_hi = jnp.where(here, roll(plane(arr, z, g, slice(C - 128, C)), base + 2, 1), acc_hi)
+    return acc_lo, acc_hi
 
 
 def start_kernel(slab, p_in, poro_in, lith_in, solid_in, p, lith, h, over, first, second, shade, poro, solid, sems, solid_sem):
@@ -115,41 +127,49 @@
     first[R : 2 * R, :] = p[o]
     first[2 * R : 3 * R, :] = h[i]
     first[3 * R : 4 * R, :] = p[i]
+    o = jnp.where(is_odd, L - 1, 0)
+    zero = jnp.zeros((GR, 128), F32)
+    lo, hi = packed(lambda arr, z, g, cols: (h, p)[arr][o, GR * g : GR * g + GR, cols], (-1,), zero, zero)
+    second[0:GR, 0:128] = lo
+    second[0:GR, 128:256] = hi
+    for k, (ref, row) in enumerate(((h, 0), (p, 0), (h, R - 1), (p, R - 1))):
+        second[GR + k : GR + k + 1, :] = ref[o, row : row + 1, :]
+    second[GR + 4 : GR + 8, :] = jnp.zeros((4, C), F32)
+
+
+def pack_own_kernel(slab, h, p, mine, first, planes, both, lo, hi):
+    is_odd = (slab[0] & 1) == 1
+    zero = jnp.zeros((GR, 128), F32)
+    own = packed(lambda arr, z, g, cols: (h, p)[arr][z, GR * g : GR * g + GR, cols], range(L), zero, zero)
+    near = packed(
+        lambda arr, z, g, cols: first[R * arr + GR * g : R * arr + GR * g + GR, cols], (-1,), zero, zero
+    )
+    for ref, a, b in zip((lo, hi), own, near):
+        ref[...] = a + jnp.where(is_odd, b, roll(b, 4 * (L + 1), 1))
+    total = mine[4 * R : 5 * R, :] + first[4 * R : 5 * R, :]
     o, i = jnp.where(is_odd, L - 1, 0), jnp.where(is_odd, L - 2, 1)
-    second[0:R, :] = h[o]
-    second[R : 2 * R, :] = p[o]
-    second[2 * R : 3 * R, :] = h[i]
-
-
-def packed(plane, layers, acc_lo, acc_hi):
-    lane = iota((GR, 128), 1)
-    for g in range(3):
-        for z in layers:
-            for arr in range(2):
-                base = 40 * g + 4 * (z + 1) + 2 * arr
-                here = (lane >= base) & (lane < base + 2)
-                acc_lo = jnp.where(here, roll(plane(arr, z, g, slice(0, 128)), base, 1), acc_lo)
-                acc_hi = jnp.where(here, roll(plane(arr, z, g, slice(C - 128, C)), base + 2, 1), acc_hi)
-    return acc_lo, acc_hi
-
-
-def pack_y_kernel(slab, first, second, own_lo, own_hi, lo, hi):
+    planes[0:R, :] = h[o]
+    planes[R : 2 * R, :] = p[o]
+    planes[2 * R : 3 * R, :] = h[i]
+    planes[3 * R : 4 * R, :] = p[i]
+    planes[4 * R : 5 * R, :] = total
+    both[...] = total
+
+
+def pack_y_kernel(slab, edges, own_lo, own_hi, lo, hi):
     is_odd = (slab[0] & 1) == 1
-
-    def plane(arr, z, g, cols):
-        at = slice(R * arr + GR * g, R * arr + GR * g + GR)
-        a, b = first[at, cols], second[at, cols]
-        return jnp.where(is_odd, a, b) if z < 0 else jnp.where(is_odd, b, a)
-
-    lo[...], hi[...] = packed(plane, (-1, L), own_lo[...], own_hi[...])
-
-
-def pack_x_kernel(slab, h, p, first, second, ylo, yhi, lo, hi):
+    for ref, own, cols in ((lo, own_lo, slice(0, 128)), (hi, own_hi, slice(128, 256))):
+        b = edges[0:GR, cols]
+        ref[...] = own[...] + jnp.where(is_odd, roll(b, 4 * (L + 1), 1), b)
+
+
+def pack_x_kernel(slab, h, p, first, edges, ylo, yhi, lo, hi):
     is_odd = (slab[0] & 1) == 1
-    for ref, o, i, yrow in ((lo, 0, 1, 0), (hi, R - 1, R - 2, GR - 1)):
+    for s, (ref, o, i, yrow) in enumerate(((lo, 0, 1, 0), (hi, R - 1, R - 2, GR - 1))):
         for arr, own in ((0, h), (1, p)):
-            at = slice(R * arr + o, R * arr + o + 1)
-            a, b = first[at, :], second[at, :]
+            at = R * arr + o
+            k = GR + 2 * s + arr
+            a, b = first[at : at + 1, :], edges[k : k + 1, :]
             top = 10 * arr
             ref[top : top + 1, :] = jnp.where(is_odd, a, b)
             for z in range(L):
@@ -297,9 +317,10 @@
         qc, flow = qn, flow2
 
 
-def above_rows(slab, first, third, rows):
+def above_rows(slab, first, planes, both, rows):
     base = jnp.where((slab[0] & 1) == 1, first[rows(4 * R), :], 0.0)
-    return base + jnp.where(slab[0] >= 2, third[rows(R), :], 0.0)
+    base = base + jnp.where(slab[0] == 2, planes[rows(4 * R), :], 0.0)
+    return base + jnp.where(slab[0] == 3, both[rows(0), :], 0.0)
 
 
 def at8(i):
@@ -327,65 +348,54 @@
     return hval, pval
 
 
-def pack_own_kernel(slab, h, p, mine, first, third, lo, hi):
-    zero = jnp.zeros((GR, 128), F32)
-    lo[...], hi[...] = packed(
-        lambda arr, z, g, cols: (h, p)[arr][z, GR * g : GR * g + GR, cols], range(L), zero, zero
-    )
-    i = jnp.where((slab[0] & 1) == 1, L - 2, 1)
-    third[0:R, :] = p[i]
-    third[R : 2 * R, :] = mine[4 * R : 5 * R, :] + first[4 * R : 5 * R, :]
-
-
-def pre_kernel(slab, h, p, first, second, w, hz, pz):
-    is_odd = (slab[0] & 1) == 1
-    for ref, at, fix in ((hz, 0, present), (pz, R, lambda t: t)):
-        a, b = first[at : at + R, :], second[at : at + R, :]
-        ref[0] = fix(jnp.where(is_odd, a, b))
-        ref[1] = fix(jnp.where(is_odd, b, a))
-
+def pre_kernel(h, p, wlo, w):
     def chunk(i, carry):
         rows = at8(i)
-        hval, pval = triples(h, p, hz, pz, i)
+        hval, pval = triples(h, p, None, None, i)
         hc, pc = hval(0), pval(0)
-        t = recip(hc[1] + hz[0, rows, :])
-        flow = t * (pc[1] - pz[0, rows, :])
-        w[2, 0, rows, :] = t
+        t, flow = None, None
         later = Later(4)
         for z in range(L):
-            hn, pn = hval(z + 1), pval(z + 1)
-            t2 = recip(hc[1] + hn[1])
-            flow2 = t2 * (pn[1] - pc[1])
-            total, change = (1.0 + t) + t2, flow2 - flow
-            stores = [(w, (2, z + 1, rows), t2)]
+            stores = []
+            total, change = 1.0, 0.0
+            if z > 0:
+                total, change = total + t, change - flow
+            if z < L - 1:
+                hn, pn = hval(z + 1), pval(z + 1)
+                t = recip(hc[1] + hn[1])
+                flow = t * (pn[1] - pc[1])
+                stores.append((w, (2, z + 1, rows), t))
+                total, change = total + t, change + flow
             for k, (hb, pb) in enumerate(zip(around_x(*hc), around_x(*pc))):
                 u = recip(hc[1] + hb)
                 stores.append((w, (k, z, rows), u))
                 total = total + u
                 change = change + u * (pb - pc[1])
             later.put(*stores, (w, (3, z, rows), total), (w, (4, z, rows), change))
-            hc, pc, t, flow = hn, pn, t2, flow2
+            hc, pc = hn, pn
         later.flush()
         return carry
 
     lax.fori_loop(0, R // 8, chunk, 0, unroll=True)
 
 
+def weight_of(w, wy, wz, z, k, rows):
+    if k == 4 and z in (0, L):
+        return wz[z // L, rows, :]
+    return (w, w, wy, wy, w)[k][(0, 1, 0, 1, 2)[k], z, rows, :]
+
+
 def inner_kernel(
-    slab, shade, h, p, over, lith, first, second, third, w, hz1, pz1, ylo, yhi, wlo, whi,
-    yst, wy, p1, iv, out0, out1, out2,
-    hz, pz, eh, ep, eq, o0, o1, o2, sems,
+    slab, shade, h, p, over, lith, first, planes, both, w, ylo, yhi, wlo, whi,
+    yst, wy, wz, p1, iv, hz, pz, out0, out1, out2,
+    eh, ep, eq, o0, o1, o2, sems,
 ):
     is_odd = (slab[0] & 1) == 1
     for k in range(2):
-        hz[k] = hz1[k]
-        pz[k] = pz1[k]
-    for ref, a, b, fix in (
-        (hz, first[2 * R : 3 * R, :], second[2 * R : 3 * R, :], present),
-        (pz, first[3 * R : 4 * R, :], third[0:R, :], lambda t: t),
-    ):
-        ref[2] = fix(jnp.where(is_odd, a, b))
-        ref[3] = fix(jnp.where(is_odd, b, a))
+        for ref, at, fix in ((hz, 2 * k * R, present), (pz, (2 * k + 1) * R, lambda t: t)):
+            a, b = first[at : at + R, :], planes[at : at + R, :]
+            ref[2 * k] = fix(jnp.where(is_odd, a, b))
+            ref[2 * k + 1] = fix(jnp.where(is_odd, b, a))
     lo, hi = beside_y((ylo, yhi), (wlo, whi))
     for s, values in enumerate((lo, hi)):
         for k in range(4):
@@ -423,7 +433,13 @@
             beside += list(zip(around_x(*hc), around_x(*pc)))
             finish(z, hc[1], pc[1], *sums(hc[1], pc[1], beside))
         for z in range(L):
-            finish(z, h[z, rows, :], p[z, rows, :], w[3, z, rows, :], w[4, z, rows, :])
+            hc, pc, total, change = h[z, rows, :], p[z, rows, :], w[3, z, rows, :], w[4, z, rows, :]
+            for k in ((0,) if z == 0 else (1,) if z == L - 1 else ()):
+                t = recip(hc + hz[k, rows, :])
+                later.kept.append((wz, (k, rows), t))
+                total = total + t
+                change = change + t * (pz[k, rows, :] - pc)
+            finish(z, hc, pc, total, change)
         later.flush()
         return carry
 
@@ -447,9 +463,9 @@
         second_chunk(
             lambda z: tuple(p1[z + 1, r, :] for r in here),
             lambda z: eq[z, rows, :],
-            lambda z, k: iv[z + 1, rows, :] if k == 5 else (w, w, wy, wy, w)[k][(0, 1, 0, 1, 2)[k], z, rows, :],
+            lambda z, k: iv[z + 1, rows, :] if k == 5 else weight_of(w, wy, wz, z, k, rows),
             lambda z: p[z, rows, :],
-            above_rows(slab, first, third, lambda top: pl.ds(pl.multiple_of(top + 8 * i, 8), 8)),
+            above_rows(slab, first, planes, both, lambda top: pl.ds(pl.multiple_of(top + 8 * i, 8), 8)),
             lambda z: over[z, rows, :],
             lambda z: lith[z, rows, :],
             shade, put,
@@ -470,8 +486,8 @@
 
 
 def outer_kernel(
-    slab, shade, h, p, over, lith, first, third, xlo, xhi, vlo, vhi,
-    hz, pz, w, yst, wy, p1, iv, in0, in1, in2,
+    slab, shade, h, p, over, lith, first, planes, both, xlo, xhi, vlo, vhi,
+    w, yst, wy, wz, p1, iv, hz, pz, in0, in1, in2,
     out0, out1, out2,
     xh, xp, xq, q1, wt, o0, o1, o2, sems,
 ):
@@ -516,7 +532,7 @@
                 return wt[s, 0, z]
             if k == 5:
                 return wt[s, 1, z]
-            return (w, w, wy, wy, w)[k][(0, 1, 0, 1, 2)[k], z, rows, :]
+            return weight_of(w, wy, wz, z, k, rows)
 
         later = Later(4)
 
@@ -528,7 +544,7 @@
             lambda z: edge_columns(columns[part], z, g),
             weight,
             lambda z: p[z, rows, :],
-            above_rows(slab, first, third, lambda t: slice(t + top, t + top + 8)),
+            above_rows(slab, first, planes, both, lambda t: slice(t + top, t + top + 8)),
             lambda z: over[z, rows, :],
             lambda z: lith[z, rows, :],
             shade, put,
@@ -575,48 +591,45 @@
     slab = lax.axis_index("slab").astype(jnp.int32).reshape(1)
     block = (L, R, C)
     dma = pltpu.SemaphoreType.DMA
-    p, lith, h, over, first, second, shade = call(
+    p, lith, h, over, first, edges, shade = call(
         start_kernel, "start", [SMEM] + [HBM] * 4,
-        [vm(*block), (block, jnp.int32, VMEM), vm(*block), vm(*block), vm(5 * R, C), vm(3 * R, C), vm(L, C)],
+        [vm(*block), (block, jnp.int32, VMEM), vm(*block), vm(*block), vm(5 * R, C), vm(GR + 8, C), vm(L, C)],
         [VMEM(block, F32), SMEM((L,), F32), dma((3, STEPS)), dma(())],
     )(slab, p_in, poro, lith_in, solid)
-    second_in = lax.ppermute(second, "slab", [(1, 2), (2, 1)])
+    edges_in = lax.ppermute(edges, "slab", [(1, 2), (2, 1)])
     first_in = lax.ppermute(first, "slab", [(0, 1), (1, 0), (2, 3), (3, 2)])
-    third, *own_y = call(
-        pack_own_kernel, "pack_own", [SMEM] + [VMEM] * 4, [vm(2 * R, C), vm(GR, 128), vm(GR, 128)]
+    planes, both, *own_y = call(
+        pack_own_kernel, "pack_own", [SMEM] + [VMEM] * 4,
+        [vm(5 * R, C), vm(R, C), vm(GR, 128), vm(GR, 128)],
     )(slab, h, p, first, first_in)
-    third_in = lax.ppermute(third, "slab", [(1, 2), (2, 1), (0, 3)])
-    wlo, whi = call(pack_y_kernel, "pack_y", [SMEM] + [VMEM] * 4, [vm(GR, 128)] * 2)(
-        slab, first_in, second_in, *own_y
-    )
+    planes, both, edges_in = lax.optimization_barrier((planes, both, edges_in))
+    planes_in = lax.ppermute(planes, "slab", [(1, 2), (2, 1)])
+    both_in = lax.ppermute(both, "slab", [(0, 3)])
+    wlo, whi = call(pack_y_kernel, "pack_y", [SMEM] + [VMEM] * 3, [vm(GR, 128)] * 2)(slab, edges_in, *own_y)
     ylo, yhi = pair("mapy", wlo, whi)
-    h2, wlo2 = lax.optimization_barrier((h, wlo))
-    w, hz, pz = call(
-        pre_kernel, "pre", [SMEM] + [VMEM] * 4, [vm(5, L + 1, R, C), vm(2, R, C), vm(2, R, C)]
-    )(slab, h2, p, first_in, second_in)
-    ylo, yhi, hz = lax.optimization_barrier((ylo, yhi, hz))
+    (w,) = call(pre_kernel, "pre", [VMEM] * 3, [vm(5, L + 1, R, C)])(h, p, wlo)
+    ylo, yhi, w = lax.optimization_barrier((ylo, yhi, w))
     vlo, vhi = call(pack_x_kernel, "pack_x", [SMEM] + [VMEM] * 6, [vm(40, C)] * 2)(
-        slab, h, p, first_in, second_in, ylo, yhi
+        slab, h, p, first_in, edges_in, ylo, yhi
     )
     xlo, xhi = pair("mapx", vlo, vhi)
     hbm = (block, F32, HBM)
-    plane = VMEM((4, R, C), F32)
-    edges = VMEM((L + 2, R, 128), F32)
-    yst, wy, p1, iv, *outs = call(
-        inner_kernel, "inner", [SMEM] + [VMEM] * 15,
-        [vm(2, 4, GR, 128), vm(2, L, R, C), vm(L + 2, R, C), vm(L + 2, R, C)] + [hbm] * 3,
-        [plane, plane, edges, edges, VMEM((L, R, 128), F32)] + [VMEM(block, F32)] * 3 + [dma((3, R // 8))],
-    )(slab, shade, h, p, over, lith, first_in, second_in, third_in, w, hz, pz, ylo, yhi, wlo, whi)
+    columns = VMEM((L + 2, R, 128), F32)
+    yst, wy, wz, p1, iv, hz, pz, *outs = call(
+        inner_kernel, "inner", [SMEM] + [VMEM] * 13,
+        [vm(2, 4, GR, 128), vm(2, L, R, C), vm(2, R, C)] + [vm(L + 2, R, C)] * 2 + [vm(4, R, C)] * 2 + [hbm] * 3,
+        [columns, columns, VMEM((L, R, 128), F32)] + [VMEM(block, F32)] * 3 + [dma((3, R // 8))],
+    )(slab, shade, h, p, over, lith, first_in, planes_in, both_in, w, ylo, yhi, wlo, whi)
     return tuple(
         call(
-            outer_kernel, "outer", [SMEM] + [VMEM] * 18 + [HBM] * 3, [hbm] * 3,
+            outer_kernel, "outer", [SMEM] + [VMEM] * 20 + [HBM] * 3, [hbm] * 3,
             [VMEM((2, 16, C), F32)] * 3
             + [VMEM((2, L + 2, 8, C), F32), VMEM((2, 2, L, 8, C), F32)]
             + [VMEM((2, L, 8, C), F32)] * 3 + [dma((2, 3))],
-            {19: 0, 20: 1, 21: 2},
+            {21: 0, 22: 1, 23: 2},
         )(
-            slab, shade, h, p, over, lith, first_in, third_in, xlo, xhi, vlo, vhi,
-            hz, pz, w, yst, wy, p1, iv, *outs,
+            slab, shade, h, p, over, lith, first_in, planes_in, both_in, xlo, xhi, vlo, vhi,
+            w, yst, wy, wz, p1, iv, hz, pz, *outs,
         )
     )
 

time: 39.3 us -> 39.4 us (level)
  starting transfers between devices: 21.8 us -> 22.6 us
  waiting for transfers between devices: 7.56 us -> 6.76 us
    ppermute x2 -> x3, starting transfers between devices: 5.56 us -> 6.33 us  [the longest x1 2.84 us: body(): edges_in = lax.ppermute(edges, 'slab', [(1, 2), (2, 1)])]
    ppermute x2 -> x3, waiting for transfers between devices: 2.41 us -> 1.87 us  [the longest x1 1.87 us: body(): edges_in = lax.ppermute(edges, 'slab', [(1, 2), (2, 1)])]
  transfers between devices with their start and end apart: 7 -> 8, of which waited for: 3 -> 3; matrix products, arithmetic and copies ran while one was open for 0% -> 0% of each run, Pallas kernels for 15% -> 14%
where the time goes in v5:
time: 39.4 us; the launch traced here: 39.1 us
  starting transfers between devices  22.6 us (57%)
  Pallas kernels  8.99 us (23%)
  waiting for transfers between devices  6.76 us (17%)
  between operations  0.78 us (2%)
    ppermute x4, starting transfers between devices, pair(): return (lax.ppermute(hi, axis, up), lax.ppermute(lo, axis, down))  14.3 us
    ppermute x4, waiting for transfers between devices, pair(): return (lax.ppermute(hi, axis, up), lax.ppermute(lo, axis, down))  4.88 us
    pallas_call x1, Pallas kernels, body(): call(inner_kernel, 'inner', [SMEM] + [VMEM] * 13, [vm(2, 4, GR, 128), vm(...  4.06 us
    ppermute x1, starting transfers between devices, body(): edges_in = lax.ppermute(edges, 'slab', [(1, 2), (2, 1)])  2.84 us
    ppermute x1, starting transfers between devices, body(): planes_in = lax.ppermute(planes, 'slab', [(1, 2), (2, 1)])  2.83 us
    pallas_call x1, Pallas kernels, body(): call(start_kernel, 'start', [SMEM] + [HBM] * 4, [vm(*block), (block, jnp....  2.01 us
    ppermute x1, starting transfers between devices, body(): first_in = lax.ppermute(first, 'slab', [(0, 1), (1, 0), (2, 3), (3, 2)])  1.92 us
    ppermute x1, waiting for transfers between devices, body(): edges_in = lax.ppermute(edges, 'slab', [(1, 2), (2, 1)])  1.87 us
  transfers between devices with their start and end apart: 8, of which 3 were waited for; matrix products, arithmetic and copies ran while one was open for 0% of the time, Pallas kernels for 14%

profile of v5, /device:TPU:238, one launch (start us, length us, event | category | flops | bytes accessed | tf_op | source)
XLA Modules:
  0.0 39.1 jit_solution(7209448787901847257)
XLA Ops:
  0.6 2.0 %start.1 = (f32[8,96,256]{2,1,0:T(8,128)S(1)}, s32[8,96,256]{2,1,0:T(8,128)S(1)}, f32[8,96,256]{2,1,0:T(8,128)S(1)}, f32[8,96,256]{2,1,0:T(8,128)S(1)}, f32[480,...) custom-call(s32[1]{0:T(128)} %bitcast.slab, f32[8,96,256]{2,1,0:T(8,128)} %p_in.1, ...), custom_call_target="tpu_custom_call" | custom-call | tf_op jit(solution)/shard_map/start/pallas_call | solution.py:594
  2.7 1.9 %collective-permute-start = (f32[480,256]{1,0:T(8,128)S(1)}, f32[480,256]{1,0:T(8,128)S(1)}, u32[]{:S(2)}, u32[]{:S(2)}) collective-permute-start(f32[480,256]{1,0:T(8,128)S(1)} %get-tuple-element.39.mine), channel_id=1, source_target_pairs={{0,128},{128,0},{256,384},{384,256},{1,129},{129,1},{257,385},{385... | collective-permute-start | bytes 1474568 | tf_op jit(solution)/shard_map/ppermute | solution.py:600
  4.6 2.8 %collective-permute-start.1 = (f32[40,256]{1,0:T(8,128)S(1)}, f32[40,256]{1,0:T(8,128)S(1)}, u32[]{:S(2)}, u32[]{:S(2)}) collective-permute-start(f32[40,256]{1,0:T(8,128)S(1)} %get-tuple-element.42), channel_id=1, source_target_pairs={{128,256},{256,128},{129,257},{257,129},{130,258},{258,130},{131,2... | collective-permute-start | bytes 122888 | tf_op jit(solution)/shard_map/ppermute | solution.py:599
  7.4 0.0 collective-permute-done.first
  7.4 0.6 %pack_own.1 = (f32[480,256]{1,0:T(8,128)S(1)}, f32[96,256]{1,0:T(8,128)S(1)}, f32[32,128]{1,0:T(8,128)S(1)}, f32[32,128]{1,0:T(8,128)S(1)}) custom-call(s32[1]{0:T(128)} %bitcast.slab, f32[8,96,256]{2,1,0:T(8,128)S(1)} %get-tuple-element.35.h, f32[8,96,256]{2,1,0:T(8,128)S(1)} %get-tuple-element.36.p, f32[480,256]{1,0:T(8,128)S(1)} %get-tuple-element.39.mine, ...), custom_call_target="tpu_custom_call" | custom-call | tf_op jit(solution)/shard_map/pack_own/pallas_call | solution.py:601
  8.0 1.9 %collective-permute-done.1.edges = f32[40,256]{1,0:T(8,128)S(1)} collective-permute-done((f32[40,256]{1,0:T(8,128)S(1)}, f32[40,256]{1,0:T(8,128)S(1)}, u32[]{:S(2)}, u32[]{:S(2)}) %collective-permute-start.1) | collective-permute-done | bytes 40992 | tf_op jit(solution)/shard_map/ppermute | solution.py:599
  9.9 2.8 %collective-permute-start.2 = (f32[480,256]{1,0:T(8,128)S(1)}, f32[480,256]{1,0:T(8,128)S(1)}, u32[]{:S(2)}, u32[]{:S(2)}) collective-permute-start(f32[480,256]{1,0:T(8,128)S(1)} %get-tuple-element.43), channel_id=1, source_target_pairs={{128,256},{256,128},{129,257},{257,129},{130,258},{258,130},{131,2... | collective-permute-start | bytes 1474568 | tf_op jit(solution)/shard_map/ppermute | solution.py:606
  12.7 0.7 %collective-permute-start.3 = (f32[96,256]{1,0:T(8,128)S(1)}, f32[96,256]{1,0:T(8,128)S(1)}, u32[]{:S(2)}, u32[]{:S(2)}) collective-permute-start(f32[96,256]{1,0:T(8,128)S(1)} %get-tuple-element.44), channel_id=1, source_target_pairs={{0,384},{1,385},{2,386},{3,387},{4,388},{5,389},{6,390},{7,391},{8... | collective-permute-start | bytes 294920 | tf_op jit(solution)/shard_map/ppermute | solution.py:607
  13.4 0.1 pack_y.1
  13.5 4.0 %collective-permute-start.4 = (f32[32,128]{1,0:T(8,128)S(1)}, f32[32,128]{1,0:T(8,128)S(1)}, u32[]{:S(2)}, u32[]{:S(2)}) collective-permute-start(f32[32,128]{1,0:T(8,128)S(1)} %get-tuple-element.48.whi), channel_id=1, source_target_pairs={{0,1},{1,2},{2,3},{3,4},{4,5},{5,6},{6,7},{8,9},{9,10},{10,11},{11... | collective-permute-start | bytes 49160 | tf_op jit(solution)/shard_map/ppermute | solution.py:580
  17.5 3.3 %collective-permute-start.5 = (f32[32,128]{1,0:T(8,128)S(1)}, f32[32,128]{1,0:T(8,128)S(1)}, u32[]{:S(2)}, u32[]{:S(2)}) collective-permute-start(f32[32,128]{1,0:T(8,128)S(1)} %get-tuple-element.49.wlo), channel_id=1, source_target_pairs={{1,0},{2,1},{3,2},{4,3},{5,4},{6,5},{7,6},{9,8},{10,9},{11,10},{12... | collective-permute-start | bytes 49160 | tf_op jit(solution)/shard_map/ppermute | solution.py:580
  20.9 0.9 %pre.1.w = f32[5,9,96,256]{3,2,1,0:T(8,128)S(1)} custom-call(f32[8,96,256]{2,1,0:T(8,128)S(1)} %get-tuple-element.35.h, f32[8,96,256]{2,1,0:T(8,128)S(1)} %get-tuple-element.36.p, f32[32,128]{1,0:T(8,128)S(1)} %get-tuple-element.49.wlo), custom_call_target="tpu_custom_call" | custom-call | tf_op jit(solution)/shard_map/pre/pallas_call | solution.py:610
  21.8 0.0 collective-permute-done.4.ylo
  21.8 3.8 %collective-permute-done.5.yhi = f32[32,128]{1,0:T(8,128)S(1)} collective-permute-done((f32[32,128]{1,0:T(8,128)S(1)}, f32[32,128]{1,0:T(8,128)S(1)}, u32[]{:S(2)}, u32[]{:S(2)}) %collective-permute-start.5) | collective-permute-done | bytes 16416 | tf_op jit(solution)/shard_map/ppermute | solution.py:580
  25.6 5.0 %collective-permute-start.6 = (f32[40,256]{1,0:T(8,128)S(1)}, f32[40,256]{1,0:T(8,128)S(1)}, u32[]{:S(2)}, u32[]{:S(2)}) collective-permute-start(f32[40,256]{1,0:T(8,128)S(1)} %get-tuple-element.52.vhi), channel_id=1, source_target_pairs={{0,8},{8,16},{16,24},{24,32},{32,40},{40,48},{48,56},{56,64},{64,7... | collective-permute-start | bytes 122888 | tf_op jit(solution)/shard_map/ppermute | solution.py:580
  30.7 1.9 %collective-permute-start.7 = (f32[40,256]{1,0:T(8,128)S(1)}, f32[40,256]{1,0:T(8,128)S(1)}, u32[]{:S(2)}, u32[]{:S(2)}) collective-permute-start(f32[40,256]{1,0:T(8,128)S(1)} %get-tuple-element.53.vlo), channel_id=1, source_target_pairs={{8,0},{16,8},{24,16},{32,24},{40,32},{48,40},{56,48},{64,56},{72,6... | collective-permute-start | bytes 122888 | tf_op jit(solution)/shard_map/ppermute | solution.py:580
  32.6 0.0 collective-permute-done.3.both
  32.6 0.0 collective-permute-done.2.planes
  32.6 4.1 %inner.1 = (f32[2,4,32,128]{3,2,1,0:T(8,128)S(1)}, f32[2,8,96,256]{3,2,1,0:T(8,128)S(1)}, f32[2,96,256]{2,1,0:T(8,128)S(1)}, f32[10,96,256]{2,1,0:T(8,128)S(1)},...) custom-call(s32[1]{0:T(128)} %bitcast.slab, ...), custom_call_target="tpu_custom_call" | custom-call | tf_op jit(solution)/shard_map/inner/pallas_call | solution.py:618
  36.7 0.0 collective-permute-done.6.xlo
  36.7 1.1 %collective-permute-done.7.xhi = f32[40,256]{1,0:T(8,128)S(1)} collective-permute-done((f32[40,256]{1,0:T(8,128)S(1)}, f32[40,256]{1,0:T(8,128)S(1)}, u32[]{:S(2)}, u32[]{:S(2)}) %collective-permute-start.7) | collective-permute-done | bytes 40992 | tf_op jit(solution)/shard_map/ppermute | solution.py:580
  37.8 1.3 %outer.1 = (f32[8,96,256]{2,1,0:T(8,128)}, f32[8,96,256]{2,1,0:T(8,128)}, f32[8,96,256]{2,1,0:T(8,128)}) custom-call(s32[1]{0:T(128)} %bitcast.slab, f32[8,256]{1,0:T(8,128)S(1)} %get-tuple-element.34.shade, f32[8,96,256]{2,1,0:T(8,128)S(1)} %get-tuple-element.35.h, ...), custom_call_target="tpu_custom_call", output_to_operand_aliasing={{0}: (21, {}), {1}: (22, {}), {2}: (23, {})} | custom-call | tf_op jit(solution)/shard_map/outer/pallas_call | solution.py:624
  (1 shorter events, 0.0 us)
Async XLA Ops:
  2.7 4.8 %collective-permute-start = (f32[480,256]{1,0:T(8,128)S(1)}, f32[480,256]{1,0:T(8,128)S(1)}, u32[]{:S(2)}, u32[]{:S(2)}) collective-permute-start(f32[480,256]{1,0:T(8,128)S(1)} %get-tuple-element.39.mine), channel_id=1, source_target_pairs={{0,128},{128,0},{256,384},{384,256},{1,129},{129,1},{257,385},{385... | collective-permute-start | bytes 1474568 | tf_op jit(solution)/shard_map/ppermute | solution.py:600
  4.6 5.3 %collective-permute-start.1 = (f32[40,256]{1,0:T(8,128)S(1)}, f32[40,256]{1,0:T(8,128)S(1)}, u32[]{:S(2)}, u32[]{:S(2)}) collective-permute-start(f32[40,256]{1,0:T(8,128)S(1)} %get-tuple-element.42), channel_id=1, source_target_pairs={{128,256},{256,128},{129,257},{257,129},{130,258},{258,130},{131,2... | collective-permute-start | bytes 122888 | tf_op jit(solution)/shard_map/ppermute | solution.py:599
  9.9 22.7 %collective-permute-start.2 = (f32[480,256]{1,0:T(8,128)S(1)}, f32[480,256]{1,0:T(8,128)S(1)}, u32[]{:S(2)}, u32[]{:S(2)}) collective-permute-start(f32[480,256]{1,0:T(8,128)S(1)} %get-tuple-element.43), channel_id=1, source_target_pairs={{128,256},{256,128},{129,257},{257,129},{130,258},{258,130},{131,2... | collective-permute-start | bytes 1474568 | tf_op jit(solution)/shard_map/ppermute | solution.py:606
  12.7 19.9 %collective-permute-start.3 = (f32[96,256]{1,0:T(8,128)S(1)}, f32[96,256]{1,0:T(8,128)S(1)}, u32[]{:S(2)}, u32[]{:S(2)}) collective-permute-start(f32[96,256]{1,0:T(8,128)S(1)} %get-tuple-element.44), channel_id=1, source_target_pairs={{0,384},{1,385},{2,386},{3,387},{4,388},{5,389},{6,390},{7,391},{8... | collective-permute-start | bytes 294920 | tf_op jit(solution)/shard_map/ppermute | solution.py:607
  13.5 8.3 %collective-permute-start.4 = (f32[32,128]{1,0:T(8,128)S(1)}, f32[32,128]{1,0:T(8,128)S(1)}, u32[]{:S(2)}, u32[]{:S(2)}) collective-permute-start(f32[32,128]{1,0:T(8,128)S(1)} %get-tuple-element.48.whi), channel_id=1, source_target_pairs={{0,1},{1,2},{2,3},{3,4},{4,5},{5,6},{6,7},{8,9},{9,10},{10,11},{11... | collective-permute-start | bytes 49160 | tf_op jit(solution)/shard_map/ppermute | solution.py:580
  17.5 8.0 %collective-permute-start.5 = (f32[32,128]{1,0:T(8,128)S(1)}, f32[32,128]{1,0:T(8,128)S(1)}, u32[]{:S(2)}, u32[]{:S(2)}) collective-permute-start(f32[32,128]{1,0:T(8,128)S(1)} %get-tuple-element.49.wlo), channel_id=1, source_target_pairs={{1,0},{2,1},{3,2},{4,3},{5,4},{6,5},{7,6},{9,8},{10,9},{11,10},{12... | collective-permute-start | bytes 49160 | tf_op jit(solution)/shard_map/ppermute | solution.py:580
  25.6 11.1 %collective-permute-start.6 = (f32[40,256]{1,0:T(8,128)S(1)}, f32[40,256]{1,0:T(8,128)S(1)}, u32[]{:S(2)}, u32[]{:S(2)}) collective-permute-start(f32[40,256]{1,0:T(8,128)S(1)} %get-tuple-element.52.vhi), channel_id=1, source_target_pairs={{0,8},{8,16},{16,24},{24,32},{32,40},{40,48},{48,56},{56,64},{64,7... | collective-permute-start | bytes 122888 | tf_op jit(solution)/shard_map/ppermute | solution.py:580
  30.7 7.1 %collective-permute-start.7 = (f32[40,256]{1,0:T(8,128)S(1)}, f32[40,256]{1,0:T(8,128)S(1)}, u32[]{:S(2)}, u32[]{:S(2)}) collective-permute-start(f32[40,256]{1,0:T(8,128)S(1)} %get-tuple-element.53.vlo), channel_id=1, source_target_pairs={{8,0},{16,8},{24,16},{32,24},{40,32},{48,40},{56,48},{64,56},{72,6... | collective-permute-start | bytes 122888 | tf_op jit(solution)/shard_map/ppermute | solution.py:580

commit v6 on v5

--- a/solution.py
+++ b/solution.py
@@ -560,6 +560,13 @@
 SMEM, VMEM, HBM = pltpu.SMEM, pltpu.VMEM, pltpu.HBM
 
 
+COSTS = {
+    "pre": pl.CostEstimate(flops=10**8, transcendentals=0, bytes_accessed=10**8),
+    "pack_x": pl.CostEstimate(flops=10**10, transcendentals=0, bytes_accessed=10**10),
+    "inner": pl.CostEstimate(flops=10**10, transcendentals=0, bytes_accessed=10**10),
+}
+
+
 def call(kernel, name, ins, outs, scratch=(), aliases=None):
     return pl.pallas_call(
         kernel,
@@ -570,6 +577,7 @@
         input_output_aliases=aliases or {},
         compiler_params=pltpu.CompilerParams(vmem_limit_bytes=VMEM_LIMIT),
         name=name,
+        cost_estimate=COSTS.get(name),
     )
 
 

time: 39.4 us -> 36.2 us (0.919)
  waiting for transfers between devices: 6.76 us -> 4.09 us
  starting transfers between devices: 22.6 us -> 22 us
    ppermute x4, waiting for transfers between devices: 4.88 us -> 2.21 us  [pair(): return (lax.ppermute(hi, axis, up), lax.ppermute(lo, axis, down))]
    ppermute x1, starting transfers between devices: 2.83 us -> 2.28 us  [body(): planes_in = lax.ppermute(planes, 'slab', [(1, 2), (2, 1)])]
  transfers between devices with their start and end apart: 8 -> 8, of which waited for: 3 -> 3; matrix products, arithmetic and copies ran while one was open for 0% -> 0% of each run, Pallas kernels for 14% -> 16%
where the time goes in v6:
time: 36.2 us; the launch traced here: 35.9 us
  starting transfers between devices  22 us (61%)
  Pallas kernels  8.99 us (25%)
  waiting for transfers between devices  4.09 us (11%)
  between operations  0.78 us (2%)
    ppermute x4, starting transfers between devices, pair(): return (lax.ppermute(hi, axis, up), lax.ppermute(lo, axis, down))  14.3 us
    pallas_call x1, Pallas kernels, body(): call(inner_kernel, 'inner', [SMEM] + [VMEM] * 13, [vm(2, 4, GR, 128), vm(...  4.06 us
    ppermute x1, starting transfers between devices, body(): edges_in = lax.ppermute(edges, 'slab', [(1, 2), (2, 1)])  2.84 us
    ppermute x1, starting transfers between devices, body(): planes_in = lax.ppermute(planes, 'slab', [(1, 2), (2, 1)])  2.28 us
    ppermute x4, waiting for transfers between devices, pair(): return (lax.ppermute(hi, axis, up), lax.ppermute(lo, axis, down))  2.21 us
    pallas_call x1, Pallas kernels, body(): call(start_kernel, 'start', [SMEM] + [HBM] * 4, [vm(*block), (block, jnp....  2.01 us
    ppermute x1, starting transfers between devices, body(): first_in = lax.ppermute(first, 'slab', [(0, 1), (1, 0), (2, 3), (3, 2)])  1.92 us
    ppermute x1, waiting for transfers between devices, body(): edges_in = lax.ppermute(edges, 'slab', [(1, 2), (2, 1)])  1.87 us
  transfers between devices with their start and end apart: 8, of which 3 were waited for; matrix products, arithmetic and copies ran while one was open for 0% of the time, Pallas kernels for 16%

profile of v6, /device:TPU:238, one launch (start us, length us, event | category | flops | bytes accessed | tf_op | source)
XLA Modules:
  0.0 35.9 jit_solution(11417725103745851738)
XLA Ops:
  0.6 2.0 %start.1 = (f32[8,96,256]{2,1,0:T(8,128)S(1)}, s32[8,96,256]{2,1,0:T(8,128)S(1)}, f32[8,96,256]{2,1,0:T(8,128)S(1)}, f32[8,96,256]{2,1,0:T(8,128)S(1)}, f32[480,...) custom-call(s32[1]{0:T(128)} %bitcast.slab, f32[8,96,256]{2,1,0:T(8,128)} %p_in.1, ...), custom_call_target="tpu_custom_call" | custom-call | tf_op jit(solution)/shard_map/start/pallas_call | solution.py:602
  2.7 1.9 %collective-permute-start = (f32[480,256]{1,0:T(8,128)S(1)}, f32[480,256]{1,0:T(8,128)S(1)}, u32[]{:S(2)}, u32[]{:S(2)}) collective-permute-start(f32[480,256]{1,0:T(8,128)S(1)} %get-tuple-element.39.mine), channel_id=1, source_target_pairs={{0,128},{128,0},{256,384},{384,256},{1,129},{129,1},{257,385},{385... | collective-permute-start | bytes 1474568 | tf_op jit(solution)/shard_map/ppermute | solution.py:608
  4.6 2.8 %collective-permute-start.1 = (f32[40,256]{1,0:T(8,128)S(1)}, f32[40,256]{1,0:T(8,128)S(1)}, u32[]{:S(2)}, u32[]{:S(2)}) collective-permute-start(f32[40,256]{1,0:T(8,128)S(1)} %get-tuple-element.42), channel_id=1, source_target_pairs={{128,256},{256,128},{129,257},{257,129},{130,258},{258,130},{131,2... | collective-permute-start | bytes 122888 | tf_op jit(solution)/shard_map/ppermute | solution.py:607
  7.4 0.0 collective-permute-done.first
  7.4 0.6 %pack_own.1 = (f32[480,256]{1,0:T(8,128)S(1)}, f32[96,256]{1,0:T(8,128)S(1)}, f32[32,128]{1,0:T(8,128)S(1)}, f32[32,128]{1,0:T(8,128)S(1)}) custom-call(s32[1]{0:T(128)} %bitcast.slab, f32[8,96,256]{2,1,0:T(8,128)S(1)} %get-tuple-element.35.h, f32[8,96,256]{2,1,0:T(8,128)S(1)} %get-tuple-element.36.p, f32[480,256]{1,0:T(8,128)S(1)} %get-tuple-element.39.mine, ...), custom_call_target="tpu_custom_call" | custom-call | tf_op jit(solution)/shard_map/pack_own/pallas_call | solution.py:609
  8.0 1.9 %collective-permute-done.1.edges = f32[40,256]{1,0:T(8,128)S(1)} collective-permute-done((f32[40,256]{1,0:T(8,128)S(1)}, f32[40,256]{1,0:T(8,128)S(1)}, u32[]{:S(2)}, u32[]{:S(2)}) %collective-permute-start.1) | collective-permute-done | bytes 40992 | tf_op jit(solution)/shard_map/ppermute | solution.py:607
  9.9 0.1 pack_y.1
  10.0 4.3 %collective-permute-start.4 = (f32[32,128]{1,0:T(8,128)S(1)}, f32[32,128]{1,0:T(8,128)S(1)}, u32[]{:S(2)}, u32[]{:S(2)}) collective-permute-start(f32[32,128]{1,0:T(8,128)S(1)} %get-tuple-element.48.whi), channel_id=1, source_target_pairs={{0,1},{1,2},{2,3},{3,4},{4,5},{5,6},{6,7},{8,9},{9,10},{10,11},{11... | collective-permute-start | bytes 49160 | tf_op jit(solution)/shard_map/ppermute | solution.py:588
  14.3 3.0 %collective-permute-start.5 = (f32[32,128]{1,0:T(8,128)S(1)}, f32[32,128]{1,0:T(8,128)S(1)}, u32[]{:S(2)}, u32[]{:S(2)}) collective-permute-start(f32[32,128]{1,0:T(8,128)S(1)} %get-tuple-element.49.wlo), channel_id=1, source_target_pairs={{1,0},{2,1},{3,2},{4,3},{5,4},{6,5},{7,6},{9,8},{10,9},{11,10},{12... | collective-permute-start | bytes 49160 | tf_op jit(solution)/shard_map/ppermute | solution.py:588
  17.3 0.7 %collective-permute-start.3 = (f32[96,256]{1,0:T(8,128)S(1)}, f32[96,256]{1,0:T(8,128)S(1)}, u32[]{:S(2)}, u32[]{:S(2)}) collective-permute-start(f32[96,256]{1,0:T(8,128)S(1)} %get-tuple-element.44), channel_id=1, source_target_pairs={{0,384},{1,385},{2,386},{3,387},{4,388},{5,389},{6,390},{7,391},{8... | collective-permute-start | bytes 294920 | tf_op jit(solution)/shard_map/ppermute | solution.py:615
  18.0 2.3 %collective-permute-start.2 = (f32[480,256]{1,0:T(8,128)S(1)}, f32[480,256]{1,0:T(8,128)S(1)}, u32[]{:S(2)}, u32[]{:S(2)}) collective-permute-start(f32[480,256]{1,0:T(8,128)S(1)} %get-tuple-element.43), channel_id=1, source_target_pairs={{128,256},{256,128},{129,257},{257,129},{130,258},{258,130},{131,2... | collective-permute-start | bytes 1474568 | tf_op jit(solution)/shard_map/ppermute | solution.py:614
  20.3 0.9 %pre.1.w = f32[5,9,96,256]{3,2,1,0:T(8,128)S(1)} custom-call(f32[8,96,256]{2,1,0:T(8,128)S(1)} %get-tuple-element.35.h, f32[8,96,256]{2,1,0:T(8,128)S(1)} %get-tuple-element.36.p, f32[32,128]{1,0:T(8,128)S(1)} %get-tuple-element.49.wlo), custom_call_target="tpu_custom_call" | custom-call | flops 100000000 | bytes 100000000 | tf_op jit(solution)/shard_map/pre/pallas_call | solution.py:618
  21.2 0.0 collective-permute-done.4.ylo
  21.2 1.1 %collective-permute-done.5.yhi = f32[32,128]{1,0:T(8,128)S(1)} collective-permute-done((f32[32,128]{1,0:T(8,128)S(1)}, f32[32,128]{1,0:T(8,128)S(1)}, u32[]{:S(2)}, u32[]{:S(2)}) %collective-permute-start.5) | collective-permute-done | bytes 16416 | tf_op jit(solution)/shard_map/ppermute | solution.py:588
  22.4 5.0 %collective-permute-start.6 = (f32[40,256]{1,0:T(8,128)S(1)}, f32[40,256]{1,0:T(8,128)S(1)}, u32[]{:S(2)}, u32[]{:S(2)}) collective-permute-start(f32[40,256]{1,0:T(8,128)S(1)} %get-tuple-element.52.vhi), channel_id=1, source_target_pairs={{0,8},{8,16},{16,24},{24,32},{32,40},{40,48},{48,56},{56,64},{64,7... | collective-permute-start | bytes 122888 | tf_op jit(solution)/shard_map/ppermute | solution.py:588
  27.4 1.9 %collective-permute-start.7 = (f32[40,256]{1,0:T(8,128)S(1)}, f32[40,256]{1,0:T(8,128)S(1)}, u32[]{:S(2)}, u32[]{:S(2)}) collective-permute-start(f32[40,256]{1,0:T(8,128)S(1)} %get-tuple-element.53.vlo), channel_id=1, source_target_pairs={{8,0},{16,8},{24,16},{32,24},{40,32},{48,40},{56,48},{64,56},{72,6... | collective-permute-start | bytes 122888 | tf_op jit(solution)/shard_map/ppermute | solution.py:588
  29.4 0.0 collective-permute-done.3.both
  29.4 0.0 collective-permute-done.2.planes
  29.4 4.1 %inner.1 = (f32[2,4,32,128]{3,2,1,0:T(8,128)S(1)}, f32[2,8,96,256]{3,2,1,0:T(8,128)S(1)}, f32[2,96,256]{2,1,0:T(8,128)S(1)}, f32[10,96,256]{2,1,0:T(8,128)S(1)},...) custom-call(s32[1]{0:T(128)} %bitcast.slab, ...), custom_call_target="tpu_custom_call" | custom-call | flops 10000000000 | bytes 10000000000 | tf_op jit(solution)/shard_map/inner/pallas_call | solution.py:626
  33.5 0.0 collective-permute-done.6.xlo
  33.5 1.1 %collective-permute-done.7.xhi = f32[40,256]{1,0:T(8,128)S(1)} collective-permute-done((f32[40,256]{1,0:T(8,128)S(1)}, f32[40,256]{1,0:T(8,128)S(1)}, u32[]{:S(2)}, u32[]{:S(2)}) %collective-permute-start.7) | collective-permute-done | bytes 40992 | tf_op jit(solution)/shard_map/ppermute | solution.py:588
  34.5 1.3 %outer.1 = (f32[8,96,256]{2,1,0:T(8,128)}, f32[8,96,256]{2,1,0:T(8,128)}, f32[8,96,256]{2,1,0:T(8,128)}) custom-call(s32[1]{0:T(128)} %bitcast.slab, f32[8,256]{1,0:T(8,128)S(1)} %get-tuple-element.34.shade, f32[8,96,256]{2,1,0:T(8,128)S(1)} %get-tuple-element.35.h, ...), custom_call_target="tpu_custom_call", output_to_operand_aliasing={{0}: (21, {}), {1}: (22, {}), {2}: (23, {})} | custom-call | tf_op jit(solution)/shard_map/outer/pallas_call | solution.py:632
  (1 shorter events, 0.0 us)
Async XLA Ops:
  2.7 4.8 %collective-permute-start = (f32[480,256]{1,0:T(8,128)S(1)}, f32[480,256]{1,0:T(8,128)S(1)}, u32[]{:S(2)}, u32[]{:S(2)}) collective-permute-start(f32[480,256]{1,0:T(8,128)S(1)} %get-tuple-element.39.mine), channel_id=1, source_target_pairs={{0,128},{128,0},{256,384},{384,256},{1,129},{129,1},{257,385},{385... | collective-permute-start | bytes 1474568 | tf_op jit(solution)/shard_map/ppermute | solution.py:608
  4.6 5.3 %collective-permute-start.1 = (f32[40,256]{1,0:T(8,128)S(1)}, f32[40,256]{1,0:T(8,128)S(1)}, u32[]{:S(2)}, u32[]{:S(2)}) collective-permute-start(f32[40,256]{1,0:T(8,128)S(1)} %get-tuple-element.42), channel_id=1, source_target_pairs={{128,256},{256,128},{129,257},{257,129},{130,258},{258,130},{131,2... | collective-permute-start | bytes 122888 | tf_op jit(solution)/shard_map/ppermute | solution.py:607
  10.0 11.2 %collective-permute-start.4 = (f32[32,128]{1,0:T(8,128)S(1)}, f32[32,128]{1,0:T(8,128)S(1)}, u32[]{:S(2)}, u32[]{:S(2)}) collective-permute-start(f32[32,128]{1,0:T(8,128)S(1)} %get-tuple-element.48.whi), channel_id=1, source_target_pairs={{0,1},{1,2},{2,3},{3,4},{4,5},{5,6},{6,7},{8,9},{9,10},{10,11},{11... | collective-permute-start | bytes 49160 | tf_op jit(solution)/shard_map/ppermute | solution.py:588
  14.3 8.0 %collective-permute-start.5 = (f32[32,128]{1,0:T(8,128)S(1)}, f32[32,128]{1,0:T(8,128)S(1)}, u32[]{:S(2)}, u32[]{:S(2)}) collective-permute-start(f32[32,128]{1,0:T(8,128)S(1)} %get-tuple-element.49.wlo), channel_id=1, source_target_pairs={{1,0},{2,1},{3,2},{4,3},{5,4},{6,5},{7,6},{9,8},{10,9},{11,10},{12... | collective-permute-start | bytes 49160 | tf_op jit(solution)/shard_map/ppermute | solution.py:588
  17.3 12.0 %collective-permute-start.3 = (f32[96,256]{1,0:T(8,128)S(1)}, f32[96,256]{1,0:T(8,128)S(1)}, u32[]{:S(2)}, u32[]{:S(2)}) collective-permute-start(f32[96,256]{1,0:T(8,128)S(1)} %get-tuple-element.44), channel_id=1, source_target_pairs={{0,384},{1,385},{2,386},{3,387},{4,388},{5,389},{6,390},{7,391},{8... | collective-permute-start | bytes 294920 | tf_op jit(solution)/shard_map/ppermute | solution.py:615
  18.0 11.4 %collective-permute-start.2 = (f32[480,256]{1,0:T(8,128)S(1)}, f32[480,256]{1,0:T(8,128)S(1)}, u32[]{:S(2)}, u32[]{:S(2)}) collective-permute-start(f32[480,256]{1,0:T(8,128)S(1)} %get-tuple-element.43), channel_id=1, source_target_pairs={{128,256},{256,128},{129,257},{257,129},{130,258},{258,130},{131,2... | collective-permute-start | bytes 1474568 | tf_op jit(solution)/shard_map/ppermute | solution.py:614
  22.4 11.1 %collective-permute-start.6 = (f32[40,256]{1,0:T(8,128)S(1)}, f32[40,256]{1,0:T(8,128)S(1)}, u32[]{:S(2)}, u32[]{:S(2)}) collective-permute-start(f32[40,256]{1,0:T(8,128)S(1)} %get-tuple-element.52.vhi), channel_id=1, source_target_pairs={{0,8},{8,16},{16,24},{24,32},{32,40},{40,48},{48,56},{56,64},{64,7... | collective-permute-start | bytes 122888 | tf_op jit(solution)/shard_map/ppermute | solution.py:588
  27.4 7.1 %collective-permute-start.7 = (f32[40,256]{1,0:T(8,128)S(1)}, f32[40,256]{1,0:T(8,128)S(1)}, u32[]{:S(2)}, u32[]{:S(2)}) collective-permute-start(f32[40,256]{1,0:T(8,128)S(1)} %get-tuple-element.53.vlo), channel_id=1, source_target_pairs={{8,0},{16,8},{24,16},{32,24},{40,32},{48,40},{56,48},{64,56},{72,6... | collective-permute-start | bytes 122888 | tf_op jit(solution)/shard_map/ppermute | solution.py:588

commit v7 on v6

--- a/solution.py
+++ b/solution.py
@@ -348,7 +348,7 @@
     return hval, pval
 
 
-def pre_kernel(h, p, wlo, w):
+def pre_kernel(h, p, w):
     def chunk(i, carry):
         rows = at8(i)
         hval, pval = triples(h, p, None, None, i)
@@ -613,10 +613,10 @@
     planes, both, edges_in = lax.optimization_barrier((planes, both, edges_in))
     planes_in = lax.ppermute(planes, "slab", [(1, 2), (2, 1)])
     both_in = lax.ppermute(both, "slab", [(0, 3)])
+    (w,) = call(pre_kernel, "pre", [VMEM] * 2, [vm(5, L + 1, R, C)])(h, p)
+    edges_in, w = lax.optimization_barrier((edges_in, w))
     wlo, whi = call(pack_y_kernel, "pack_y", [SMEM] + [VMEM] * 3, [vm(GR, 128)] * 2)(slab, edges_in, *own_y)
     ylo, yhi = pair("mapy", wlo, whi)
-    (w,) = call(pre_kernel, "pre", [VMEM] * 3, [vm(5, L + 1, R, C)])(h, p, wlo)
-    ylo, yhi, w = lax.optimization_barrier((ylo, yhi, w))
     vlo, vhi = call(pack_x_kernel, "pack_x", [SMEM] + [VMEM] * 6, [vm(40, C)] * 2)(
         slab, h, p, first_in, edges_in, ylo, yhi
     )

time: 36.2 us -> 36.2 us (level)
    ppermute x4, waiting for transfers between devices: 2.21 us -> 3.14 us  [pair(): return (lax.ppermute(hi, axis, up), lax.ppermute(lo, axis, down))]
    ppermute x1, waiting for transfers between devices: 1.87 us -> 0.96 us  [body(): edges_in = lax.ppermute(edges, 'slab', [(1, 2), (2, 1)])]
where the time goes in v7:
time: 36.2 us; the launch traced here: 35.9 us
  starting transfers between devices  22 us (61%)
  Pallas kernels  8.97 us (25%)
  waiting for transfers between devices  4.11 us (11%)
  between operations  0.78 us (2%)
    ppermute x4, starting transfers between devices, pair(): return (lax.ppermute(hi, axis, up), lax.ppermute(lo, axis, down))  14.3 us
    pallas_call x1, Pallas kernels, body(): call(inner_kernel, 'inner', [SMEM] + [VMEM] * 13, [vm(2, 4, GR, 128), vm(...  4.04 us
    ppermute x4, waiting for transfers between devices, pair(): return (lax.ppermute(hi, axis, up), lax.ppermute(lo, axis, down))  3.14 us
    ppermute x1, starting transfers between devices, body(): edges_in = lax.ppermute(edges, 'slab', [(1, 2), (2, 1)])  2.84 us
    ppermute x1, starting transfers between devices, body(): planes_in = lax.ppermute(planes, 'slab', [(1, 2), (2, 1)])  2.28 us
    pallas_call x1, Pallas kernels, body(): call(start_kernel, 'start', [SMEM] + [HBM] * 4, [vm(*block), (block, jnp....  2.01 us
    ppermute x1, starting transfers between devices, body(): first_in = lax.ppermute(first, 'slab', [(0, 1), (1, 0), (2, 3), (3, 2)])  1.92 us
    pallas_call x1, Pallas kernels, body(): call(outer_kernel, 'outer', [SMEM] + [VMEM] * 20 + [HBM] * 3, [hbm] * 3,...  1.31 us
  transfers between devices with their start and end apart: 8, of which 3 were waited for; matrix products, arithmetic and copies ran while one was open for 0% of the time, Pallas kernels for 16%

profile of v7, /device:TPU:238, one launch (start us, length us, event | category | flops | bytes accessed | tf_op | source)
XLA Modules:
  0.0 35.9 jit_solution(13469827952633950508)
XLA Ops:
  0.6 2.0 %start.1 = (f32[8,96,256]{2,1,0:T(8,128)S(1)}, s32[8,96,256]{2,1,0:T(8,128)S(1)}, f32[8,96,256]{2,1,0:T(8,128)S(1)}, f32[8,96,256]{2,1,0:T(8,128)S(1)}, f32[480,...) custom-call(s32[1]{0:T(128)} %bitcast.slab, f32[8,96,256]{2,1,0:T(8,128)} %p_in.1, ...), custom_call_target="tpu_custom_call" | custom-call | tf_op jit(solution)/shard_map/start/pallas_call | solution.py:602
  2.7 1.9 %collective-permute-start = (f32[480,256]{1,0:T(8,128)S(1)}, f32[480,256]{1,0:T(8,128)S(1)}, u32[]{:S(2)}, u32[]{:S(2)}) collective-permute-start(f32[480,256]{1,0:T(8,128)S(1)} %get-tuple-element.38.mine), channel_id=1, source_target_pairs={{0,128},{128,0},{256,384},{384,256},{1,129},{129,1},{257,385},{385... | collective-permute-start | bytes 1474568 | tf_op jit(solution)/shard_map/ppermute | solution.py:608
  4.6 2.8 %collective-permute-start.1 = (f32[40,256]{1,0:T(8,128)S(1)}, f32[40,256]{1,0:T(8,128)S(1)}, u32[]{:S(2)}, u32[]{:S(2)}) collective-permute-start(f32[40,256]{1,0:T(8,128)S(1)} %get-tuple-element.41), channel_id=1, source_target_pairs={{128,256},{256,128},{129,257},{257,129},{130,258},{258,130},{131,2... | collective-permute-start | bytes 122888 | tf_op jit(solution)/shard_map/ppermute | solution.py:607
  7.4 0.9 %pre.1.w = f32[5,9,96,256]{3,2,1,0:T(8,128)S(1)} custom-call(f32[8,96,256]{2,1,0:T(8,128)S(1)} %get-tuple-element.34.h, f32[8,96,256]{2,1,0:T(8,128)S(1)} %get-tuple-element.35.p), custom_call_target="tpu_custom_call" | custom-call | flops 100000000 | bytes 100000000 | tf_op jit(solution)/shard_map/pre/pallas_call | solution.py:616
  8.3 0.0 collective-permute-done.first
  8.3 0.6 %pack_own.1 = (f32[480,256]{1,0:T(8,128)S(1)}, f32[96,256]{1,0:T(8,128)S(1)}, f32[32,128]{1,0:T(8,128)S(1)}, f32[32,128]{1,0:T(8,128)S(1)}) custom-call(s32[1]{0:T(128)} %bitcast.slab, f32[8,96,256]{2,1,0:T(8,128)S(1)} %get-tuple-element.34.h, f32[8,96,256]{2,1,0:T(8,128)S(1)} %get-tuple-element.35.p, f32[480,256]{1,0:T(8,128)S(1)} %get-tuple-element.38.mine, ...), custom_call_target="tpu_custom_call" | custom-call | tf_op jit(solution)/shard_map/pack_own/pallas_call | solution.py:609
  8.9 1.0 %collective-permute-done.1.edges = f32[40,256]{1,0:T(8,128)S(1)} collective-permute-done((f32[40,256]{1,0:T(8,128)S(1)}, f32[40,256]{1,0:T(8,128)S(1)}, u32[]{:S(2)}, u32[]{:S(2)}) %collective-permute-start.1) | collective-permute-done | bytes 40992 | tf_op jit(solution)/shard_map/ppermute | solution.py:607
  9.9 0.1 pack_y.1
  10.0 4.3 %collective-permute-start.4 = (f32[32,128]{1,0:T(8,128)S(1)}, f32[32,128]{1,0:T(8,128)S(1)}, u32[]{:S(2)}, u32[]{:S(2)}) collective-permute-start(f32[32,128]{1,0:T(8,128)S(1)} %get-tuple-element.48.whi), channel_id=1, source_target_pairs={{0,1},{1,2},{2,3},{3,4},{4,5},{5,6},{6,7},{8,9},{9,10},{10,11},{11... | collective-permute-start | bytes 49160 | tf_op jit(solution)/shard_map/ppermute | solution.py:588
  14.3 3.0 %collective-permute-start.5 = (f32[32,128]{1,0:T(8,128)S(1)}, f32[32,128]{1,0:T(8,128)S(1)}, u32[]{:S(2)}, u32[]{:S(2)}) collective-permute-start(f32[32,128]{1,0:T(8,128)S(1)} %get-tuple-element.49.wlo), channel_id=1, source_target_pairs={{1,0},{2,1},{3,2},{4,3},{5,4},{6,5},{7,6},{9,8},{10,9},{11,10},{12... | collective-permute-start | bytes 49160 | tf_op jit(solution)/shard_map/ppermute | solution.py:588
  17.3 0.7 %collective-permute-start.3 = (f32[96,256]{1,0:T(8,128)S(1)}, f32[96,256]{1,0:T(8,128)S(1)}, u32[]{:S(2)}, u32[]{:S(2)}) collective-permute-start(f32[96,256]{1,0:T(8,128)S(1)} %get-tuple-element.43), channel_id=1, source_target_pairs={{0,384},{1,385},{2,386},{3,387},{4,388},{5,389},{6,390},{7,391},{8... | collective-permute-start | bytes 294920 | tf_op jit(solution)/shard_map/ppermute | solution.py:615
  18.0 2.3 %collective-permute-start.2 = (f32[480,256]{1,0:T(8,128)S(1)}, f32[480,256]{1,0:T(8,128)S(1)}, u32[]{:S(2)}, u32[]{:S(2)}) collective-permute-start(f32[480,256]{1,0:T(8,128)S(1)} %get-tuple-element.42), channel_id=1, source_target_pairs={{128,256},{256,128},{129,257},{257,129},{130,258},{258,130},{131,2... | collective-permute-start | bytes 1474568 | tf_op jit(solution)/shard_map/ppermute | solution.py:614
  20.3 0.0 collective-permute-done.4.ylo
  20.3 2.0 %collective-permute-done.5.yhi = f32[32,128]{1,0:T(8,128)S(1)} collective-permute-done((f32[32,128]{1,0:T(8,128)S(1)}, f32[32,128]{1,0:T(8,128)S(1)}, u32[]{:S(2)}, u32[]{:S(2)}) %collective-permute-start.5) | collective-permute-done | bytes 16416 | tf_op jit(solution)/shard_map/ppermute | solution.py:588
  22.4 5.0 %collective-permute-start.6 = (f32[40,256]{1,0:T(8,128)S(1)}, f32[40,256]{1,0:T(8,128)S(1)}, u32[]{:S(2)}, u32[]{:S(2)}) collective-permute-start(f32[40,256]{1,0:T(8,128)S(1)} %get-tuple-element.50.vhi), channel_id=1, source_target_pairs={{0,8},{8,16},{16,24},{24,32},{32,40},{40,48},{48,56},{56,64},{64,7... | collective-permute-start | bytes 122888 | tf_op jit(solution)/shard_map/ppermute | solution.py:588
  27.4 1.9 %collective-permute-start.7 = (f32[40,256]{1,0:T(8,128)S(1)}, f32[40,256]{1,0:T(8,128)S(1)}, u32[]{:S(2)}, u32[]{:S(2)}) collective-permute-start(f32[40,256]{1,0:T(8,128)S(1)} %get-tuple-element.51.vlo), channel_id=1, source_target_pairs={{8,0},{16,8},{24,16},{32,24},{40,32},{48,40},{56,48},{64,56},{72,6... | collective-permute-start | bytes 122888 | tf_op jit(solution)/shard_map/ppermute | solution.py:588
  29.4 0.0 collective-permute-done.3.both
  29.4 0.0 collective-permute-done.2.planes
  29.4 4.0 %inner.1 = (f32[2,4,32,128]{3,2,1,0:T(8,128)S(1)}, f32[2,8,96,256]{3,2,1,0:T(8,128)S(1)}, f32[2,96,256]{2,1,0:T(8,128)S(1)}, f32[10,96,256]{2,1,0:T(8,128)S(1)},...) custom-call(s32[1]{0:T(128)} %bitcast.slab, ...), custom_call_target="tpu_custom_call" | custom-call | flops 10000000000 | bytes 10000000000 | tf_op jit(solution)/shard_map/inner/pallas_call | solution.py:626
  33.4 0.0 collective-permute-done.6.xlo
  33.4 1.1 %collective-permute-done.7.xhi = f32[40,256]{1,0:T(8,128)S(1)} collective-permute-done((f32[40,256]{1,0:T(8,128)S(1)}, f32[40,256]{1,0:T(8,128)S(1)}, u32[]{:S(2)}, u32[]{:S(2)}) %collective-permute-start.7) | collective-permute-done | bytes 40992 | tf_op jit(solution)/shard_map/ppermute | solution.py:588
  34.5 1.3 %outer.1 = (f32[8,96,256]{2,1,0:T(8,128)}, f32[8,96,256]{2,1,0:T(8,128)}, f32[8,96,256]{2,1,0:T(8,128)}) custom-call(s32[1]{0:T(128)} %bitcast.slab, f32[8,256]{1,0:T(8,128)S(1)} %get-tuple-element.33.shade, f32[8,96,256]{2,1,0:T(8,128)S(1)} %get-tuple-element.34.h, ...), custom_call_target="tpu_custom_call", output_to_operand_aliasing={{0}: (21, {}), {1}: (22, {}), {2}: (23, {})} | custom-call | tf_op jit(solution)/shard_map/outer/pallas_call | solution.py:632
  (1 shorter events, 0.0 us)
Async XLA Ops:
  2.7 5.7 %collective-permute-start = (f32[480,256]{1,0:T(8,128)S(1)}, f32[480,256]{1,0:T(8,128)S(1)}, u32[]{:S(2)}, u32[]{:S(2)}) collective-permute-start(f32[480,256]{1,0:T(8,128)S(1)} %get-tuple-element.38.mine), channel_id=1, source_target_pairs={{0,128},{128,0},{256,384},{384,256},{1,129},{129,1},{257,385},{385... | collective-permute-start | bytes 1474568 | tf_op jit(solution)/shard_map/ppermute | solution.py:608
  4.6 5.3 %collective-permute-start.1 = (f32[40,256]{1,0:T(8,128)S(1)}, f32[40,256]{1,0:T(8,128)S(1)}, u32[]{:S(2)}, u32[]{:S(2)}) collective-permute-start(f32[40,256]{1,0:T(8,128)S(1)} %get-tuple-element.41), channel_id=1, source_target_pairs={{128,256},{256,128},{129,257},{257,129},{130,258},{258,130},{131,2... | collective-permute-start | bytes 122888 | tf_op jit(solution)/shard_map/ppermute | solution.py:607
  10.0 10.3 %collective-permute-start.4 = (f32[32,128]{1,0:T(8,128)S(1)}, f32[32,128]{1,0:T(8,128)S(1)}, u32[]{:S(2)}, u32[]{:S(2)}) collective-permute-start(f32[32,128]{1,0:T(8,128)S(1)} %get-tuple-element.48.whi), channel_id=1, source_target_pairs={{0,1},{1,2},{2,3},{3,4},{4,5},{5,6},{6,7},{8,9},{9,10},{10,11},{11... | collective-permute-start | bytes 49160 | tf_op jit(solution)/shard_map/ppermute | solution.py:588
  14.3 8.0 %collective-permute-start.5 = (f32[32,128]{1,0:T(8,128)S(1)}, f32[32,128]{1,0:T(8,128)S(1)}, u32[]{:S(2)}, u32[]{:S(2)}) collective-permute-start(f32[32,128]{1,0:T(8,128)S(1)} %get-tuple-element.49.wlo), channel_id=1, source_target_pairs={{1,0},{2,1},{3,2},{4,3},{5,4},{6,5},{7,6},{9,8},{10,9},{11,10},{12... | collective-permute-start | bytes 49160 | tf_op jit(solution)/shard_map/ppermute | solution.py:588
  17.3 12.0 %collective-permute-start.3 = (f32[96,256]{1,0:T(8,128)S(1)}, f32[96,256]{1,0:T(8,128)S(1)}, u32[]{:S(2)}, u32[]{:S(2)}) collective-permute-start(f32[96,256]{1,0:T(8,128)S(1)} %get-tuple-element.43), channel_id=1, source_target_pairs={{0,384},{1,385},{2,386},{3,387},{4,388},{5,389},{6,390},{7,391},{8... | collective-permute-start | bytes 294920 | tf_op jit(solution)/shard_map/ppermute | solution.py:615
  18.0 11.4 %collective-permute-start.2 = (f32[480,256]{1,0:T(8,128)S(1)}, f32[480,256]{1,0:T(8,128)S(1)}, u32[]{:S(2)}, u32[]{:S(2)}) collective-permute-start(f32[480,256]{1,0:T(8,128)S(1)} %get-tuple-element.42), channel_id=1, source_target_pairs={{128,256},{256,128},{129,257},{257,129},{130,258},{258,130},{131,2... | collective-permute-start | bytes 1474568 | tf_op jit(solution)/shard_map/ppermute | solution.py:614
  22.4 11.0 %collective-permute-start.6 = (f32[40,256]{1,0:T(8,128)S(1)}, f32[40,256]{1,0:T(8,128)S(1)}, u32[]{:S(2)}, u32[]{:S(2)}) collective-permute-start(f32[40,256]{1,0:T(8,128)S(1)} %get-tuple-element.50.vhi), channel_id=1, source_target_pairs={{0,8},{8,16},{16,24},{24,32},{32,40},{40,48},{48,56},{56,64},{64,7... | collective-permute-start | bytes 122888 | tf_op jit(solution)/shard_map/ppermute | solution.py:588
  27.4 7.1 %collective-permute-start.7 = (f32[40,256]{1,0:T(8,128)S(1)}, f32[40,256]{1,0:T(8,128)S(1)}, u32[]{:S(2)}, u32[]{:S(2)}) collective-permute-start(f32[40,256]{1,0:T(8,128)S(1)} %get-tuple-element.51.vlo), channel_id=1, source_target_pairs={{8,0},{16,8},{24,16},{32,24},{40,32},{48,40},{56,48},{64,56},{72,6... | collective-permute-start | bytes 122888 | tf_op jit(solution)/shard_map/ppermute | solution.py:588

commit v8 on v6

--- a/solution.py
+++ b/solution.py
@@ -152,7 +152,6 @@
     planes[R : 2 * R, :] = p[o]
     planes[2 * R : 3 * R, :] = h[i]
     planes[3 * R : 4 * R, :] = p[i]
-    planes[4 * R : 5 * R, :] = total
     both[...] = total
 
 
@@ -317,10 +316,9 @@
         qc, flow = qn, flow2
 
 
-def above_rows(slab, first, planes, both, rows):
+def above_rows(slab, first, both, rows):
     base = jnp.where((slab[0] & 1) == 1, first[rows(4 * R), :], 0.0)
-    base = base + jnp.where(slab[0] == 2, planes[rows(4 * R), :], 0.0)
-    return base + jnp.where(slab[0] == 3, both[rows(0), :], 0.0)
+    return base + jnp.where(slab[0] >= 2, both[rows(0), :], 0.0)
 
 
 def at8(i):
@@ -465,7 +463,7 @@
             lambda z: eq[z, rows, :],
             lambda z, k: iv[z + 1, rows, :] if k == 5 else weight_of(w, wy, wz, z, k, rows),
             lambda z: p[z, rows, :],
-            above_rows(slab, first, planes, both, lambda top: pl.ds(pl.multiple_of(top + 8 * i, 8), 8)),
+            above_rows(slab, first, both, lambda top: pl.ds(pl.multiple_of(top + 8 * i, 8), 8)),
             lambda z: over[z, rows, :],
             lambda z: lith[z, rows, :],
             shade, put,
@@ -544,7 +542,7 @@
             lambda z: edge_columns(columns[part], z, g),
             weight,
             lambda z: p[z, rows, :],
-            above_rows(slab, first, planes, both, lambda t: slice(t + top, t + top + 8)),
+            above_rows(slab, first, both, lambda t: slice(t + top, t + top + 8)),
             lambda z: over[z, rows, :],
             lambda z: lith[z, rows, :],
             shade, put,
@@ -608,11 +606,11 @@
     first_in = lax.ppermute(first, "slab", [(0, 1), (1, 0), (2, 3), (3, 2)])
     planes, both, *own_y = call(
         pack_own_kernel, "pack_own", [SMEM] + [VMEM] * 4,
-        [vm(5 * R, C), vm(R, C), vm(GR, 128), vm(GR, 128)],
+        [vm(4 * R, C), vm(R, C), vm(GR, 128), vm(GR, 128)],
     )(slab, h, p, first, first_in)
     planes, both, edges_in = lax.optimization_barrier((planes, both, edges_in))
     planes_in = lax.ppermute(planes, "slab", [(1, 2), (2, 1)])
-    both_in = lax.ppermute(both, "slab", [(0, 3)])
+    both_in = lax.ppermute(both, "slab", [(1, 2), (0, 3)])
     wlo, whi = call(pack_y_kernel, "pack_y", [SMEM] + [VMEM] * 3, [vm(GR, 128)] * 2)(slab, edges_in, *own_y)
     ylo, yhi = pair("mapy", wlo, whi)
     (w,) = call(pre_kernel, "pre", [VMEM] * 3, [vm(5, L + 1, R, C)])(h, p, wlo)

time: 36.2 us -> 38.6 us (1.066)
  the two profiles are of different devices: /device:TPU:238 before, /device:TPU:242 now
where the time goes in v8:
time: 38.6 us; the launch traced here: 38.3 us
  starting transfers between devices  25.2 us (65%)
  Pallas kernels  9 us (23%)
  waiting for transfers between devices  3.25 us (8%)
  between operations  0.79 us (2%)
    ppermute x4, starting transfers between devices, pair(): return (lax.ppermute(hi, axis, up), lax.ppermute(lo, axis, down))  15.2 us
    ppermute x1, starting transfers between devices, body(): planes_in = lax.ppermute(planes, 'slab', [(1, 2), (2, 1)])  4.27 us
    pallas_call x1, Pallas kernels, body(): call(inner_kernel, 'inner', [SMEM] + [VMEM] * 13, [vm(2, 4, GR, 128), vm(...  4.06 us
    ppermute x1, starting transfers between devices, body(): edges_in = lax.ppermute(edges, 'slab', [(1, 2), (2, 1)])  2.55 us
    ppermute x1, waiting for transfers between devices, body(): edges_in = lax.ppermute(edges, 'slab', [(1, 2), (2, 1)])  2.16 us
    pallas_call x1, Pallas kernels, body(): call(start_kernel, 'start', [SMEM] + [HBM] * 4, [vm(*block), (block, jnp....  2.01 us
    ppermute x1, starting transfers between devices, body(): first_in = lax.ppermute(first, 'slab', [(0, 1), (1, 0), (2, 3), (3, 2)])  1.92 us
    pallas_call x1, Pallas kernels, body(): call(outer_kernel, 'outer', [SMEM] + [VMEM] * 20 + [HBM] * 3, [hbm] * 3,...  1.31 us
  transfers between devices with their start and end apart: 8, of which 2 were waited for; matrix products, arithmetic and copies ran while one was open for 0% of the time, Pallas kernels for 15%

profile of v8, /device:TPU:242, one launch (start us, length us, event | category | flops | bytes accessed | tf_op | source)
XLA Modules:
  0.0 38.3 jit_solution(18197189026593964658)
XLA Ops:
  0.6 2.0 %start.1 = (f32[8,96,256]{2,1,0:T(8,128)S(1)}, s32[8,96,256]{2,1,0:T(8,128)S(1)}, f32[8,96,256]{2,1,0:T(8,128)S(1)}, f32[8,96,256]{2,1,0:T(8,128)S(1)}, f32[480,...) custom-call(s32[1]{0:T(128)} %bitcast.slab, f32[8,96,256]{2,1,0:T(8,128)} %p_in.1, ...), custom_call_target="tpu_custom_call" | custom-call | tf_op jit(solution)/shard_map/start/pallas_call | solution.py:600
  2.7 1.9 %collective-permute-start = (f32[480,256]{1,0:T(8,128)S(1)}, f32[480,256]{1,0:T(8,128)S(1)}, u32[]{:S(2)}, u32[]{:S(2)}) collective-permute-start(f32[480,256]{1,0:T(8,128)S(1)} %get-tuple-element.39.mine), channel_id=1, source_target_pairs={{0,128},{128,0},{256,384},{384,256},{1,129},{129,1},{257,385},{385... | collective-permute-start | bytes 1474568 | tf_op jit(solution)/shard_map/ppermute | solution.py:606
  4.6 2.5 %collective-permute-start.1 = (f32[40,256]{1,0:T(8,128)S(1)}, f32[40,256]{1,0:T(8,128)S(1)}, u32[]{:S(2)}, u32[]{:S(2)}) collective-permute-start(f32[40,256]{1,0:T(8,128)S(1)} %get-tuple-element.42), channel_id=1, source_target_pairs={{128,256},{256,128},{129,257},{257,129},{130,258},{258,130},{131,2... | collective-permute-start | bytes 122888 | tf_op jit(solution)/shard_map/ppermute | solution.py:605
  7.1 0.0 collective-permute-done.first
  7.1 0.6 %pack_own.1 = (f32[384,256]{1,0:T(8,128)S(1)}, f32[96,256]{1,0:T(8,128)S(1)}, f32[32,128]{1,0:T(8,128)S(1)}, f32[32,128]{1,0:T(8,128)S(1)}) custom-call(s32[1]{0:T(128)} %bitcast.slab, f32[8,96,256]{2,1,0:T(8,128)S(1)} %get-tuple-element.35.h, f32[8,96,256]{2,1,0:T(8,128)S(1)} %get-tuple-element.36.p, f32[480,256]{1,0:T(8,128)S(1)} %get-tuple-element.39.mine, ...), custom_call_target="tpu_custom_call" | custom-call | tf_op jit(solution)/shard_map/pack_own/pallas_call | solution.py:607
  7.7 2.2 %collective-permute-done.1.edges = f32[40,256]{1,0:T(8,128)S(1)} collective-permute-done((f32[40,256]{1,0:T(8,128)S(1)}, f32[40,256]{1,0:T(8,128)S(1)}, u32[]{:S(2)}, u32[]{:S(2)}) %collective-permute-start.1) | collective-permute-done | bytes 40992 | tf_op jit(solution)/shard_map/ppermute | solution.py:605
  9.9 0.1 pack_y.1
  10.0 4.0 %collective-permute-start.4 = (f32[32,128]{1,0:T(8,128)S(1)}, f32[32,128]{1,0:T(8,128)S(1)}, u32[]{:S(2)}, u32[]{:S(2)}) collective-permute-start(f32[32,128]{1,0:T(8,128)S(1)} %get-tuple-element.48.whi), channel_id=1, source_target_pairs={{0,1},{1,2},{2,3},{3,4},{4,5},{5,6},{6,7},{8,9},{9,10},{10,11},{11... | collective-permute-start | bytes 49160 | tf_op jit(solution)/shard_map/ppermute | solution.py:586
  14.0 4.2 %collective-permute-start.5 = (f32[32,128]{1,0:T(8,128)S(1)}, f32[32,128]{1,0:T(8,128)S(1)}, u32[]{:S(2)}, u32[]{:S(2)}) collective-permute-start(f32[32,128]{1,0:T(8,128)S(1)} %get-tuple-element.49.wlo), channel_id=1, source_target_pairs={{1,0},{2,1},{3,2},{4,3},{5,4},{6,5},{7,6},{9,8},{10,9},{11,10},{12... | collective-permute-start | bytes 49160 | tf_op jit(solution)/shard_map/ppermute | solution.py:586
  18.2 1.3 %collective-permute-start.3 = (f32[96,256]{1,0:T(8,128)S(1)}, f32[96,256]{1,0:T(8,128)S(1)}, u32[]{:S(2)}, u32[]{:S(2)}) collective-permute-start(f32[96,256]{1,0:T(8,128)S(1)} %get-tuple-element.44), channel_id=1, source_target_pairs={{128,256},{0,384},{129,257},{1,385},{130,258},{2,386},{131,259},{3... | collective-permute-start | bytes 294920 | tf_op jit(solution)/shard_map/ppermute | solution.py:613
  19.5 4.3 %collective-permute-start.2 = (f32[384,256]{1,0:T(8,128)S(1)}, f32[384,256]{1,0:T(8,128)S(1)}, u32[]{:S(2)}, u32[]{:S(2)}) collective-permute-start(f32[384,256]{1,0:T(8,128)S(1)} %get-tuple-element.43), channel_id=1, source_target_pairs={{128,256},{256,128},{129,257},{257,129},{130,258},{258,130},{131,2... | collective-permute-start | bytes 1179656 | tf_op jit(solution)/shard_map/ppermute | solution.py:612
  23.8 0.9 %pre.1.w = f32[5,9,96,256]{3,2,1,0:T(8,128)S(1)} custom-call(f32[8,96,256]{2,1,0:T(8,128)S(1)} %get-tuple-element.35.h, f32[8,96,256]{2,1,0:T(8,128)S(1)} %get-tuple-element.36.p, f32[32,128]{1,0:T(8,128)S(1)} %get-tuple-element.49.wlo), custom_call_target="tpu_custom_call" | custom-call | flops 100000000 | bytes 100000000 | tf_op jit(solution)/shard_map/pre/pallas_call | solution.py:616
  24.7 0.0 collective-permute-done.4.ylo
  24.7 0.0 collective-permute-done.5.yhi
  24.8 5.0 %collective-permute-start.6 = (f32[40,256]{1,0:T(8,128)S(1)}, f32[40,256]{1,0:T(8,128)S(1)}, u32[]{:S(2)}, u32[]{:S(2)}) collective-permute-start(f32[40,256]{1,0:T(8,128)S(1)} %get-tuple-element.52.vhi), channel_id=1, source_target_pairs={{0,8},{8,16},{16,24},{24,32},{32,40},{40,48},{48,56},{56,64},{64,7... | collective-permute-start | bytes 122888 | tf_op jit(solution)/shard_map/ppermute | solution.py:586
  29.8 1.9 %collective-permute-start.7 = (f32[40,256]{1,0:T(8,128)S(1)}, f32[40,256]{1,0:T(8,128)S(1)}, u32[]{:S(2)}, u32[]{:S(2)}) collective-permute-start(f32[40,256]{1,0:T(8,128)S(1)} %get-tuple-element.53.vlo), channel_id=1, source_target_pairs={{8,0},{16,8},{24,16},{32,24},{40,32},{48,40},{56,48},{64,56},{72,6... | collective-permute-start | bytes 122888 | tf_op jit(solution)/shard_map/ppermute | solution.py:586
  31.8 0.0 collective-permute-done.3.both
  31.8 0.0 collective-permute-done.2.planes
  31.8 4.1 %inner.1 = (f32[2,4,32,128]{3,2,1,0:T(8,128)S(1)}, f32[2,8,96,256]{3,2,1,0:T(8,128)S(1)}, f32[2,96,256]{2,1,0:T(8,128)S(1)}, f32[10,96,256]{2,1,0:T(8,128)S(1)},...) custom-call(s32[1]{0:T(128)} %bitcast.slab, ...), custom_call_target="tpu_custom_call" | custom-call | flops 10000000000 | bytes 10000000000 | tf_op jit(solution)/shard_map/inner/pallas_call | solution.py:624
  35.9 0.0 collective-permute-done.6.xlo
  35.9 1.1 %collective-permute-done.7.xhi = f32[40,256]{1,0:T(8,128)S(1)} collective-permute-done((f32[40,256]{1,0:T(8,128)S(1)}, f32[40,256]{1,0:T(8,128)S(1)}, u32[]{:S(2)}, u32[]{:S(2)}) %collective-permute-start.7) | collective-permute-done | bytes 40992 | tf_op jit(solution)/shard_map/ppermute | solution.py:586
  37.0 1.3 %outer.1 = (f32[8,96,256]{2,1,0:T(8,128)}, f32[8,96,256]{2,1,0:T(8,128)}, f32[8,96,256]{2,1,0:T(8,128)}) custom-call(s32[1]{0:T(128)} %bitcast.slab, f32[8,256]{1,0:T(8,128)S(1)} %get-tuple-element.34.shade, f32[8,96,256]{2,1,0:T(8,128)S(1)} %get-tuple-element.35.h, ...), custom_call_target="tpu_custom_call", output_to_operand_aliasing={{0}: (21, {}), {1}: (22, {}), {2}: (23, {})} | custom-call | tf_op jit(solution)/shard_map/outer/pallas_call | solution.py:630
  (1 shorter events, 0.0 us)
Async XLA Ops:
  2.7 4.5 %collective-permute-start = (f32[480,256]{1,0:T(8,128)S(1)}, f32[480,256]{1,0:T(8,128)S(1)}, u32[]{:S(2)}, u32[]{:S(2)}) collective-permute-start(f32[480,256]{1,0:T(8,128)S(1)} %get-tuple-element.39.mine), channel_id=1, source_target_pairs={{0,128},{128,0},{256,384},{384,256},{1,129},{129,1},{257,385},{385... | collective-permute-start | bytes 1474568 | tf_op jit(solution)/shard_map/ppermute | solution.py:606
  4.6 5.3 %collective-permute-start.1 = (f32[40,256]{1,0:T(8,128)S(1)}, f32[40,256]{1,0:T(8,128)S(1)}, u32[]{:S(2)}, u32[]{:S(2)}) collective-permute-start(f32[40,256]{1,0:T(8,128)S(1)} %get-tuple-element.42), channel_id=1, source_target_pairs={{128,256},{256,128},{129,257},{257,129},{130,258},{258,130},{131,2... | collective-permute-start | bytes 122888 | tf_op jit(solution)/shard_map/ppermute | solution.py:605
  10.0 14.7 %collective-permute-start.4 = (f32[32,128]{1,0:T(8,128)S(1)}, f32[32,128]{1,0:T(8,128)S(1)}, u32[]{:S(2)}, u32[]{:S(2)}) collective-permute-start(f32[32,128]{1,0:T(8,128)S(1)} %get-tuple-element.48.whi), channel_id=1, source_target_pairs={{0,1},{1,2},{2,3},{3,4},{4,5},{5,6},{6,7},{8,9},{9,10},{10,11},{11... | collective-permute-start | bytes 49160 | tf_op jit(solution)/shard_map/ppermute | solution.py:586
  14.0 10.7 %collective-permute-start.5 = (f32[32,128]{1,0:T(8,128)S(1)}, f32[32,128]{1,0:T(8,128)S(1)}, u32[]{:S(2)}, u32[]{:S(2)}) collective-permute-start(f32[32,128]{1,0:T(8,128)S(1)} %get-tuple-element.49.wlo), channel_id=1, source_target_pairs={{1,0},{2,1},{3,2},{4,3},{5,4},{6,5},{7,6},{9,8},{10,9},{11,10},{12... | collective-permute-start | bytes 49160 | tf_op jit(solution)/shard_map/ppermute | solution.py:586
  18.2 13.5 %collective-permute-start.3 = (f32[96,256]{1,0:T(8,128)S(1)}, f32[96,256]{1,0:T(8,128)S(1)}, u32[]{:S(2)}, u32[]{:S(2)}) collective-permute-start(f32[96,256]{1,0:T(8,128)S(1)} %get-tuple-element.44), channel_id=1, source_target_pairs={{128,256},{0,384},{129,257},{1,385},{130,258},{2,386},{131,259},{3... | collective-permute-start | bytes 294920 | tf_op jit(solution)/shard_map/ppermute | solution.py:613
  19.5 12.2 %collective-permute-start.2 = (f32[384,256]{1,0:T(8,128)S(1)}, f32[384,256]{1,0:T(8,128)S(1)}, u32[]{:S(2)}, u32[]{:S(2)}) collective-permute-start(f32[384,256]{1,0:T(8,128)S(1)} %get-tuple-element.43), channel_id=1, source_target_pairs={{128,256},{256,128},{129,257},{257,129},{130,258},{258,130},{131,2... | collective-permute-start | bytes 1179656 | tf_op jit(solution)/shard_map/ppermute | solution.py:612
  24.8 11.1 %collective-permute-start.6 = (f32[40,256]{1,0:T(8,128)S(1)}, f32[40,256]{1,0:T(8,128)S(1)}, u32[]{:S(2)}, u32[]{:S(2)}) collective-permute-start(f32[40,256]{1,0:T(8,128)S(1)} %get-tuple-element.52.vhi), channel_id=1, source_target_pairs={{0,8},{8,16},{16,24},{24,32},{32,40},{40,48},{48,56},{56,64},{64,7... | collective-permute-start | bytes 122888 | tf_op jit(solution)/shard_map/ppermute | solution.py:586
  29.8 7.1 %collective-permute-start.7 = (f32[40,256]{1,0:T(8,128)S(1)}, f32[40,256]{1,0:T(8,128)S(1)}, u32[]{:S(2)}, u32[]{:S(2)}) collective-permute-start(f32[40,256]{1,0:T(8,128)S(1)} %get-tuple-element.53.vlo), channel_id=1, source_target_pairs={{8,0},{16,8},{24,16},{32,24},{40,32},{48,40},{56,48},{64,56},{72,6... | collective-permute-start | bytes 122888 | tf_op jit(solution)/shard_map/ppermute | solution.py:586
